TPU v7x, 128 devices: a whole 4x4x4 slice. The times are simulated.
128 devices in a mesh: rows: 32 (over z, x_hi, y), tp: 4 (over x_lo, core).
Axes of the slice: x: 4 (x_hi: 2, x_lo: 2; x = x_hi * 2 + x_lo), y: 4, z: 4, core: 2. Of those that a mesh axis runs over, the one named last changes fastest.
Arguments:
- tokens: int32 [4, 128], P(None, 'rows'), may hold values from 0 to 76031
- lengths: int32 [128], P('rows'), may hold values from 256 to 1024, as said below
- embedding: bfloat16 [76032, 32, 256], P(None, 'rows', 'tp')
- attn_gain: bfloat16 [8192], P('tp'), may hold values from 0.099609375 to 1.8984375
- key_weight: bfloat16 [8192, 1024], P('tp')
- value_weight: bfloat16 [8192, 1024], P('tp'), may hold values from -0.0625 to 0.0625
- policy_keys: bfloat16 [128, 1024, 1024], P('rows', None, 'tp')
- policy_values: bfloat16 [128, 1024, 1024], P('rows', None, 'tp'), may hold values from -6 to 6
- critic_lengths: int32 [128], P('rows'), may hold values from 256 to 1024, as said below
- critic_gain: bfloat16 [8192], P('tp'), may hold values from 0.099609375 to 1.8984375
- critic_keys: bfloat16 [128, 1024, 1024], P('rows', None, 'tp')
- critic_values: bfloat16 [128, 1024, 1024], P('rows', None, 'tp'), may hold values from -6 to 6
- value_gain: bfloat16 [8192], P('tp'), may hold values from 0.099609375 to 1.8984375
- value_head: bfloat16 [8192, 51], P('tp')
Outputs:
- policy_hidden: bfloat16 [4, 128, 8192], P(None, 'rows', 'tp')
- values: float32 [4, 128], P(None, 'rows')
Inputs may be any that keep to these rules, and one draw needn't show every extreme that they name: `lengths`: positions at or past a row's length are unused; the first row of each block of 4 rows has length 1024. `critic_lengths`: positions at or past a row's length are unused; the first row of each block of 4 rows has length 1024.
All inputs are finite; a program needn't handle non-finite values.
Results may differ from a plain program's by a relative error of at most 0.038.
Values may be sent and summed in bfloat16 or wider, within the bound.
No kernel may reach another device: no remote copies, remote signals or barrier semaphores. Data moves between devices by JAX's collectives and lax.ppermute only.
A program may use at most 128 MiB of HBM per device.

v0:
```python
import math

import jax
import jax.numpy as jnp
from jax import lax
from jax.sharding import PartitionSpec as P

D = 8192
HEAD_DIM = 128
ATOMS = 51


norm_eps = 1e-06
atom_span = 10.0


def passed_along(shard, axis, by):
    peers = lax.axis_size(axis)
    return lax.ppermute(shard, axis, [(i, (i + by) % peers) for i in range(peers)])


def attend(query, keys, values, lengths, extra_keys, extra_values):
    row_count = query.shape[0]
    cache_size = keys.shape[1]
    kv_count = keys.shape[2] // HEAD_DIM
    group_size = query.shape[1] // HEAD_DIM // kv_count
    scale = 1.0 / math.sqrt(HEAD_DIM)
    grouped = query.reshape(row_count, kv_count, group_size, HEAD_DIM)
    cache_keys = keys.reshape(row_count, cache_size, kv_count, HEAD_DIM)
    scores = (
        jnp.einsum("rkgd,rtkd->rkgt", grouped, cache_keys, preferred_element_type=jnp.float32)
        * scale
    )
    visible = lax.broadcasted_iota(jnp.int32, (row_count, cache_size), 1) < lengths[:, None]
    scores = jnp.where(visible[:, None, None, :], scores, -1e30)
    highest = jnp.max(scores, axis=-1)
    if extra_keys is not None:
        count = extra_keys.shape[1]
        fresh_keys = extra_keys.reshape(row_count, count, kv_count, HEAD_DIM)
        extra_scores = (
            jnp.einsum("rkgd,rtkd->rkgt", grouped, fresh_keys, preferred_element_type=jnp.float32)
            * scale
        )
        highest = jnp.maximum(highest, jnp.max(extra_scores, axis=-1))
    weights = jnp.exp(scores - highest[..., None])
    totals = jnp.sum(weights, axis=-1)
    if extra_keys is not None:
        extra_weights = jnp.exp(extra_scores - highest[..., None])
        totals = totals + jnp.sum(extra_weights, axis=-1)
    inverse = 1.0 / totals
    probs = (weights * inverse[..., None]).astype(jnp.bfloat16)
    cache_values = values.reshape(row_count, cache_size, kv_count, HEAD_DIM)
    attended = jnp.einsum(
        "rkgt,rtkd->rkgd", probs, cache_values, preferred_element_type=jnp.float32
    )
    if extra_keys is not None:
        extra_probs = (extra_weights * inverse[..., None]).astype(jnp.bfloat16)
        fresh_values = extra_values.reshape(row_count, count, kv_count, HEAD_DIM)
        attended = attended + jnp.einsum(
            "rkgt,rtkd->rkgd", extra_probs, fresh_values, preferred_element_type=jnp.float32
        )
    return attended.reshape(row_count, -1)


def on_device(
    tokens,
    lengths,
    embedding,
    attn_gain,
    key_weight,
    value_weight,
    policy_keys,
    policy_values,
    critic_lengths,
    critic_gain,
    critic_keys,
    critic_values,
    value_gain,
    value_head,
):
    step_count = tokens.shape[0]
    row_groups = lax.axis_size("rows")
    kv_width = policy_keys.shape[2]
    all_tokens = lax.all_gather(tokens, "rows", axis=1, tiled=True)
    table_block = embedding.reshape(embedding.shape[0], embedding.shape[2])
    picked_blocks = jnp.take(table_block, all_tokens, axis=0)
    looked_up = lax.all_to_all(picked_blocks, "rows", split_axis=1, concat_axis=2, tiled=True)
    head_offset = lax.axis_index("tp") * kv_width
    attn_scale = attn_gain.astype(jnp.float32)
    critic_scale = critic_gain.astype(jnp.float32)
    value_scale = value_gain.astype(jnp.float32)
    atom_index = lax.broadcasted_iota(jnp.int32, (ATOMS,), 0).astype(jnp.float32)
    atom_values = -atom_span + 2.0 * atom_span * atom_index / (ATOMS - 1)
    fresh_keys = []
    fresh_values = []
    hiddens = []
    results = []
    for decode_step in range(step_count):
        step_rows = looked_up[decode_step]
        picked_f = step_rows.astype(jnp.float32)
        gained = (picked_f * attn_scale).astype(jnp.bfloat16)
        part_keys = jnp.dot(gained, key_weight, preferred_element_type=jnp.float32)
        part_values = jnp.dot(gained, value_weight, preferred_element_type=jnp.float32)
        full_keys, full_values, squares = lax.psum(
            (part_keys, part_values, jnp.sum(picked_f * picked_f, axis=-1)), "tp"
        )
        inv = lax.rsqrt(squares / D + norm_eps)[:, None]
        new_key = (inv * lax.dynamic_slice_in_dim(full_keys, head_offset, kv_width, 1)).astype(
            jnp.bfloat16
        )
        new_value = (inv * lax.dynamic_slice_in_dim(full_values, head_offset, kv_width, 1)).astype(
            jnp.bfloat16
        )
        query = (gained.astype(jnp.float32) * inv).astype(jnp.bfloat16)
        fresh_keys.append(new_key)
        fresh_values.append(new_value)
        attended = attend(
            query,
            policy_keys,
            policy_values,
            lengths,
            jnp.stack(fresh_keys, axis=1),
            jnp.stack(fresh_values, axis=1),
        )
        hidden = (picked_f + attended).astype(jnp.bfloat16)
        hiddens.append(hidden)
        arrived = passed_along(hidden, "rows", row_groups // 2)
        critic_rows = arrived.astype(jnp.float32)
        squares_h = lax.psum(jnp.sum(critic_rows * critic_rows, axis=-1), "tp")
        inv_h = lax.rsqrt(squares_h / D + norm_eps)[:, None]
        critic_query = (critic_rows * critic_scale * inv_h).astype(jnp.bfloat16)
        critic_out = attend(critic_query, critic_keys, critic_values, critic_lengths, None, None)
        combined = critic_rows + critic_out
        scaled = (combined * value_scale).astype(jnp.bfloat16)
        part_logits = jnp.dot(scaled, value_head, preferred_element_type=jnp.float32)
        full_logits, squares_c = lax.psum(
            (part_logits, jnp.sum(combined * combined, axis=-1)), "tp"
        )
        logits = lax.rsqrt(squares_c / D + norm_eps)[:, None] * full_logits
        probs = jax.nn.softmax(logits, axis=-1)
        results.append(jnp.sum(probs * atom_values[None, :], axis=-1))
    return (jnp.stack(hiddens, axis=0), jnp.stack(results, axis=0))


def solution(mesh):
    placed = (
        P(None, "rows"),
        P("rows"),
        P(None, "rows", "tp"),
        P("tp"),
        P("tp", None),
        P("tp", None),
        P("rows", None, "tp"),
        P("rows", None, "tp"),
        P("rows"),
        P("tp"),
        P("rows", None, "tp"),
        P("rows", None, "tp"),
        P("tp"),
        P("tp", None),
    )
    return jax.shard_map(
        on_device,
        mesh=mesh,
        in_specs=placed,
        out_specs=(P(None, "rows", "tp"), P(None, "rows")),
        check_vma=False,
    )
```

profile of v0, /device:TPU:1, one launch (start us, length us, event | category | flops | bytes accessed | tf_op | source)
XLA Modules:
  0.0 274.4 jit_solution(12212932258048924741)
XLA Ops:
  7.2 0.9 copy.182
  8.1 83.3 %all-gather = s32[32,4,4]{2,1,0:T(4,128)S(1)} all-gather(s32[1,4,4]{2,1,0:T(4,128)S(1)} %bitcast.327), channel_id=1, replica_groups=mesh['rows'=32,'tp'=4] {'rows'}, dimensions={0}, use_global_device_ids=true | all-gather | bytes 2112 | tf_op jit(solution)/shard_map/all_gather | solution.py:84
  91.5 18.2 %copy.185 = bf16[76032,1,64]{2,0,1:T(8,128)(2,1)} copy(bf16[76032,1,64]{0,2,1:T(8,128)(2,1)} %param.16) | data formatting | bytes 19464192 | tf_op args[2]
  109.9 10.1 %gather_fusion = bf16[512,64]{1,0:T(8,128)(2,1)S(1)} fusion(bf16[76032,64]{1,0:T(8,128)(2,1)} %bitcast.315, s32[1024]{0:T(1024)S(1)} %pad_clamp_fusion), kind=kCustom, calls=%fused_computation | custom fusion | bytes 133120 | tf_op jit(solution)/shard_map/jit(_take)/gather | solution.py:86
  120.0 0.2 fusion.257
  120.2 0.8 reshape.480
  121.0 3.9 %all-to-all-start = ((bf16[32,2,512]{2,1,0:T(2,128)(2,1)}), bf16[32,2,512]{2,1,0:T(2,128)(2,1)S(1)}, u32[]{:S(2)}, u32[]{:S(2)}) async-start(bf16[32,2,512]{2,1,0:T(2,128)(2,1)} %reshape.480), calls=%async_computation | async-start | bytes 131072 | tf_op jit(solution)/shard_map/all_to_all | solution.py:87
  125.0 8.7 %all-to-all-done = bf16[32,2,512]{2,1,0:T(2,128)(2,1)S(1)} async-done(((bf16[32,2,512]{2,1,0:T(2,128)(2,1)}), bf16[32,2,512]{2,1,0:T(2,128)(2,1)S(1)}, u32[]{:S(2)}, u32[]{:S(2)}) %all-to-all-start) | async-done | bytes 65568 | tf_op jit(solution)/shard_map/all_to_all | solution.py:87
  134.0 3.6 %fusion.232 = f32[4,1024]{1,0:T(4,128)} fusion(bf16[2048,1024]{1,0:T(8,128)(2,1)} %param.19, f32[4,2048]{1,0:T(4,128)S(1)} %reshape.453, f32[2048]{0:T(1024)S(1)} %get-tuple-element.45), kind=kOutput, calls=%fused_computation.308 | convolution fusion | flops 16793600 | bytes 4251648 | tf_op jit(solution)/shard_map/dot_general | solution.py:103
  137.6 1.3 fusion.233
  138.9 3.6 %fusion.234 = f32[4,1024]{1,0:T(4,128)} fusion(bf16[2048,1024]{1,0:T(8,128)(2,1)} %param.19, f32[4,2048]{1,0:T(4,128)S(1)} %reshape.457, f32[2048]{0:T(1024)S(1)} %get-tuple-element.45), kind=kOutput, calls=%fused_computation.310 | convolution fusion | flops 16793600 | bytes 4251648 | tf_op jit(solution)/shard_map/dot_general | solution.py:103
  142.5 1.2 fusion.235
  143.9 3.6 %fusion.236 = f32[4,1024]{1,0:T(4,128)} fusion(bf16[2048,1024]{1,0:T(8,128)(2,1)} %param.19, f32[4,2048]{1,0:T(4,128)S(1)} %reshape.460, f32[2048]{0:T(1024)S(1)} %get-tuple-element.45), kind=kOutput, calls=%fused_computation.312 | convolution fusion | flops 16793600 | bytes 4251648 | tf_op jit(solution)/shard_map/dot_general | solution.py:103
  147.5 1.3 fusion.237
  148.8 3.6 %fusion.238 = f32[4,1024]{1,0:T(4,128)} fusion(bf16[2048,1024]{1,0:T(8,128)(2,1)} %param.19, f32[4,2048]{1,0:T(4,128)S(1)} %reshape.463, f32[2048]{0:T(1024)S(1)} %get-tuple-element.45), kind=kOutput, calls=%fused_computation.314 | convolution fusion | flops 16793600 | bytes 4251648 | tf_op jit(solution)/shard_map/dot_general | solution.py:103
  152.5 1.3 fusion.239
  153.7 0.7 multiply_reduce_fusion.3
  155.3 48.2 %all-reduce.5.cloned.1.call-done = (f32[4,1024]{1,0:T(4,128)}, f32[4]{0:T(128)}, f32[4,1024]{1,0:T(4,128)}, f32[4]{0:T(128)}, f32[4,1024]{1,0:T(4,128)}, /*index...) async-done(((f32[4,1024]{1,0:T(4,128)}, f32[4]{0:T(128)}, ...) | async-done | bytes 131152 | tf_op jit(solution)/shard_map/psum | solution.py:104
  203.5 0.6 add_rsqrt_fusion.10
  204.1 0.6 add_rsqrt_fusion.11
  204.7 0.8 multiply_convert_fusion.46
  205.5 0.6 add_rsqrt_fusion.8
  206.2 0.7 add_rsqrt_fusion.9
  206.9 0.8 multiply_convert_fusion.42
  207.7 0.8 fusion.248
  208.4 0.8 fusion.250
  209.2 0.2 fusion.251
  209.4 0.2 fusion.249
  209.7 0.2 fusion.134
  209.9 0.2 fusion.186
  210.1 2.0 fusion.114
  212.2 3.1 %collective-permute-start.2 = (bf16[4,2048]{1,0:T(4,128)(2,1)S(1)}, bf16[4,2048]{1,0:T(4,128)(2,1)S(1)}, u32[]{:S(2)}, u32[]{:S(2)}) collective-permute-start(bf16[4,2048]{1,0:T(4,128)(2,1)S(1)} %fusion.161), channel_id=1, source_target_pairs={{0,64},{4,68},{8,72},{12,76},{16,80},{20,84},{24,88},{28,92},{32,9... | collective-permute-start | bytes 49160 | tf_op jit(solution)/shard_map/ppermute | solution.py:19
  215.4 0.2 fusion.133
  215.6 0.2 fusion.217
  215.8 2.0 fusion.111
  218.1 0.7 fusion.252
  219.0 0.2 fusion.132
  219.2 0.2 copy-done.6
  219.4 0.4 fusion.108
  219.9 2.8 %collective-permute-start = (bf16[4,2048]{1,0:T(4,128)(2,1)S(1)}, bf16[4,2048]{1,0:T(4,128)(2,1)S(1)}, u32[]{:S(2)}, u32[]{:S(2)}) collective-permute-start(bf16[4,2048]{1,0:T(4,128)(2,1)S(1)} %fusion.163), channel_id=1, source_target_pairs={{0,64},{4,68},{8,72},{12,76},{16,80},{20,84},{24,88},{28,92},{32,9... | collective-permute-start | bytes 49160 | tf_op jit(solution)/shard_map/ppermute | solution.py:19
  222.7 0.8 fusion.246
  223.5 0.2 fusion.247
  223.7 0.2 fusion.135
  223.9 0.2 fusion.187
  224.1 2.0 fusion.117
  226.2 0.4 collective-permute-start.3
  227.1 3.3 %collective-permute-done.3 = bf16[4,2048]{1,0:T(4,128)(2,1)S(1)} collective-permute-done((bf16[4,2048]{1,0:T(4,128)(2,1)S(1)}, bf16[4,2048]{1,0:T(4,128)(2,1)S(1)}, u32[]{:S(2)}, u32[]{:S(2)}) %collective-permute-start.3) | collective-permute-done | bytes 16416 | tf_op jit(solution)/shard_map/ppermute | solution.py:19
  230.5 0.7 pad_maximum_fusion
  231.2 6.1 %all-reduce.1 = (f32[4]{0:T(128)S(1)}, f32[4]{0:T(128)S(1)}, f32[4]{0:T(128)S(1)}, f32[4]{0:T(128)S(1)}) all-reduce(f32[4]{0:T(128)S(1)} %fusion.150, f32[4]{0:T(128)S(1)} %fusion.153, f32[4]{0:T(128)S(1)} %fusion.156, f32[4]{0:T(128)S(1)} %fusion.159), channel_id=1, replica_groups=mesh['rows'=32,'tp'=4] {'tp'}, use_global_device_ids=true, to_apply=%region_31.32 | all-reduce | flops 16 | bytes 128 | tf_op jit(solution)/shard_map/psum | solution.py:129
  237.5 2.4 fusion.105
  239.8 0.2 fusion.256
  240.1 0.6 fusion.99
  240.7 0.2 fusion.255
  241.0 2.0 fusion.129
  243.0 2.1 fusion.126
  245.1 2.2 fusion.93
  247.3 0.2 fusion.254
  247.5 2.0 fusion.123
  249.6 2.3 fusion.87
  251.9 0.2 fusion.253
  252.1 2.0 fusion.120
  255.4 9.7 %all-reduce = (f32[4,51]{1,0:T(4,128)S(1)}, f32[4]{0:T(128)S(1)}, f32[4,51]{1,0:T(4,128)S(1)}, f32[4]{0:T(128)S(1)}, f32[4,51]{1,0:T(4,128)S(1)}, /*index=5*/f32...) all-reduce(f32[4,51]{1,0:T(4,128)S(1)} %fusion.164, ...), channel_id=1, replica_groups=mesh['rows'=32,'tp'=4] {'tp'}, use_global_device_ids=true, to_apply=%region_36.37 | all-reduce | flops 832 | bytes 6656 | tf_op jit(solution)/shard_map/psum | solution.py:136
  266.7 0.2 multiply_reduce_fusion.11
  267.0 0.6 pad_maximum_fusion.1
  (125 shorter events, 6.1 us)
Async XLA Ops:
  7.2 200.5 %copy-start = (bf16[4,1024,256]{2,1,0:T(8,128)(2,1)S(1)}, bf16[4,1024,256]{2,1,0:T(8,128)(2,1)}, u32[]{:S(2)}) copy-start(bf16[4,1024,256]{2,1,0:T(8,128)(2,1)} %param.20) | copy-start | bytes 6291460
  91.5 33.4 %copy-start.8 = (bf16[2048]{0:T(1024)(128)(2,1)S(1)}, bf16[2048]{0:T(1024)(128)(2,1)}, u32[]{:S(2)}) copy-start(bf16[2048]{0:T(1024)(128)(2,1)} %param.17) | copy-start | bytes 12292
  91.5 33.4 %copy-start.11 = (s32[4]{0:T(128)S(1)}, s32[4]{0:T(128)}, u32[]{:S(2)}) copy-start(s32[4]{0:T(128)} %param.15) | copy-start | bytes 52
  121.0 12.7 %all-to-all-start = ((bf16[32,2,512]{2,1,0:T(2,128)(2,1)}), bf16[32,2,512]{2,1,0:T(2,128)(2,1)S(1)}, u32[]{:S(2)}, u32[]{:S(2)}) async-start(bf16[32,2,512]{2,1,0:T(2,128)(2,1)} %reshape.480), calls=%async_computation | async-start | bytes 131072 | tf_op jit(solution)/shard_map/all_to_all | solution.py:87
  124.8 78.7 %all-reduce.5.cloned.1.call-start = ((), (), s32[]{:S(2)}) async-start(), calls=%async_computation.1 | async-start | bytes 266240 | tf_op jit(solution)/shard_map/psum | solution.py:104
  134.0 3.6 %copy-start.1 = (bf16[2048,1024]{1,0:T(8,128)(2,1)S(1)}, bf16[2048,1024]{1,0:T(8,128)(2,1)}, u32[]{:S(2)}) copy-start(bf16[2048,1024]{1,0:T(8,128)(2,1)} %param.18) | copy-start | bytes 12582916
  138.9 3.6 %copy-start.2 = (bf16[2048,1024]{1,0:T(8,128)(2,1)S(1)}, bf16[2048,1024]{1,0:T(8,128)(2,1)}, u32[]{:S(2)}) copy-start(bf16[2048,1024]{1,0:T(8,128)(2,1)} %param.18) | copy-start | bytes 12582916
  143.9 3.6 %copy-start.3 = (bf16[2048,1024]{1,0:T(8,128)(2,1)S(1)}, bf16[2048,1024]{1,0:T(8,128)(2,1)}, u32[]{:S(2)}) copy-start(bf16[2048,1024]{1,0:T(8,128)(2,1)} %param.18) | copy-start | bytes 12582916
  148.8 3.6 %copy-start.4 = (bf16[2048,1024]{1,0:T(8,128)(2,1)S(1)}, bf16[2048,1024]{1,0:T(8,128)(2,1)}, u32[]{:S(2)}) copy-start(bf16[2048,1024]{1,0:T(8,128)(2,1)} %param.18) | copy-start | bytes 12582916
  152.4 2.0 copy-start.12
  152.4 2.1 copy-start.9
  152.4 2.1 copy-start.10
  212.2 14.5 %collective-permute-start.2 = (bf16[4,2048]{1,0:T(4,128)(2,1)S(1)}, bf16[4,2048]{1,0:T(4,128)(2,1)S(1)}, u32[]{:S(2)}, u32[]{:S(2)}) collective-permute-start(bf16[4,2048]{1,0:T(4,128)(2,1)S(1)} %fusion.161), channel_id=1, source_target_pairs={{0,64},{4,68},{8,72},{12,76},{16,80},{20,84},{24,88},{28,92},{32,9... | collective-permute-start | bytes 49160 | tf_op jit(solution)/shard_map/ppermute | solution.py:19
  217.8 1.6 copy-start.6
  217.9 8.9 %collective-permute-start.1 = (bf16[4,2048]{1,0:T(4,128)(2,1)S(1)}, bf16[4,2048]{1,0:T(4,128)(2,1)S(1)}, u32[]{:S(2)}, u32[]{:S(2)}) collective-permute-start(bf16[4,2048]{1,0:T(4,128)(2,1)S(1)} %fusion.162), channel_id=1, source_target_pairs={{0,64},{4,68},{8,72},{12,76},{16,80},{20,84},{24,88},{28,92},{32,9... | collective-permute-start | bytes 49160 | tf_op jit(solution)/shard_map/ppermute | solution.py:19
  219.9 7.0 %collective-permute-start = (bf16[4,2048]{1,0:T(4,128)(2,1)S(1)}, bf16[4,2048]{1,0:T(4,128)(2,1)S(1)}, u32[]{:S(2)}, u32[]{:S(2)}) collective-permute-start(bf16[4,2048]{1,0:T(4,128)(2,1)S(1)} %fusion.163), channel_id=1, source_target_pairs={{0,64},{4,68},{8,72},{12,76},{16,80},{20,84},{24,88},{28,92},{32,9... | collective-permute-start | bytes 49160 | tf_op jit(solution)/shard_map/ppermute | solution.py:19
  226.2 4.2 %collective-permute-start.3 = (bf16[4,2048]{1,0:T(4,128)(2,1)S(1)}, bf16[4,2048]{1,0:T(4,128)(2,1)S(1)}, u32[]{:S(2)}, u32[]{:S(2)}) collective-permute-start(bf16[4,2048]{1,0:T(4,128)(2,1)S(1)} %fusion.160), channel_id=1, source_target_pairs={{0,64},{4,68},{8,72},{12,76},{16,80},{20,84},{24,88},{28,92},{32,9... | collective-permute-start | bytes 49160 | tf_op jit(solution)/shard_map/ppermute | solution.py:19
  237.3 2.7 copy-start.5
  249.6 4.9 %copy-start.7 = (bf16[2048,51]{0,1:T(8,128)(2,1)S(1)}, bf16[2048,51]{0,1:T(8,128)(2,1)}, u32[]{:S(2)}) copy-start(bf16[2048,51]{0,1:T(8,128)(2,1)} %param.27) | copy-start | bytes 626692
Sparse Core Ops, SparseCore 0:
  154.6 48.8 all-reduce.4
where the time goes:
time: 276 us; the launch traced here: 274 us
  blocking collectives  99.1 us (36%)
  waiting for transfers between devices  60.3 us (22%)
  matrix products  46.8 us (17%)
  local copies, waits for them, and re-layouts  31.9 us (12%)
  between operations  14.5 us (5%)
  other arithmetic  11.6 us (4%)
  starting transfers between devices  10.3 us (4%)
    all_gather x1, blocking collectives, on_device(): all_tokens = lax.all_gather(tokens, 'rows', axis=1, tiled=True)  83.3 us
    psum x1, waiting for transfers between devices, on_device(): lax.psum((part_keys, part_values, jnp.sum(picked_f * picked_f, axis=-1)),...  48.2 us
    unnamed x31, local copies, waits for them, and re-layouts  20.4 us
    dot_general x8, matrix products, attend(): jnp.einsum('rkgt,rtkd->rkgd', probs, cache_values, preferred_element_type...  14.7 us
    dot_general x4, matrix products, on_device(): jnp.dot(gained, value_weight, preferred_element_type=jnp.float32)  14.4 us
    dot_general x8, matrix products, attend(): jnp.einsum('rkgd,rtkd->rkgt', grouped, cache_keys, preferred_element_type...  10.6 us
    gather x1, local copies, waits for them, and re-layouts, on_device(): picked_blocks = jnp.take(table_block, all_tokens, axis=0)  10.1 us
    psum x1, blocking collectives, on_device(): lax.psum((part_logits, jnp.sum(combined * combined, axis=-1)), 'tp')  9.75 us
  transfers between devices with their start and end apart: 6, of which 3 were waited for; matrix products, arithmetic and copies ran while one was open for 3% of the time, Pallas kernels for 0%

commit v1 on v0

v1 whole, which is shorter than its diff:
```python
import math

import jax
import jax.numpy as jnp
from jax import lax
from jax.experimental import pallas as pl
from jax.experimental.pallas import tpu as pltpu
from jax.sharding import PartitionSpec as P

D = 8192
HEAD_DIM = 128
ATOMS = 51
LANES = 128

norm_eps = 1e-06
atom_span = 10.0


def pick_rows_kernel(token_ref, table_ref, out_ref):
    width = table_ref.shape[0]
    groups = out_ref.shape[0] // LANES
    lane = lax.broadcasted_iota(jnp.int32, (width, LANES), 1)

    def column(token, place):
        block = pl.multiple_of((token // LANES) * LANES, LANES)
        tile = table_ref[:, pl.ds(block, LANES)].astype(jnp.float32)
        shift = jnp.bitwise_and(place - token + LANES * LANES * 8, LANES - 1)
        return pltpu.roll(tile, shift, 1)

    for group in range(groups):

        def step(place, carry):
            first, second = carry
            base = (group * (LANES // 8) + place // 8) * 16 + place % 8
            here = lane == place
            first = jnp.where(here, column(token_ref[base], place), first)
            second = jnp.where(here, column(token_ref[base + 8], place), second)
            return first, second

        empty = jnp.zeros((width, LANES), jnp.float32)
        first, second = lax.fori_loop(0, LANES, step, (empty, empty), unroll=4)
        both = jnp.concatenate([first, second], axis=0)
        out_ref[pl.ds(group * LANES, LANES), :] = both.T.astype(out_ref.dtype)


def pick_rows(tokens, table):
    width = table.shape[0]
    rows = tokens.shape[0] * width // LANES
    return pl.pallas_call(
        pick_rows_kernel,
        out_shape=jax.ShapeDtypeStruct((rows, LANES), table.dtype),
        in_specs=[
            pl.BlockSpec(memory_space=pltpu.SMEM),
            pl.BlockSpec(memory_space=pltpu.VMEM),
        ],
        out_specs=pl.BlockSpec(memory_space=pltpu.VMEM),
        compiler_params=pltpu.CompilerParams(vmem_limit_bytes=16 * 1024 * 1024),
        name="pick_rows",
    )(tokens, table)


def swapped(shard, by):
    peers = lax.axis_size("tp")
    return lax.ppermute(shard, "tp", [(i, i ^ by) for i in range(peers)])


def passed_along(shard, axis, by):
    peers = lax.axis_size(axis)
    return lax.ppermute(shard, axis, [(i, (i + by) % peers) for i in range(peers)])


def summed(shard):
    peers = lax.axis_size("tp")
    arrived = [swapped(shard, by) for by in range(1, peers)]
    return shard + (arrived[0] + (arrived[1] + arrived[2]))


def grouped_heads(rows, row_count):
    kv_count = rows.shape[1] // (8 * HEAD_DIM)
    split = rows.reshape(row_count, -1, kv_count, 8, HEAD_DIM)
    return split.transpose(0, 2, 1, 3, 4).reshape(row_count, kv_count, -1, HEAD_DIM)


def raw_scores(grouped, keys):
    row_count, cache_size = keys.shape[:2]
    cache_keys = keys.reshape(row_count, cache_size, -1, HEAD_DIM)
    return jnp.einsum("rkgd,rtkd->rkgt", grouped, cache_keys, preferred_element_type=jnp.float32)


def on_device(
    tokens,
    lengths,
    embedding,
    attn_gain,
    key_weight,
    value_weight,
    policy_keys,
    policy_values,
    critic_lengths,
    critic_gain,
    critic_keys,
    critic_values,
    value_gain,
    value_head,
):
    steps, row_count = tokens.shape
    row_groups = lax.axis_size("rows")
    kv_width = policy_keys.shape[2]
    kv_count = kv_width // HEAD_DIM
    cache_size = policy_keys.shape[1]
    scale = 1.0 / math.sqrt(HEAD_DIM)
    count = steps * row_count
    tp = lax.axis_index("tp")

    mine = tokens.T.reshape(1, count)
    all_tokens = lax.all_to_all(
        jnp.broadcast_to(mine, (row_groups, count)), "rows", split_axis=0, concat_axis=0, tiled=True
    )
    table = embedding.transpose(1, 2, 0).reshape(embedding.shape[2], embedding.shape[0])
    picked = pick_rows(all_tokens.reshape(-1), table)
    picked = picked.reshape(row_groups, count // 2, LANES)
    blocks = lax.all_to_all(picked, "rows", split_axis=0, concat_axis=0, tiled=True)
    blocks = blocks.reshape(row_groups, count // 2, 2, LANES // 2)
    x = blocks.transpose(2, 1, 0, 3).reshape(count, -1)

    picked_f = x.astype(jnp.float32)
    gained = (picked_f * attn_gain.astype(jnp.float32)).astype(jnp.bfloat16)
    part_keys = jnp.dot(gained, key_weight, preferred_element_type=jnp.float32)
    part_values = jnp.dot(gained, value_weight, preferred_element_type=jnp.float32)
    squares = jnp.sum(picked_f * picked_f, axis=-1)

    def piece(by):
        at = (tp ^ by) * kv_width
        return jnp.concatenate(
            [
                lax.dynamic_slice_in_dim(part_keys, at, kv_width, 1),
                lax.dynamic_slice_in_dim(part_values, at, kv_width, 1),
                jnp.broadcast_to(squares[:, None], (count, LANES)),
            ],
            axis=1,
        )

    total = piece(0)
    for by in (1, 2, 3):
        total = total + swapped(piece(by), by)
    inv = lax.rsqrt(total[:, -1:] / D + norm_eps)
    new_key = (inv * total[:, :kv_width]).astype(jnp.bfloat16)
    new_value = (inv * total[:, kv_width : 2 * kv_width]).astype(jnp.bfloat16)

    grouped = grouped_heads(gained, row_count)
    scores = raw_scores(grouped, policy_keys)
    inv_rows = jnp.repeat(inv.reshape(row_count, 1, steps, 1), 8, axis=2) * scale
    visible = lax.broadcasted_iota(jnp.int32, (row_count, cache_size), 1) < lengths[:, None]
    scores = jnp.where(visible[:, None, None, :], scores * inv_rows, -1e30)
    fresh_keys = new_key.reshape(row_count, steps, kv_count, HEAD_DIM)
    fresh_values = new_value.reshape(row_count, steps, kv_count, HEAD_DIM)
    extra = jnp.einsum("rkgd,rtkd->rkgt", grouped, fresh_keys, preferred_element_type=jnp.float32)
    earlier = (jnp.arange(steps)[None, :] <= jnp.arange(steps * 8)[:, None] // 8)[None, None]
    extra = jnp.where(earlier, extra * inv_rows, -1e30)
    highest = jnp.maximum(jnp.max(scores, axis=-1), jnp.max(extra, axis=-1))[..., None]
    weights = jnp.exp(scores - highest)
    extra_weights = jnp.exp(extra - highest)
    inverse = 1.0 / (jnp.sum(weights, axis=-1) + jnp.sum(extra_weights, axis=-1))[..., None]
    probs = (weights * inverse).astype(jnp.bfloat16)
    extra_probs = (extra_weights * inverse).astype(jnp.bfloat16)
    attended = jnp.einsum(
        "rkgt,rtkd->rkgd",
        probs,
        policy_values.reshape(row_count, cache_size, kv_count, HEAD_DIM),
        preferred_element_type=jnp.float32,
    ) + jnp.einsum(
        "rkgt,rtkd->rkgd", extra_probs, fresh_values, preferred_element_type=jnp.float32
    )
    attended = attended.reshape(row_count, kv_count, steps, 8 * HEAD_DIM).transpose(0, 2, 1, 3)
    hidden = (picked_f + attended.reshape(count, -1)).astype(jnp.bfloat16)

    arrived = passed_along(hidden, "rows", row_groups // 2)
    critic_rows = arrived.astype(jnp.float32)
    squares_h = summed(
        jnp.broadcast_to(jnp.sum(critic_rows * critic_rows, axis=-1)[:, None], (count, LANES))
    )[:, :1]
    gained_h = (critic_rows * critic_gain.astype(jnp.float32)).astype(jnp.bfloat16)
    scores = raw_scores(grouped_heads(gained_h, row_count), critic_keys)
    inv_h = lax.rsqrt(squares_h / D + norm_eps)
    inv_rows = jnp.repeat(inv_h.reshape(row_count, 1, steps, 1), 8, axis=2) * scale
    visible = lax.broadcasted_iota(jnp.int32, (row_count, cache_size), 1) < critic_lengths[:, None]
    scores = jnp.where(visible[:, None, None, :], scores * inv_rows, -1e30)
    weights = jnp.exp(scores - jnp.max(scores, axis=-1, keepdims=True))
    probs = (weights / jnp.sum(weights, axis=-1, keepdims=True)).astype(jnp.bfloat16)
    critic_out = jnp.einsum(
        "rkgt,rtkd->rkgd",
        probs,
        critic_values.reshape(row_count, cache_size, kv_count, HEAD_DIM),
        preferred_element_type=jnp.float32,
    )
    critic_out = critic_out.reshape(row_count, kv_count, steps, 8 * HEAD_DIM).transpose(0, 2, 1, 3)
    combined = critic_rows + critic_out.reshape(count, -1)
    scaled = (combined * value_gain.astype(jnp.float32)).astype(jnp.bfloat16)
    part_logits = jnp.dot(scaled, value_head, preferred_element_type=jnp.float32)
    squares_c = jnp.sum(combined * combined, axis=-1, keepdims=True)
    full = summed(jnp.concatenate([part_logits, squares_c], axis=1))
    logits = lax.rsqrt(full[:, ATOMS:] / D + norm_eps) * full[:, :ATOMS]
    atom_index = lax.broadcasted_iota(jnp.int32, (ATOMS,), 0).astype(jnp.float32)
    atom_values = -atom_span + 2.0 * atom_span * atom_index / (ATOMS - 1)
    probs = jax.nn.softmax(logits, axis=-1)
    values = jnp.sum(probs * atom_values[None, :], axis=-1)
    return (
        hidden.reshape(row_count, steps, -1).transpose(1, 0, 2),
        values.reshape(row_count, steps).T,
    )


def solution(mesh):
    placed = (
        P(None, "rows"),
        P("rows"),
        P(None, "rows", "tp"),
        P("tp"),
        P("tp", None),
        P("tp", None),
        P("rows", None, "tp"),
        P("rows", None, "tp"),
        P("rows"),
        P("tp"),
        P("rows", None, "tp"),
        P("rows", None, "tp"),
        P("tp"),
        P("tp", None),
    )
    return jax.shard_map(
        on_device,
        mesh=mesh,
        in_specs=placed,
        out_specs=(P(None, "rows", "tp"), P(None, "rows")),
        check_vma=False,
    )
```

time: 276 us -> 91.9 us (0.33)
  blocking collectives: 99.1 us -> 0 us
  waiting for transfers between devices: 60.3 us -> 24.4 us
  matrix products: 46.8 us -> 11.9 us
  local copies, waits for them, and re-layouts: 31.9 us -> 11 us
  starting transfers between devices: 10.3 us -> 27.2 us
  between operations: 14.5 us -> 0.9 us
  Pallas kernels: 0 us -> 10.8 us
  other arithmetic: 11.6 us -> 5.24 us
    all_gather x1 -> x0, blocking collectives: 83.3 us -> none  [on_device(): all_tokens = lax.all_gather(tokens, 'rows', axis=1, tiled=True)]
    psum x1 -> x0, waiting for transfers between devices: 48.2 us -> none  [on_device(): lax.psum((part_keys, part_values, jnp.sum(picked_f * picked_f, axis=-1)),...]
    dot_general x23 -> x6, matrix products: 26.7 us -> 7.11 us  [the longest x2 3.33 us: raw_scores(): jnp.einsum('rkgd,rtkd->rkgt', grouped, cache_keys, preferred_element_type...]
    psum x2 -> x0, blocking collectives: 15.9 us -> none  [the longest x1 9.75 us: on_device(): lax.psum((part_logits, jnp.sum(combined * combined, axis=-1)), 'tp')]
    unnamed x31 -> x22, local copies, waits for them, and re-layouts: 20.4 us -> 5.86 us
    dot_general x4 -> x1, matrix products: 14.4 us -> 2.99 us  [on_device(): jnp.dot(gained, value_weight, preferred_element_type=jnp.float32)]
    all_to_all x1 -> x2, starting transfers between devices: 3.86 us -> 15.2 us  [the longest x1 11.3 us: on_device(): lax.all_to_all(jnp.broadcast_to(mine, (row_groups, count)), 'rows', split...]
    ppermute x0 -> x9, starting transfers between devices: none -> 10.9 us  [swapped(): return lax.ppermute(shard, 'tp', [(i, i ^ by) for i in range(peers)])]
  transfers between devices with their start and end apart: 6 -> 12, of which waited for: 3 -> 8; matrix products, arithmetic and copies ran while one was open for 3% -> 3% of each run, Pallas kernels for 0% -> 0%
where the time goes in v1:
time: 91.9 us; the launch traced here: 91.4 us
  starting transfers between devices  27.2 us (30%)
  waiting for transfers between devices  24.4 us (27%)
  matrix products  11.9 us (13%)
  local copies, waits for them, and re-layouts  11 us (12%)
  Pallas kernels  10.8 us (12%)
  other arithmetic  5.24 us (6%)
    all_to_all x1, starting transfers between devices, on_device(): lax.all_to_all(jnp.broadcast_to(mine, (row_groups, count)), 'rows', split...  11.3 us
    ppermute x9, starting transfers between devices, swapped(): return lax.ppermute(shard, 'tp', [(i, i ^ by) for i in range(peers)])  10.9 us
    pallas_call x1, Pallas kernels, pick_rows(): pl.pallas_call(pick_rows_kernel, out_shape=jax.ShapeDtypeStruct((rows, LA...  10.8 us
    all_to_all x1, waiting for transfers between devices, on_device(): lax.all_to_all(picked, 'rows', split_axis=0, concat_axis=0, tiled=True)  8.91 us
    all_to_all x1, waiting for transfers between devices, on_device(): lax.all_to_all(jnp.broadcast_to(mine, (row_groups, count)), 'rows', split...  7.14 us
    unnamed x22, local copies, waits for them, and re-layouts  5.86 us
    ppermute x9, waiting for transfers between devices, swapped(): return lax.ppermute(shard, 'tp', [(i, i ^ by) for i in range(peers)])  4.77 us
    all_to_all x1, starting transfers between devices, on_device(): lax.all_to_all(picked, 'rows', split_axis=0, concat_axis=0, tiled=True)  3.85 us
  transfers between devices with their start and end apart: 12, of which 8 were waited for; matrix products, arithmetic and copies ran while one was open for 3% of the time, Pallas kernels for 0%

profile of v1, /device:TPU:1, one launch (start us, length us, event | category | flops | bytes accessed | tf_op | source)
XLA Modules:
  0.0 91.4 jit_solution(5902080834973205395)
XLA Ops:
  0.6 0.9 %copy.89 = s32[4,4]{1,0:T(4,128)S(1)} copy(s32[4,4]{0,1:T(4,128)} %bitcast.112) | data formatting | bytes 128 | tf_op jit(solution)/shard_map/transpose | solution.py:115
  1.6 0.6 broadcast_in_dim.47
  2.3 11.3 %all-to-all-start = ((s32[32,1,16]{2,1,0:T(1,128)}), s32[32,1,16]{2,1,0:T(1,128)S(1)}, u32[]{:S(2)}, u32[]{:S(2)}) async-start(s32[32,1,16]{2,1,0:T(1,128)} %broadcast_in_dim.47), calls=%async_computation | async-start | bytes 32768 | tf_op jit(solution)/shard_map/all_to_all | solution.py:116
  13.6 0.7 fusion.77
  14.3 0.7 iota_compare_fusion.1
  15.0 7.1 %all-to-all-done = s32[32,1,16]{2,1,0:T(1,128)S(1)} async-done(((s32[32,1,16]{2,1,0:T(1,128)}), s32[32,1,16]{2,1,0:T(1,128)S(1)}, u32[]{:S(2)}, u32[]{:S(2)}) %all-to-all-start) | async-done | bytes 2080 | tf_op jit(solution)/shard_map/all_to_all | solution.py:116
  22.2 0.5 broadcast.154
  22.7 0.7 reduce.15
  23.5 3.8 %copy-done.1 = bf16[76032,1,64]{0,2,1:T(8,128)(2,1)S(1)} copy-done((bf16[76032,1,64]{0,2,1:T(8,128)(2,1)S(1)}, bf16[76032,1,64]{0,2,1:T(8,128)(2,1)}, u32[]{:S(2)}) %copy-start.1) | copy-done | bytes 9732120
  27.2 10.8 %pick_rows.1 = bf16[256,128]{1,0:T(8,128)(2,1)} custom-call(s32[512]{0:T(512)S(1)} %reshape.245.token_ref, bf16[64,76032]{1,0:T(8,128)(2,1)S(1)} %bitcast.101), custom_call_target="tpu_custom_call" | custom-call | tf_op jit(solution)/shard_map/pick_rows/pallas_call | solution.py:49
  38.0 3.9 %all-to-all-start.1 = ((bf16[32,8,128]{2,1,0:T(8,128)(2,1)}), bf16[32,8,128]{2,1,0:T(8,128)(2,1)S(1)}, u32[]{:S(2)}, u32[]{:S(2)}) async-start(bf16[32,8,128]{2,1,0:T(8,128)(2,1)} %bitcast.3), calls=%async_computation.1 | async-start | bytes 131072 | tf_op jit(solution)/shard_map/all_to_all | solution.py:122
  41.9 8.9 %all-to-all-done.1 = bf16[32,8,128]{2,1,0:T(8,128)(2,1)S(1)} async-done(((bf16[32,8,128]{2,1,0:T(8,128)(2,1)}), bf16[32,8,128]{2,1,0:T(8,128)(2,1)S(1)}, u32[]{:S(2)}, u32[]{:S(2)}) %all-to-all-start.1) | async-done | bytes 65568 | tf_op jit(solution)/shard_map/all_to_all | solution.py:122
  50.8 0.2 reshape.266
  51.0 0.1 copy.90
  51.2 0.1 reduce_sum.83
  51.5 0.1 reshape.265
  51.6 3.0 %fusion.51 = f32[16,1024]{1,0:T(8,128)S(1)} fusion(bf16[2048,1024]{1,0:T(8,128)(2,1)} %param.19, f32[16,2048]{1,0:T(8,128)S(1)} %reshape.265, f32[2048]{0:T(1024)S(1)} %get-tuple-element.33), kind=kOutput, calls=%fused_computation.59 | convolution fusion | flops 67174400 | bytes 4399104 | tf_op jit(solution)/shard_map/dot_general | solution.py:129
  54.6 0.4 copy-done.2
  55.1 0.7 fusion.52
  55.8 3.5 %collective-permute-start.2 = (f32[16,640]{1,0:T(8,128)S(1)}, f32[16,640]{1,0:T(8,128)S(1)}, u32[]{:S(2)}, u32[]{:S(2)}) collective-permute-start(f32[16,640]{1,0:T(8,128)S(1)} %get-tuple-element.32), channel_id=1, source_target_pairs={{0,3},{1,2},{2,1},{3,0},{4,7},{5,6},{6,5},{7,4},{8,11},{9,10},{10,... | collective-permute-start | bytes 122888 | tf_op jit(solution)/shard_map/ppermute | solution.py:64
  59.3 1.2 %collective-permute-start.1 = (f32[16,640]{1,0:T(8,128)S(1)}, f32[16,640]{1,0:T(8,128)S(1)}, u32[]{:S(2)}, u32[]{:S(2)}) collective-permute-start(f32[16,640]{1,0:T(8,128)S(1)} %get-tuple-element.31), channel_id=1, source_target_pairs={{0,2},{1,3},{2,0},{3,1},{4,6},{5,7},{6,4},{7,5},{8,10},{9,11},{10,... | collective-permute-start | bytes 122888 | tf_op jit(solution)/shard_map/ppermute | solution.py:64
  60.4 0.1 reshape.264
  60.5 0.4 collective-permute-done.2
  61.0 1.8 %collective-permute-done.1 = f32[16,640]{1,0:T(8,128)S(1)} collective-permute-done((f32[16,640]{1,0:T(8,128)S(1)}, f32[16,640]{1,0:T(8,128)S(1)}, u32[]{:S(2)}, u32[]{:S(2)}) %collective-permute-start.1) | collective-permute-done | bytes 40992 | tf_op jit(solution)/shard_map/ppermute | solution.py:64
  62.8 0.2 multiply_reduce_fusion.3
  63.0 0.1 mul.173
  63.2 0.1 mul.174
  63.4 0.2 fusion.79
  63.6 0.9 fusion.78
  64.5 0.3 fusion.31
  64.9 0.2 fusion.56
  65.1 0.5 fusion.27
  65.7 0.1 copy.167
  65.9 1.1 %collective-permute-start.3 = (bf16[16,2048]{1,0:T(8,128)(2,1)S(1)}, bf16[16,2048]{1,0:T(8,128)(2,1)S(1)}, u32[]{:S(2)}, u32[]{:S(2)}) collective-permute-start(bf16[16,2048]{1,0:T(8,128)(2,1)S(1)} %add_convert_fusion), channel_id=1, source_target_pairs={{0,64},{4,68},{8,72},{12,76},{16,80},{20,84},{24,88},{28,92},{32,9... | collective-permute-start | bytes 196616 | tf_op jit(solution)/shard_map/ppermute | solution.py:69
  67.0 3.5 %collective-permute-done.3 = bf16[16,2048]{1,0:T(8,128)(2,1)S(1)} collective-permute-done((bf16[16,2048]{1,0:T(8,128)(2,1)S(1)}, bf16[16,2048]{1,0:T(8,128)(2,1)S(1)}, u32[]{:S(2)}, u32[]{:S(2)}) %collective-permute-start.3) | collective-permute-done | bytes 65568 | tf_op jit(solution)/shard_map/ppermute | solution.py:69
  70.6 0.1 fusion.40
  70.8 1.7 %collective-permute-start.4 = (f32[16,128]{1,0:T(8,128)S(1)}, f32[16,128]{1,0:T(8,128)S(1)}, u32[]{:S(2)}, u32[]{:S(2)}) collective-permute-start(f32[16,128]{1,0:T(8,128)S(1)} %broadcast_in_dim.56), channel_id=1, source_target_pairs={{0,1},{1,0},{2,3},{3,2},{4,5},{5,4},{6,7},{7,6},{8,9},{9,8},{10,11... | collective-permute-start | bytes 24584 | tf_op jit(solution)/shard_map/ppermute | solution.py:64
  72.5 0.4 collective-permute-start.6
  72.9 1.0 %collective-permute-start.5 = (f32[16,128]{1,0:T(8,128)S(1)}, f32[16,128]{1,0:T(8,128)S(1)}, u32[]{:S(2)}, u32[]{:S(2)}) collective-permute-start(f32[16,128]{1,0:T(8,128)S(1)} %broadcast_in_dim.56), channel_id=1, source_target_pairs={{0,2},{1,3},{2,0},{3,1},{4,6},{5,7},{6,4},{7,5},{8,10},{9,11},{10,... | collective-permute-start | bytes 24584 | tf_op jit(solution)/shard_map/ppermute | solution.py:64
  74.0 0.5 multiply_add_fusion
  74.5 0.1 reshape.263
  74.6 0.1 reshape.254
  74.8 0.8 collective-permute-done.6
  75.6 0.2 fusion.65
  75.8 0.1 mul.191
  76.0 0.1 mul.192
  76.1 2.4 %fusion.24 = f32[4,2,32,1024]{3,2,1,0:T(8,128)S(1)} fusion(f32[4,32]{1,0:T(4,128)S(1)} %mul.192, pred[4,1024]{1,0:T(4,128)(4,1)S(1)} %iota_compare_fusion, bf16[4,2,4,8,128]{4,3,1,2,0:T(8,128)(2,1)S(1)} %bitcast.109, bf16[4,1024,256]{2,1,0:T(8,128)(2,1)} %param.24), kind=kOutput, calls=%fused_computation.18 | convolution fusion | flops 67633152 | bytes 3215872 | tf_op jit(solution)/shard_map/rkgd,rtkd->rkgt/dot_general | solution.py:87
  78.5 0.3 fusion.80
  78.8 2.9 %fusion.1 = f32[4,2,32,128]{3,2,1,0:T(8,128)} fusion(f32[4,2,32]{2,1,0:T(2,128)S(1)} %fusion.80, f32[4,2,32,1024]{3,2,1,0:T(8,128)S(1)} %fusion.24, bf16[4,1024,256]{2,1,0:T(8,128)(2,1)} %param.25), kind=kOutput, calls=%fused_computation.1 | convolution fusion | flops 67896576 | bytes 3277824 | tf_op jit(solution)/shard_map/rkgt,rtkd->rkgd/dot_general | solution.py:190
  81.7 0.9 %reshape.260 = f32[4,2,4,1024]{3,2,1,0:T(4,128)S(1)} reshape(f32[4,2,32,128]{3,2,1,0:T(8,128)} %fusion.1) | data formatting | bytes 262144 | tf_op jit(solution)/shard_map/reshape | solution.py:196
  82.7 0.1 copy.103
  82.8 0.1 multiply_reduce_fusion
  83.0 0.1 copy.104
  83.0 1.1 %fusion.39 = f32[16,51]{1,0:T(8,128)S(1)} fusion(bf16[2048,51]{0,1:T(8,128)(2,1)} %param.27, f32[16,2048]{1,0:T(8,128)S(1)} %bitcast.103, bf16[16,2048]{1,0:T(8,128)(2,1)S(1)} %collective-permute-done.3, f32[2048]{0:T(1024)S(1)} %convert_element_type.107), kind=kOutput, calls=%fused_computation.47 | convolution fusion | flops 3473408 | bytes 416960 | tf_op jit(solution)/shard_map/dot_general | solution.py:199
  84.2 1.4 %collective-permute-start.7 = (f32[16,52]{1,0:T(8,128)S(1)}, f32[16,52]{1,0:T(8,128)S(1)}, u32[]{:S(2)}, u32[]{:S(2)}) collective-permute-start(f32[16,52]{1,0:T(8,128)S(1)} %pad_maximum_fusion.4), channel_id=1, source_target_pairs={{0,1},{1,0},{2,3},{3,2},{4,5},{5,4},{6,7},{7,6},{8,9},{9,8},{10,11... | collective-permute-start | bytes 9992 | tf_op jit(solution)/shard_map/ppermute | solution.py:64
  85.7 1.1 %collective-permute-start.8 = (f32[16,52]{1,0:T(8,128)S(1)}, f32[16,52]{1,0:T(8,128)S(1)}, u32[]{:S(2)}, u32[]{:S(2)}) collective-permute-start(f32[16,52]{1,0:T(8,128)S(1)} %pad_maximum_fusion.4), channel_id=1, source_target_pairs={{0,2},{1,3},{2,0},{3,1},{4,6},{5,7},{6,4},{7,5},{8,10},{9,11},{10,... | collective-permute-start | bytes 9992 | tf_op jit(solution)/shard_map/ppermute | solution.py:64
  86.7 0.7 collective-permute-start.9
  87.4 0.7 copy.105
  88.2 1.6 %collective-permute-done.9 = f32[16,52]{1,0:T(8,128)S(1)} collective-permute-done((f32[16,52]{1,0:T(8,128)S(1)}, f32[16,52]{1,0:T(8,128)S(1)}, u32[]{:S(2)}, u32[]{:S(2)}) %collective-permute-start.9) | collective-permute-done | bytes 3360 | tf_op jit(solution)/shard_map/ppermute | solution.py:64
  89.9 0.2 fusion.59
  90.0 0.2 fusion.74
  90.2 0.2 fusion.72
  90.4 0.2 multiply_reduce_fusion.2
  90.7 0.7 copy.106
  (53 shorter events, 1.6 us)
Async XLA Ops:
  0.6 62.9 %copy-start = (bf16[4,1024,256]{2,1,0:T(8,128)(2,1)S(1)}, bf16[4,1024,256]{2,1,0:T(8,128)(2,1)}, u32[]{:S(2)}) copy-start(bf16[4,1024,256]{2,1,0:T(8,128)(2,1)} %param.20) | copy-start | bytes 6291460
  2.3 19.9 %all-to-all-start = ((s32[32,1,16]{2,1,0:T(1,128)}), s32[32,1,16]{2,1,0:T(1,128)S(1)}, u32[]{:S(2)}, u32[]{:S(2)}) async-start(s32[32,1,16]{2,1,0:T(1,128)} %broadcast_in_dim.47), calls=%async_computation | async-start | bytes 32768 | tf_op jit(solution)/shard_map/all_to_all | solution.py:116
  23.5 3.8 %copy-start.1 = (bf16[76032,1,64]{0,2,1:T(8,128)(2,1)S(1)}, bf16[76032,1,64]{0,2,1:T(8,128)(2,1)}, u32[]{:S(2)}) copy-start(bf16[76032,1,64]{0,2,1:T(8,128)(2,1)} %param.16) | copy-start | bytes 29196292
  38.0 12.8 %all-to-all-start.1 = ((bf16[32,8,128]{2,1,0:T(8,128)(2,1)}), bf16[32,8,128]{2,1,0:T(8,128)(2,1)S(1)}, u32[]{:S(2)}, u32[]{:S(2)}) async-start(bf16[32,8,128]{2,1,0:T(8,128)(2,1)} %bitcast.3), calls=%async_computation.1 | async-start | bytes 131072 | tf_op jit(solution)/shard_map/all_to_all | solution.py:122
  51.6 3.5 %copy-start.2 = (bf16[2048,1024]{1,0:T(8,128)(2,1)S(1)}, bf16[2048,1024]{1,0:T(8,128)(2,1)}, u32[]{:S(2)}) copy-start(bf16[2048,1024]{1,0:T(8,128)(2,1)} %param.18) | copy-start | bytes 12582916
  55.8 5.1 %collective-permute-start.2 = (f32[16,640]{1,0:T(8,128)S(1)}, f32[16,640]{1,0:T(8,128)S(1)}, u32[]{:S(2)}, u32[]{:S(2)}) collective-permute-start(f32[16,640]{1,0:T(8,128)S(1)} %get-tuple-element.32), channel_id=1, source_target_pairs={{0,3},{1,2},{2,1},{3,0},{4,7},{5,6},{6,5},{7,4},{8,11},{9,10},{10,... | collective-permute-start | bytes 122888 | tf_op jit(solution)/shard_map/ppermute | solution.py:64
  59.3 3.5 %collective-permute-start.1 = (f32[16,640]{1,0:T(8,128)S(1)}, f32[16,640]{1,0:T(8,128)S(1)}, u32[]{:S(2)}, u32[]{:S(2)}) collective-permute-start(f32[16,640]{1,0:T(8,128)S(1)} %get-tuple-element.31), channel_id=1, source_target_pairs={{0,2},{1,3},{2,0},{3,1},{4,6},{5,7},{6,4},{7,5},{8,10},{9,11},{10,... | collective-permute-start | bytes 122888 | tf_op jit(solution)/shard_map/ppermute | solution.py:64
  60.4 2.4 %collective-permute-start = (f32[16,640]{1,0:T(8,128)S(1)}, f32[16,640]{1,0:T(8,128)S(1)}, u32[]{:S(2)}, u32[]{:S(2)}) collective-permute-start(f32[16,640]{1,0:T(8,128)S(1)} %get-tuple-element.30), channel_id=1, source_target_pairs={{0,1},{1,0},{2,3},{3,2},{4,5},{5,4},{6,7},{7,6},{8,9},{9,8},{10,11... | collective-permute-start | bytes 122888 | tf_op jit(solution)/shard_map/ppermute | solution.py:64
  63.5 1.6 %copy-start.7 = (bf16[4,1024,256]{2,1,0:T(8,128)(2,1)S(1)}, bf16[4,1024,256]{2,1,0:T(8,128)(2,1)}, u32[]{:S(2)}) copy-start(bf16[4,1024,256]{2,1,0:T(8,128)(2,1)} %param.21) | copy-start | bytes 6291460
  65.1 1.8 %copy-start.5 = (s32[4]{0:T(128)S(1)}, s32[4]{0:T(128)}, u32[]{:S(2)}) copy-start(s32[4]{0:T(128)} %param.22) | copy-start | bytes 52
  65.1 1.9 %copy-start.3 = (bf16[2048]{0:T(1024)(128)(2,1)S(1)}, bf16[2048]{0:T(1024)(128)(2,1)}, u32[]{:S(2)}) copy-start(bf16[2048]{0:T(1024)(128)(2,1)} %param.23) | copy-start | bytes 12292
  65.1 9.3 %copy-start.4 = (bf16[2048]{0:T(1024)(128)(2,1)S(1)}, bf16[2048]{0:T(1024)(128)(2,1)}, u32[]{:S(2)}) copy-start(bf16[2048]{0:T(1024)(128)(2,1)} %param.26) | copy-start | bytes 12292
  65.9 4.7 %collective-permute-start.3 = (bf16[16,2048]{1,0:T(8,128)(2,1)S(1)}, bf16[16,2048]{1,0:T(8,128)(2,1)S(1)}, u32[]{:S(2)}, u32[]{:S(2)}) collective-permute-start(bf16[16,2048]{1,0:T(8,128)(2,1)S(1)} %add_convert_fusion), channel_id=1, source_target_pairs={{0,64},{4,68},{8,72},{12,76},{16,80},{20,84},{24,88},{28,92},{32,9... | collective-permute-start | bytes 196616 | tf_op jit(solution)/shard_map/ppermute | solution.py:69
  70.8 4.0 %collective-permute-start.4 = (f32[16,128]{1,0:T(8,128)S(1)}, f32[16,128]{1,0:T(8,128)S(1)}, u32[]{:S(2)}, u32[]{:S(2)}) collective-permute-start(f32[16,128]{1,0:T(8,128)S(1)} %broadcast_in_dim.56), channel_id=1, source_target_pairs={{0,1},{1,0},{2,3},{3,2},{4,5},{5,4},{6,7},{7,6},{8,9},{9,8},{10,11... | collective-permute-start | bytes 24584 | tf_op jit(solution)/shard_map/ppermute | solution.py:64
  72.5 3.1 %collective-permute-start.6 = (f32[16,128]{1,0:T(8,128)S(1)}, f32[16,128]{1,0:T(8,128)S(1)}, u32[]{:S(2)}, u32[]{:S(2)}) collective-permute-start(f32[16,128]{1,0:T(8,128)S(1)} %broadcast_in_dim.56), channel_id=1, source_target_pairs={{0,3},{1,2},{2,1},{3,0},{4,7},{5,6},{6,5},{7,4},{8,11},{9,10},{10,... | collective-permute-start | bytes 24584 | tf_op jit(solution)/shard_map/ppermute | solution.py:64
  72.9 2.7 %collective-permute-start.5 = (f32[16,128]{1,0:T(8,128)S(1)}, f32[16,128]{1,0:T(8,128)S(1)}, u32[]{:S(2)}, u32[]{:S(2)}) collective-permute-start(f32[16,128]{1,0:T(8,128)S(1)} %broadcast_in_dim.56), channel_id=1, source_target_pairs={{0,2},{1,3},{2,0},{3,1},{4,6},{5,7},{6,4},{7,5},{8,10},{9,11},{10,... | collective-permute-start | bytes 24584 | tf_op jit(solution)/shard_map/ppermute | solution.py:64
  78.8 11.6 %copy-start.6 = (f32[51]{0:T(128)S(1)}, f32[51]{0:T(128)}, u32[]{:S(2)}) copy-start(f32[51]{0:T(128)} %multiply_add_fusion) | copy-start | bytes 616
  84.2 3.9 %collective-permute-start.7 = (f32[16,52]{1,0:T(8,128)S(1)}, f32[16,52]{1,0:T(8,128)S(1)}, u32[]{:S(2)}, u32[]{:S(2)}) collective-permute-start(f32[16,52]{1,0:T(8,128)S(1)} %pad_maximum_fusion.4), channel_id=1, source_target_pairs={{0,1},{1,0},{2,3},{3,2},{4,5},{5,4},{6,7},{7,6},{8,9},{9,8},{10,11... | collective-permute-start | bytes 9992 | tf_op jit(solution)/shard_map/ppermute | solution.py:64
  85.7 2.5 %collective-permute-start.8 = (f32[16,52]{1,0:T(8,128)S(1)}, f32[16,52]{1,0:T(8,128)S(1)}, u32[]{:S(2)}, u32[]{:S(2)}) collective-permute-start(f32[16,52]{1,0:T(8,128)S(1)} %pad_maximum_fusion.4), channel_id=1, source_target_pairs={{0,2},{1,3},{2,0},{3,1},{4,6},{5,7},{6,4},{7,5},{8,10},{9,11},{10,... | collective-permute-start | bytes 9992 | tf_op jit(solution)/shard_map/ppermute | solution.py:64
  86.7 3.1 %collective-permute-start.9 = (f32[16,52]{1,0:T(8,128)S(1)}, f32[16,52]{1,0:T(8,128)S(1)}, u32[]{:S(2)}, u32[]{:S(2)}) collective-permute-start(f32[16,52]{1,0:T(8,128)S(1)} %pad_maximum_fusion.4), channel_id=1, source_target_pairs={{0,3},{1,2},{2,1},{3,0},{4,7},{5,6},{6,5},{7,4},{8,11},{9,10},{10,... | collective-permute-start | bytes 9992 | tf_op jit(solution)/shard_map/ppermute | solution.py:64

commit v2 on v0

v2 whole, which is shorter than its diff:
```python
import functools
import math

import jax
import jax.numpy as jnp
from jax import lax
from jax.experimental import pallas as pl
from jax.experimental.pallas import tpu as pltpu
from jax.sharding import PartitionSpec as P

D = 8192
HEAD_DIM = 128
GROUP = 8
ATOMS = 51
LANES = 128
HALF = 64
MIB = 1024 * 1024

norm_eps = 1e-06
atom_span = 10.0
masked = -1e30
attn_scale = 1.0 / math.sqrt(HEAD_DIM)

SMEM = pl.BlockSpec(memory_space=pltpu.SMEM)
VMEM = pl.BlockSpec(memory_space=pltpu.VMEM)
NT = (((1,), (1,)), ((), ()))


def kernel_call(body, outs, specs, scratch=(), limit=16, flops=0, moved=0, name=None):
    return pl.pallas_call(
        body,
        out_shape=outs,
        in_specs=specs,
        out_specs=jax.tree.map(lambda _: VMEM, outs),
        scratch_shapes=scratch,
        compiler_params=pltpu.CompilerParams(vmem_limit_bytes=limit * MIB),
        cost_estimate=pl.CostEstimate(flops=flops, bytes_accessed=moved, transcendentals=0),
        name=name,
    )


def array(shape, dtype):
    return jax.ShapeDtypeStruct(shape, dtype)


def pick_rows_kernel(token_ref, table_ref, out_ref):
    width = table_ref.shape[0]
    lane = lax.broadcasted_iota(jnp.int32, (width, LANES), 1)

    def column(token, place):
        block = pl.multiple_of(jnp.bitwise_and(token, ~(LANES - 1)), LANES)
        tile = table_ref[:, pl.ds(block, LANES)].astype(jnp.float32)
        return pltpu.roll(tile, jnp.bitwise_and(place - token, LANES - 1), 1)

    for group in range(out_ref.shape[0] // LANES):

        def step(place, carry):
            first, second = carry
            destination = group * (LANES // 8) + lax.shift_right_logical(place, 3)
            decode_step = jnp.bitwise_and(place, 3)
            row = jnp.bitwise_and(lax.shift_right_logical(place, 2), 1)
            here = lane == place
            first = jnp.where(here, column(token_ref[destination, decode_step, row], place), first)
            second = jnp.where(
                here, column(token_ref[destination, decode_step, row + 2], place), second
            )
            return first, second

        empty = jnp.zeros((width, LANES), jnp.float32)
        first, second = lax.fori_loop(0, LANES, step, (empty, empty), unroll=32)
        both = jnp.concatenate([first, second], axis=0)
        out_ref[pl.ds(group * LANES, LANES), :] = both.T.astype(out_ref.dtype)


def pick_rows(tokens, table):
    rows = tokens.size * table.shape[0] // LANES
    return kernel_call(
        pick_rows_kernel, array((rows, LANES), table.dtype), [SMEM, VMEM], name="pick_rows"
    )(tokens, table)


def project_kernel(
    tp_ref, blocks_ref, gain_ref, key_ref, value_ref, x_ref, query_ref, *rest
):
    parts, (gained_ref, placed_ref) = rest[:4], rest[4:]
    count, width = x_ref.shape
    kv_width = key_ref.shape[1] // 4
    left = lax.broadcasted_iota(jnp.int32, (8, LANES), 1) < HALF
    squares = jnp.zeros((count, LANES), jnp.float32)
    for k in range(width // LANES):
        pair = blocks_ref[pl.ds(16 * k, 16), :].astype(jnp.float32)
        one, two = pair[:8], pair[8:]
        low = jnp.where(left, one, pltpu.roll(two, HALF, 1))
        high = jnp.where(left, pltpu.roll(one, HALF, 1), two)
        x = jnp.concatenate([low, high], axis=0)
        squares += x * x
        columns = pl.ds(k * LANES, LANES)
        x_ref[:, columns] = x.astype(x_ref.dtype)
        gained = x * gain_ref[:, columns]
        gained_ref[:, columns] = gained.astype(gained_ref.dtype)
        head, group = divmod(k, GROUP)
        for row in range(4):
            placed_ref[2 * row + head, pl.ds(4 * group, 4), :] = gained[4 * row : 4 * row + 4]
    query_ref[...] = placed_ref[...].astype(query_ref.dtype)
    total = jnp.broadcast_to(jnp.sum(squares, axis=1, keepdims=True), (count, LANES))
    gained = gained_ref[...]
    for by, part_ref in enumerate(parts):
        start = pl.multiple_of(jnp.bitwise_xor(tp_ref[0], by) * kv_width, kv_width)
        peer = pl.ds(start, kv_width)
        part_ref[:, :kv_width] = jnp.dot(
            gained, key_ref[:, peer], preferred_element_type=jnp.float32
        )
        part_ref[:, kv_width : 2 * kv_width] = jnp.dot(
            gained, value_ref[:, peer], preferred_element_type=jnp.float32
        )
        part_ref[:, 2 * kv_width :] = total


def project(tp, blocks, gain, key_weight, value_weight):
    width, kv_all = key_weight.shape
    count = blocks.shape[0] * LANES // width
    part = array((count, kv_all // 2 + LANES), jnp.float32)
    heads = width // (GROUP * HEAD_DIM)
    queries = (4 * heads, 4 * GROUP, HEAD_DIM)
    x, query, *parts = kernel_call(
        project_kernel,
        (array((count, width), jnp.bfloat16), array(queries, jnp.bfloat16)) + (part,) * 4,
        [SMEM] + [VMEM] * 4,
        scratch=[pltpu.VMEM((count, width), jnp.bfloat16), pltpu.VMEM(queries, jnp.float32)],
        flops=4 * count * width * kv_all,
        moved=4 * width * kv_all,
        name="project",
    )(tp, blocks, gain, key_weight, value_weight)
    return x, query, parts


def scores_kernel(query_ref, keys_ref, out_ref):
    for at in range(query_ref.shape[0]):
        row, head = divmod(at, 2)
        keys = keys_ref[row, :, pl.ds(head * HEAD_DIM, HEAD_DIM)]
        out_ref[at] = lax.dot_general(
            query_ref[at], keys, NT, preferred_element_type=jnp.float32
        )


def raw_scores(query, keys, name):
    out = array(query.shape[:2] + (keys.shape[1],), jnp.float32)
    return kernel_call(
        scores_kernel,
        out,
        [VMEM, VMEM],
        flops=2 * out.size * HEAD_DIM,
        moved=2 * keys.size + 4 * out.size,
        name=name,
    )(query, keys)


def spread_rows(inv, spread_ref):
    for row in range(4):
        for group in range(GROUP):
            spread_ref[row, pl.ds(4 * group, 4), :] = inv[4 * row : 4 * row + 4]


def scaled_scores(raw, spread, length):
    wide = jnp.concatenate([spread] * (raw.shape[1] // LANES), axis=1)
    visible = lax.broadcasted_iota(jnp.int32, raw.shape, 1) < length
    return jnp.where(visible, raw * wide, masked)


def policy_kernel(
    length_ref,
    own_ref,
    one_ref,
    two_ref,
    three_ref,
    raw_ref,
    query_ref,
    x_ref,
    values_ref,
    passed_ref,
    squares_ref,
    hidden_ref,
    spread_ref,
    rows_ref,
):
    count, width = x_ref.shape
    kv_width = values_ref.shape[2]
    total = own_ref[...] + (one_ref[...] + (two_ref[...] + three_ref[...]))
    inv = lax.rsqrt(total[:, 2 * kv_width :] * (1.0 / D) + norm_eps)
    wide = jnp.concatenate([inv] * (kv_width // LANES), axis=1)
    new_key = (wide * total[:, :kv_width]).astype(jnp.bfloat16)
    new_value = (wide * total[:, kv_width : 2 * kv_width]).astype(jnp.bfloat16)
    spread_rows(inv * attn_scale, spread_ref)
    queries = query_ref.shape[1]
    query_step = jnp.bitwise_and(lax.broadcasted_iota(jnp.int32, (queries, count), 0), 3)
    fresh = lax.broadcasted_iota(jnp.int32, (queries, count), 1)
    earlier = jnp.bitwise_and(fresh, 3) <= query_step
    for at in range(query_ref.shape[0]):
        row, head = divmod(at, 2)
        columns = slice(head * HEAD_DIM, (head + 1) * HEAD_DIM)
        spread = spread_ref[row]
        scores = scaled_scores(raw_ref[at], spread, length_ref[row])
        extra = lax.dot_general(
            query_ref[at], new_key[:, columns], NT, preferred_element_type=jnp.float32
        )
        mine = jnp.logical_and(lax.shift_right_logical(fresh, 2) == row, earlier)
        extra = jnp.where(mine, extra * spread[:, :count], masked)
        highest = jnp.maximum(
            jnp.max(scores, axis=1, keepdims=True), jnp.max(extra, axis=1, keepdims=True)
        )
        weights = jnp.exp(scores - highest)
        extra = jnp.exp(extra - highest)
        inverse = 1.0 / (
            jnp.sum(weights, axis=1, keepdims=True) + jnp.sum(extra, axis=1, keepdims=True)
        )
        attended = jnp.dot(
            weights.astype(jnp.bfloat16),
            values_ref[row, :, columns],
            preferred_element_type=jnp.float32,
        ) + jnp.dot(
            extra.astype(jnp.bfloat16), new_value[:, columns], preferred_element_type=jnp.float32
        )
        attended = attended * inverse
        for group in range(GROUP):
            rows_ref[head * GROUP + group, pl.ds(4 * row, 4), :] = attended[
                4 * group : 4 * group + 4
            ]
    squares = jnp.zeros((count, LANES), jnp.float32)
    for k in range(width // LANES):
        columns = pl.ds(k * LANES, LANES)
        hidden = (x_ref[:, columns].astype(jnp.float32) + rows_ref[k]).astype(jnp.bfloat16)
        passed_ref[:, columns] = hidden
        hidden = hidden.astype(jnp.float32)
        squares += hidden * hidden
        rows_ref[k] = hidden
    squares_ref[...] = jnp.broadcast_to(
        jnp.sum(squares, axis=1, keepdims=True), squares_ref.shape
    )
    for step in range(4):
        for k in range(width // LANES):
            columns = pl.ds(k * LANES, LANES)
            hidden_ref[step, :, columns] = rows_ref[k, pl.ds(step, 4, stride=4), :].astype(
                hidden_ref.dtype
            )


def policy(lengths, parts, raw, query, x, values):
    count, width = x.shape
    return kernel_call(
        policy_kernel,
        (
            array((count, width), jnp.bfloat16),
            array((count, LANES), jnp.float32),
            array((4, 4, width), jnp.bfloat16),
        ),
        [SMEM] + [VMEM] * 8,
        scratch=[
            pltpu.VMEM((4, 4 * GROUP, LANES), jnp.float32),
            pltpu.VMEM((width // LANES, count, LANES), jnp.float32),
        ],
        flops=2 * raw.size * HEAD_DIM,
        moved=2 * values.size + 4 * raw.size,
        name="policy",
    )(lengths, *parts, raw, query, x, values)


def critic_scores_kernel(rows_ref, gain_ref, keys_ref, out_ref, placed_ref):
    for k in range(rows_ref.shape[1] // LANES):
        columns = pl.ds(k * LANES, LANES)
        gained = rows_ref[:, columns].astype(jnp.float32) * gain_ref[:, columns]
        head, group = divmod(k, GROUP)
        for row in range(4):
            placed_ref[2 * row + head, pl.ds(4 * group, 4), :] = gained[4 * row : 4 * row + 4]
    for at in range(placed_ref.shape[0]):
        row, head = divmod(at, 2)
        keys = keys_ref[row, :, pl.ds(head * HEAD_DIM, HEAD_DIM)]
        out_ref[at] = lax.dot_general(
            placed_ref[at].astype(jnp.bfloat16), keys, NT, preferred_element_type=jnp.float32
        )


def critic_scores(rows, gain, keys):
    heads = keys.shape[2] // HEAD_DIM
    placed = (4 * heads, 4 * GROUP, HEAD_DIM)
    out = array(placed[:2] + (keys.shape[1],), jnp.float32)
    return kernel_call(
        critic_scores_kernel,
        out,
        [VMEM] * 3,
        scratch=[pltpu.VMEM(placed, jnp.float32)],
        flops=2 * out.size * HEAD_DIM,
        moved=2 * keys.size + 4 * out.size,
        name="critic_scores",
    )(rows, gain, keys)


def critic_kernel(
    length_ref,
    own_ref,
    one_ref,
    two_ref,
    three_ref,
    raw_ref,
    rows_ref,
    gain_ref,
    values_ref,
    head_ref,
    out_ref,
    spread_ref,
    attended_ref,
    scaled_ref,
):
    count, width = rows_ref.shape
    total = own_ref[...] + (one_ref[...] + (two_ref[...] + three_ref[...]))
    spread_rows(lax.rsqrt(total * (1.0 / D) + norm_eps) * attn_scale, spread_ref)
    for at in range(raw_ref.shape[0]):
        row, head = divmod(at, 2)
        columns = slice(head * HEAD_DIM, (head + 1) * HEAD_DIM)
        scores = scaled_scores(raw_ref[at], spread_ref[row], length_ref[row])
        weights = jnp.exp(scores - jnp.max(scores, axis=1, keepdims=True))
        inverse = 1.0 / jnp.sum(weights, axis=1, keepdims=True)
        attended = inverse * jnp.dot(
            weights.astype(jnp.bfloat16),
            values_ref[row, :, columns],
            preferred_element_type=jnp.float32,
        )
        for group in range(GROUP):
            at_columns = pl.ds((head * GROUP + group) * HEAD_DIM, HEAD_DIM)
            attended_ref[pl.ds(4 * row, 4), at_columns] = attended[4 * group : 4 * group + 4]
    squares = jnp.zeros((count, LANES), jnp.float32)
    for k in range(width // LANES):
        columns = pl.ds(k * LANES, LANES)
        combined = rows_ref[:, columns].astype(jnp.float32) + attended_ref[:, columns]
        squares += combined * combined
        scaled_ref[:, columns] = (combined * gain_ref[:, columns]).astype(scaled_ref.dtype)
    logits = lax.dot_general(
        scaled_ref[...], head_ref[...], NT, preferred_element_type=jnp.float32
    )
    out_ref[...] = jnp.broadcast_to(jnp.sum(squares, axis=1, keepdims=True), (count, LANES))
    out_ref[:, :ATOMS] = logits


def critic(lengths, parts, raw, rows, gain, values, head):
    count, width = rows.shape
    return kernel_call(
        critic_kernel,
        array((count, LANES), jnp.float32),
        [SMEM] + [VMEM] * 9,
        scratch=[
            pltpu.VMEM((4, 4 * GROUP, LANES), jnp.float32),
            pltpu.VMEM((count, width), jnp.float32),
            pltpu.VMEM((count, width), jnp.bfloat16),
        ],
        flops=2 * raw.size * HEAD_DIM,
        moved=2 * values.size + 4 * raw.size,
        name="critic",
    )(lengths, *parts, raw, rows, gain, values, head)


def expect_kernel(own_ref, one_ref, two_ref, three_ref, out_ref):
    total = own_ref[...] + (one_ref[...] + (two_ref[...] + three_ref[...]))
    lane = lax.broadcasted_iota(jnp.int32, total.shape, 1)
    at = lax.broadcasted_iota(jnp.int32, total.shape, 0)
    logits = lax.rsqrt(total[:, LANES - 1 :] * (1.0 / D) + norm_eps) * total
    real = lane < ATOMS
    logits = jnp.where(real, logits, masked)
    weights = jnp.exp(logits - jnp.max(logits, axis=1, keepdims=True))
    atoms = -atom_span + 2.0 * atom_span * lane.astype(jnp.float32) / (ATOMS - 1)
    value = jnp.sum(weights * atoms, axis=1, keepdims=True) / jnp.sum(
        weights, axis=1, keepdims=True
    )
    placed = jnp.where(lane == lax.shift_right_logical(at, 2), value, 0.0)
    rows = [
        jnp.sum(jnp.where(jnp.bitwise_and(at, 3) == step, placed, 0.0), axis=0, keepdims=True)
        for step in range(4)
    ]
    out_ref[...] = jnp.concatenate(rows, axis=0)[:, :4]


def expect(parts):
    return kernel_call(expect_kernel, array((4, 4), jnp.float32), [VMEM] * 4, name="expect")(*parts)


def swapped(shard, by):
    peers = lax.axis_size("tp")
    return lax.ppermute(shard, "tp", [(i, i ^ by) for i in range(peers)])


def passed_along(shard, axis, by):
    peers = lax.axis_size(axis)
    return lax.ppermute(shard, axis, [(i, (i + by) % peers) for i in range(peers)])


def with_peers(shard):
    return [shard] + [swapped(shard, by) for by in (1, 2, 3)]


def on_device(
    tokens,
    lengths,
    embedding,
    attn_gain,
    key_weight,
    value_weight,
    policy_keys,
    policy_values,
    critic_lengths,
    critic_gain,
    critic_keys,
    critic_values,
    value_gain,
    value_head,
):
    row_groups = lax.axis_size("rows")
    tp = lax.axis_index("tp").astype(jnp.int32).reshape(1)

    def as_row(gain):
        return gain.astype(jnp.float32).reshape(1, -1)

    table = embedding.transpose(1, 2, 0).reshape(embedding.shape[2], embedding.shape[0])
    all_tokens = lax.all_to_all(
        jnp.broadcast_to(tokens[None], (row_groups,) + tokens.shape), "rows", 0, 0
    )
    picked = pick_rows(all_tokens, table)
    blocks = lax.all_to_all(picked.reshape(row_groups, -1, LANES), "rows", 0, 0)
    x, query, parts = project(
        tp, blocks.reshape(picked.shape), as_row(attn_gain), key_weight, value_weight
    )
    arrived = parts[:1] + [swapped(parts[by], by) for by in (1, 2, 3)]
    raw = raw_scores(query, policy_keys, "policy_scores")
    passed, squares, hidden = policy(lengths, arrived, raw, query, x, policy_values)

    rows = passed_along(passed, "rows", row_groups // 2)
    squares = passed_along(squares, "rows", row_groups // 2)
    raw = critic_scores(rows, as_row(critic_gain), critic_keys)
    logits = critic(
        critic_lengths,
        with_peers(squares),
        raw,
        rows,
        as_row(value_gain),
        critic_values,
        value_head.T,
    )
    values = expect(with_peers(logits))
    return hidden, values


def solution(mesh):
    placed = (
        P(None, "rows"),
        P("rows"),
        P(None, "rows", "tp"),
        P("tp"),
        P("tp", None),
        P("tp", None),
        P("rows", None, "tp"),
        P("rows", None, "tp"),
        P("rows"),
        P("tp"),
        P("rows", None, "tp"),
        P("rows", None, "tp"),
        P("tp"),
        P("tp", None),
    )
    return jax.shard_map(
        on_device,
        mesh=mesh,
        in_specs=placed,
        out_specs=(P(None, "rows", "tp"), P(None, "rows")),
        check_vma=False,
    )
```

time: 276 us -> 76.3 us (0.28)
  blocking collectives: 99.1 us -> 20 us
  matrix products: 46.8 us -> 0 us
  waiting for transfers between devices: 60.3 us -> 16.1 us
  local copies, waits for them, and re-layouts: 31.9 us -> 8.88 us
  between operations: 14.5 us -> 0.75 us
  Pallas kernels: 0 us -> 13.7 us
  other arithmetic: 11.6 us -> 0.01 us
  starting transfers between devices: 10.3 us -> 16.6 us
    all_gather x1 -> x0, blocking collectives: 83.3 us -> none  [on_device(): all_tokens = lax.all_gather(tokens, 'rows', axis=1, tiled=True)]
    psum x1 -> x0, waiting for transfers between devices: 48.2 us -> none  [on_device(): lax.psum((part_keys, part_values, jnp.sum(picked_f * picked_f, axis=-1)),...]
    dot_general x35 -> x0, matrix products: 46.8 us -> none  [the longest x8 14.7 us: attend(): jnp.einsum('rkgt,rtkd->rkgd', probs, cache_values, preferred_element_type...]
    all_to_all x0 -> x1, blocking collectives: none -> 20 us  [on_device(): lax.all_to_all(jnp.broadcast_to(tokens[None], (row_groups,) + tokens.shap...]
    psum x2 -> x0, blocking collectives: 15.9 us -> none  [the longest x1 9.75 us: on_device(): lax.psum((part_logits, jnp.sum(combined * combined, axis=-1)), 'tp')]
    pallas_call x0 -> x7, Pallas kernels: none -> 13.7 us  [the longest x1 5.29 us: pick_rows(): kernel_call(pick_rows_kernel, array((rows, LANES), table.dtype), [SMEM, V...]
    unnamed x31 -> x26, local copies, waits for them, and re-layouts: 20.4 us -> 8.19 us
    gather x1 -> x0, local copies, waits for them, and re-layouts: 10.1 us -> none  [on_device(): picked_blocks = jnp.take(table_block, all_tokens, axis=0)]
  transfers between devices with their start and end apart: 6 -> 12, of which waited for: 3 -> 7; matrix products, arithmetic and copies ran while one was open for 3% -> 0% of each run, Pallas kernels for 0% -> 2%
where the time goes in v2:
time: 76.3 us; the launch traced here: 75.9 us
  blocking collectives  20 us (26%)
  starting transfers between devices  16.6 us (22%)
  waiting for transfers between devices  16.1 us (21%)
  Pallas kernels  13.7 us (18%)
  local copies, waits for them, and re-layouts  8.88 us (12%)
    all_to_all x1, blocking collectives, on_device(): lax.all_to_all(jnp.broadcast_to(tokens[None], (row_groups,) + tokens.shap...  20 us
    ppermute x9, starting transfers between devices, swapped(): return lax.ppermute(shard, 'tp', [(i, i ^ by) for i in range(peers)])  9.74 us
    all_to_all x1, waiting for transfers between devices, on_device(): blocks = lax.all_to_all(picked.reshape(row_groups, -1, LANES), 'rows', 0, 0)  8.89 us
    unnamed x26, local copies, waits for them, and re-layouts  8.19 us
    pallas_call x1, Pallas kernels, pick_rows(): kernel_call(pick_rows_kernel, array((rows, LANES), table.dtype), [SMEM, V...  5.29 us
    ppermute x9, waiting for transfers between devices, swapped(): return lax.ppermute(shard, 'tp', [(i, i ^ by) for i in range(peers)])  4.78 us
    all_to_all x1, starting transfers between devices, on_device(): blocks = lax.all_to_all(picked.reshape(row_groups, -1, LANES), 'rows', 0, 0)  3.85 us
    pallas_call x1, Pallas kernels, policy(): kernel_call(policy_kernel, (array((count, width), jnp.bfloat16), array((c...  3.24 us
  transfers between devices with their start and end apart: 12, of which 7 were waited for; matrix products, arithmetic and copies ran while one was open for 0% of the time, Pallas kernels for 2%

profile of v2, /device:TPU:1, one launch (start us, length us, event | category | flops | bytes accessed | tf_op | source)
XLA Modules:
  0.0 75.9 jit_solution(295641147021013347)
XLA Ops:
  0.6 0.7 broadcast_in_dim.2
  1.3 20.0 %all_to_all.10.token_ref = s32[32,4,4]{2,1,0:T(4,128)S(1)} all-to-all(s32[32,4,4]{2,1,0:T(4,128)S(1)} %broadcast_in_dim.2), channel_id=1, replica_groups=mesh['rows'=32,'tp'=4] {'rows'}, dimensions={0} | all-to-all | bytes 4096 | tf_op jit(solution)/shard_map/all_to_all | solution.py:421
  21.3 0.0 copy-start
  21.3 3.8 %copy-done = bf16[76032,1,64]{0,2,1:T(8,128)(2,1)S(1)} copy-done((bf16[76032,1,64]{0,2,1:T(8,128)(2,1)S(1)}, bf16[76032,1,64]{0,2,1:T(8,128)(2,1)}, u32[]{:S(2)}) %copy-start) | copy-done | bytes 9732120
  25.1 0.0 copy-start.10
  25.1 5.3 %pick_rows.1 = bf16[256,128]{1,0:T(8,128)(2,1)} custom-call(s32[32,4,4]{2,1,0:T(4,128)S(1)} %all_to_all.10.token_ref, bf16[64,76032]{1,0:T(8,128)(2,1)S(1)} %bitcast.10), custom_call_target="tpu_custom_call" | custom-call | tf_op jit(solution)/shard_map/pick_rows/pallas_call | solution.py:77
  30.4 3.9 %all-to-all-start.1 = ((bf16[32,8,128]{2,1,0:T(8,128)(2,1)}), bf16[32,8,128]{2,1,0:T(8,128)(2,1)S(1)}, u32[]{:S(2)}, u32[]{:S(2)}) async-start(bf16[32,8,128]{2,1,0:T(8,128)(2,1)} %bitcast.3), calls=%async_computation.1 | async-start | bytes 131072 | tf_op jit(solution)/shard_map/all_to_all | solution.py:425
  34.2 0.0 copy-done.10
  34.2 8.9 %all-to-all-done.1 = bf16[32,8,128]{2,1,0:T(8,128)(2,1)S(1)} async-done(((bf16[32,8,128]{2,1,0:T(8,128)(2,1)}), bf16[32,8,128]{2,1,0:T(8,128)(2,1)S(1)}, u32[]{:S(2)}, u32[]{:S(2)}) %all-to-all-start.1) | async-done | bytes 65568 | tf_op jit(solution)/shard_map/all_to_all | solution.py:425
  43.1 0.0 copy-start.1
  43.1 2.2 %copy-done.1 = bf16[2048,1024]{1,0:T(8,128)(2,1)S(1)} copy-done((bf16[2048,1024]{1,0:T(8,128)(2,1)S(1)}, bf16[2048,1024]{1,0:T(8,128)(2,1)}, u32[]{:S(2)}) %copy-start.1) | copy-done | bytes 4194328
  45.3 0.0 copy-start.2
  45.3 2.2 %copy-done.2 = bf16[2048,1024]{1,0:T(8,128)(2,1)S(1)} copy-done((bf16[2048,1024]{1,0:T(8,128)(2,1)S(1)}, bf16[2048,1024]{1,0:T(8,128)(2,1)}, u32[]{:S(2)}) %copy-start.2) | copy-done | bytes 4194328
  47.5 0.0 copy-start.3
  47.5 1.3 %project.1 = (bf16[16,2048]{1,0:T(8,128)(2,1)S(1)}, bf16[8,32,128]{2,1,0:T(8,128)(2,1)S(1)}, f32[16,640]{1,0:T(8,128)S(1)}, f32[16,640]{1,0:T(8,128)S(1)}, f32[16,640]{1,0:T(8,128)S(1)}, /*index=5*/f32[16,640]{1,0:T(8,128)S(1)}) custom-call(s32[1]{0:T(128)} %bitcast.tp_ref, bf16[256,128]{1,0:T(8,128)(2,1)S(1)} %bitcast.11, f32[1,2048]{1,0:T(1,128)S(1)} %bitcast.14, ...), custom_call_target="tpu_custom_call" | custom-call | flops 134217728 | bytes 8388608 | tf_op jit(solution)/shard_map/project/pallas_call | solution.py:125
  48.8 0.0 copy-start.4
  48.8 0.0 copy-start.8
  48.8 3.2 %collective-permute-start = (f32[16,640]{1,0:T(8,128)S(1)}, f32[16,640]{1,0:T(8,128)S(1)}, u32[]{:S(2)}, u32[]{:S(2)}) collective-permute-start(f32[16,640]{1,0:T(8,128)S(1)} %get-tuple-element.12), channel_id=1, source_target_pairs={{0,1},{1,0},{2,3},{3,2},{4,5},{5,4},{6,7},{7,6},{8,9},{9,8},{10,11... | collective-permute-start | bytes 122888 | tf_op jit(solution)/shard_map/ppermute | solution.py:386
  52.0 0.3 collective-permute-start.1
  52.3 1.4 %collective-permute-start.2 = (f32[16,640]{1,0:T(8,128)S(1)}, f32[16,640]{1,0:T(8,128)S(1)}, u32[]{:S(2)}, u32[]{:S(2)}) collective-permute-start(f32[16,640]{1,0:T(8,128)S(1)} %get-tuple-element.14), channel_id=1, source_target_pairs={{0,3},{1,2},{2,1},{3,0},{4,7},{5,6},{6,5},{7,4},{8,11},{9,10},{10,... | collective-permute-start | bytes 122888 | tf_op jit(solution)/shard_map/ppermute | solution.py:386
  53.7 0.0 copy-done.3
  53.7 0.8 %policy_scores.1.raw_ref = f32[8,32,1024]{2,1,0:T(8,128)S(1)} custom-call(bf16[8,32,128]{2,1,0:T(8,128)(2,1)S(1)} %get-tuple-element.15.query_ref, bf16[4,1024,256]{2,1,0:T(8,128)(2,1)S(1)} %copy-done.3), custom_call_target="tpu_custom_call" | custom-call | flops 67108864 | bytes 3145728 | tf_op jit(solution)/shard_map/policy_scores/pallas_call | solution.py:148
  54.5 0.0 copy-start.11
  54.5 0.0 copy-start.12
  54.6 0.0 copy-start.5
  54.6 0.0 collective-permute-done.one_ref
  54.6 0.3 collective-permute-done.1.two_ref
  54.9 1.4 %collective-permute-done.2.three_ref = f32[16,640]{1,0:T(8,128)S(1)} collective-permute-done((f32[16,640]{1,0:T(8,128)S(1)}, f32[16,640]{1,0:T(8,128)S(1)}, u32[]{:S(2)}, u32[]{:S(2)}) %collective-permute-start.2) | collective-permute-done | bytes 40992 | tf_op jit(solution)/shard_map/ppermute | solution.py:386
  56.3 0.0 copy-done.4
  56.3 0.0 copy-done.8
  56.3 3.2 %policy.1 = (bf16[16,2048]{1,0:T(8,128)(2,1)S(1)}, f32[16,128]{1,0:T(8,128)S(1)}, bf16[4,4,2048]{2,1,0:T(4,128)(2,1)}) custom-call(s32[4]{0:T(128)S(1)} %copy-done.8, f32[16,640]{1,0:T(8,128)S(1)} %get-tuple-element.11.own_ref, f32[16,640]{1,0:T(8,128)S(1)} %collective-permute-done.one_ref, f32[16,640]{1,0:T(8,128)S(1)} %collective-permute-done.1.two_ref, ...), custom_call_target="tpu_custom_call" | custom-call | flops 67108864 | bytes 3145728 | tf_op jit(solution)/shard_map/policy/pallas_call | solution.py:249
  59.5 0.0 copy-start.6
  59.5 0.0 copy-start.7
  59.5 0.0 copy-start.9
  59.5 1.0 %collective-permute-start.7 = (bf16[16,2048]{1,0:T(8,128)(2,1)S(1)}, bf16[16,2048]{1,0:T(8,128)(2,1)S(1)}, u32[]{:S(2)}, u32[]{:S(2)}) collective-permute-start(bf16[16,2048]{1,0:T(8,128)(2,1)S(1)} %get-tuple-element.19), channel_id=1, source_target_pairs={{0,64},{4,68},{8,72},{12,76},{16,80},{20,84},{24,88},{28,92},{32,9... | collective-permute-start | bytes 196616 | tf_op jit(solution)/shard_map/ppermute | solution.py:391
  60.5 2.0 %collective-permute-start.3 = (f32[16,128]{1,0:T(8,128)S(1)}, f32[16,128]{1,0:T(8,128)S(1)}, u32[]{:S(2)}, u32[]{:S(2)}) collective-permute-start(f32[16,128]{1,0:T(8,128)S(1)} %get-tuple-element.18), channel_id=1, source_target_pairs={{0,64},{4,68},{8,72},{12,76},{16,80},{20,84},{24,88},{28,92},{32,9... | collective-permute-start | bytes 24584 | tf_op jit(solution)/shard_map/ppermute | solution.py:391
  62.5 2.4 %collective-permute-done.3.own_ref = f32[16,128]{1,0:T(8,128)S(1)} collective-permute-done((f32[16,128]{1,0:T(8,128)S(1)}, f32[16,128]{1,0:T(8,128)S(1)}, u32[]{:S(2)}, u32[]{:S(2)}) %collective-permute-start.3) | collective-permute-done | bytes 8224 | tf_op jit(solution)/shard_map/ppermute | solution.py:391
  64.9 1.3 %collective-permute-start.4 = (f32[16,128]{1,0:T(8,128)S(1)}, f32[16,128]{1,0:T(8,128)S(1)}, u32[]{:S(2)}, u32[]{:S(2)}) collective-permute-start(f32[16,128]{1,0:T(8,128)S(1)} %collective-permute-done.3.own_ref), channel_id=1, source_target_pairs={{0,1},{1,0},{2,3},{3,2},{4,5},{5,4},{6,7},{7,6},{8,9},{9,8},{10,11... | collective-permute-start | bytes 24584 | tf_op jit(solution)/shard_map/ppermute | solution.py:386
  66.2 0.8 %collective-permute-start.5 = (f32[16,128]{1,0:T(8,128)S(1)}, f32[16,128]{1,0:T(8,128)S(1)}, u32[]{:S(2)}, u32[]{:S(2)}) collective-permute-start(f32[16,128]{1,0:T(8,128)S(1)} %collective-permute-done.3.own_ref), channel_id=1, source_target_pairs={{0,2},{1,3},{2,0},{3,1},{4,6},{5,7},{6,4},{7,5},{8,10},{9,11},{10,... | collective-permute-start | bytes 24584 | tf_op jit(solution)/shard_map/ppermute | solution.py:386
  67.0 0.8 %collective-permute-start.6 = (f32[16,128]{1,0:T(8,128)S(1)}, f32[16,128]{1,0:T(8,128)S(1)}, u32[]{:S(2)}, u32[]{:S(2)}) collective-permute-start(f32[16,128]{1,0:T(8,128)S(1)} %collective-permute-done.3.own_ref), channel_id=1, source_target_pairs={{0,3},{1,2},{2,1},{3,0},{4,7},{5,6},{6,5},{7,4},{8,11},{9,10},{10,... | collective-permute-start | bytes 24584 | tf_op jit(solution)/shard_map/ppermute | solution.py:386
  67.9 0.0 copy-done.11
  67.9 0.0 copy-done.12
  67.9 0.0 collective-permute-done.7.rows_ref
  67.9 0.0 copy-done.5
  67.9 0.8 %critic_scores.1.raw_ref = f32[8,32,1024]{2,1,0:T(8,128)S(1)} custom-call(bf16[16,2048]{1,0:T(8,128)(2,1)S(1)} %collective-permute-done.7.rows_ref, f32[1,2048]{1,0:T(1,128)S(1)} %bitcast.15, bf16[4,1024,256]{2,1,0:T(8,128)(2,1)S(1)} %copy-done.5), custom_call_target="tpu_custom_call" | custom-call | flops 67108864 | bytes 3145728 | tf_op jit(solution)/shard_map/critic_scores/pallas_call | solution.py:286
  68.7 0.0 collective-permute-done.4.one_ref
  68.7 0.0 collective-permute-done.5.two_ref
  68.7 1.4 %collective-permute-done.6.three_ref = f32[16,128]{1,0:T(8,128)S(1)} collective-permute-done((f32[16,128]{1,0:T(8,128)S(1)}, f32[16,128]{1,0:T(8,128)S(1)}, u32[]{:S(2)}, u32[]{:S(2)}) %collective-permute-start.6) | collective-permute-done | bytes 8224 | tf_op jit(solution)/shard_map/ppermute | solution.py:386
  70.1 0.0 copy-done.6
  70.1 0.0 copy-done.7
  70.1 0.0 copy-done.9
  70.1 1.4 %critic.1.own_ref = f32[16,128]{1,0:T(8,128)S(1)} custom-call(s32[4]{0:T(128)S(1)} %copy-done.9, f32[16,128]{1,0:T(8,128)S(1)} %collective-permute-done.3.own_ref, f32[16,128]{1,0:T(8,128)S(1)} %collective-permute-done.4.one_ref, f32[16,128]{1,0:T(8,128)S(1)} %collective-permute-done.5.two_ref, f32[16,128]{1,0:T(8,128)S(1)} %collective-permute-done.6.three_ref, ...), custom_call_target="tpu_custom_call" | custom-call | flops 67108864 | bytes 3145728 | tf_op jit(solution)/shard_map/critic/pallas_call | solution.py:345
  71.5 0.8 %collective-permute-start.10 = (f32[16,128]{1,0:T(8,128)S(1)}, f32[16,128]{1,0:T(8,128)S(1)}, u32[]{:S(2)}, u32[]{:S(2)}) collective-permute-start(f32[16,128]{1,0:T(8,128)S(1)} %critic.1.own_ref), channel_id=1, source_target_pairs={{0,3},{1,2},{2,1},{3,0},{4,7},{5,6},{6,5},{7,4},{8,11},{9,10},{10,... | collective-permute-start | bytes 24584 | tf_op jit(solution)/shard_map/ppermute | solution.py:386
  72.4 0.2 collective-permute-start.8
  72.6 0.8 %collective-permute-start.9 = (f32[16,128]{1,0:T(8,128)S(1)}, f32[16,128]{1,0:T(8,128)S(1)}, u32[]{:S(2)}, u32[]{:S(2)}) collective-permute-start(f32[16,128]{1,0:T(8,128)S(1)} %critic.1.own_ref), channel_id=1, source_target_pairs={{0,2},{1,3},{2,0},{3,1},{4,6},{5,7},{6,4},{7,5},{8,10},{9,11},{10,... | collective-permute-start | bytes 24584 | tf_op jit(solution)/shard_map/ppermute | solution.py:386
  73.4 1.2 %collective-permute-done.10.three_ref = f32[16,128]{1,0:T(8,128)S(1)} collective-permute-done((f32[16,128]{1,0:T(8,128)S(1)}, f32[16,128]{1,0:T(8,128)S(1)}, u32[]{:S(2)}, u32[]{:S(2)}) %collective-permute-start.10) | collective-permute-done | bytes 8224 | tf_op jit(solution)/shard_map/ppermute | solution.py:386
  74.6 0.0 collective-permute-done.8.one_ref
  74.6 0.5 collective-permute-done.9.two_ref
  75.1 0.8 %expect.1 = f32[4,4]{1,0:T(4,128)} custom-call(f32[16,128]{1,0:T(8,128)S(1)} %critic.1.own_ref, f32[16,128]{1,0:T(8,128)S(1)} %collective-permute-done.8.one_ref, f32[16,128]{1,0:T(8,128)S(1)} %collective-permute-done.9.two_ref, f32[16,128]{1,0:T(8,128)S(1)} %collective-permute-done.10.three_ref), custom_call_target="tpu_custom_call" | custom-call | tf_op jit(solution)/shard_map/expect/pallas_call | solution.py:381
  (3 shorter events, 0.0 us)
Async XLA Ops:
  21.3 3.8 %copy-start = (bf16[76032,1,64]{0,2,1:T(8,128)(2,1)S(1)}, bf16[76032,1,64]{0,2,1:T(8,128)(2,1)}, u32[]{:S(2)}) copy-start(bf16[76032,1,64]{0,2,1:T(8,128)(2,1)} %param.16) | copy-start | bytes 29196292
  25.1 9.2 %copy-start.10 = (bf16[2048]{0:T(1024)(128)(2,1)S(1)}, bf16[2048]{0:T(1024)(128)(2,1)}, u32[]{:S(2)}) copy-start(bf16[2048]{0:T(1024)(128)(2,1)} %param.17) | copy-start | bytes 12292
  30.4 12.8 %all-to-all-start.1 = ((bf16[32,8,128]{2,1,0:T(8,128)(2,1)}), bf16[32,8,128]{2,1,0:T(8,128)(2,1)S(1)}, u32[]{:S(2)}, u32[]{:S(2)}) async-start(bf16[32,8,128]{2,1,0:T(8,128)(2,1)} %bitcast.3), calls=%async_computation.1 | async-start | bytes 131072 | tf_op jit(solution)/shard_map/all_to_all | solution.py:425
  43.1 2.2 %copy-start.1 = (bf16[2048,1024]{1,0:T(8,128)(2,1)S(1)}, bf16[2048,1024]{1,0:T(8,128)(2,1)}, u32[]{:S(2)}) copy-start(bf16[2048,1024]{1,0:T(8,128)(2,1)} %key_ref.1) | copy-start | bytes 12582916
  45.3 2.2 %copy-start.2 = (bf16[2048,1024]{1,0:T(8,128)(2,1)S(1)}, bf16[2048,1024]{1,0:T(8,128)(2,1)}, u32[]{:S(2)}) copy-start(bf16[2048,1024]{1,0:T(8,128)(2,1)} %value_ref.1) | copy-start | bytes 12582916
  47.5 6.2 %copy-start.3 = (bf16[4,1024,256]{2,1,0:T(8,128)(2,1)S(1)}, bf16[4,1024,256]{2,1,0:T(8,128)(2,1)}, u32[]{:S(2)}) copy-start(bf16[4,1024,256]{2,1,0:T(8,128)(2,1)} %keys_ref.2) | copy-start | bytes 6291460
  48.8 7.5 %copy-start.4 = (bf16[4,1024,256]{2,1,0:T(8,128)(2,1)S(1)}, bf16[4,1024,256]{2,1,0:T(8,128)(2,1)}, u32[]{:S(2)}) copy-start(bf16[4,1024,256]{2,1,0:T(8,128)(2,1)} %values_ref.2) | copy-start | bytes 6291460
  48.8 7.5 %copy-start.8 = (s32[4]{0:T(128)S(1)}, s32[4]{0:T(128)}, u32[]{:S(2)}) copy-start(s32[4]{0:T(128)} %length_ref.2) | copy-start | bytes 52
  48.8 5.7 %collective-permute-start = (f32[16,640]{1,0:T(8,128)S(1)}, f32[16,640]{1,0:T(8,128)S(1)}, u32[]{:S(2)}, u32[]{:S(2)}) collective-permute-start(f32[16,640]{1,0:T(8,128)S(1)} %get-tuple-element.12), channel_id=1, source_target_pairs={{0,1},{1,0},{2,3},{3,2},{4,5},{5,4},{6,7},{7,6},{8,9},{9,8},{10,11... | collective-permute-start | bytes 122888 | tf_op jit(solution)/shard_map/ppermute | solution.py:386
  52.0 2.9 %collective-permute-start.1 = (f32[16,640]{1,0:T(8,128)S(1)}, f32[16,640]{1,0:T(8,128)S(1)}, u32[]{:S(2)}, u32[]{:S(2)}) collective-permute-start(f32[16,640]{1,0:T(8,128)S(1)} %get-tuple-element.13), channel_id=1, source_target_pairs={{0,2},{1,3},{2,0},{3,1},{4,6},{5,7},{6,4},{7,5},{8,10},{9,11},{10,... | collective-permute-start | bytes 122888 | tf_op jit(solution)/shard_map/ppermute | solution.py:386
  52.3 4.0 %collective-permute-start.2 = (f32[16,640]{1,0:T(8,128)S(1)}, f32[16,640]{1,0:T(8,128)S(1)}, u32[]{:S(2)}, u32[]{:S(2)}) collective-permute-start(f32[16,640]{1,0:T(8,128)S(1)} %get-tuple-element.14), channel_id=1, source_target_pairs={{0,3},{1,2},{2,1},{3,0},{4,7},{5,6},{6,5},{7,4},{8,11},{9,10},{10,... | collective-permute-start | bytes 122888 | tf_op jit(solution)/shard_map/ppermute | solution.py:386
  54.5 13.3 %copy-start.11 = (bf16[2048]{0:T(1024)(128)(2,1)S(1)}, bf16[2048]{0:T(1024)(128)(2,1)}, u32[]{:S(2)}) copy-start(bf16[2048]{0:T(1024)(128)(2,1)} %param.23) | copy-start | bytes 12292
  54.5 13.3 %copy-start.12 = (bf16[2048]{0:T(1024)(128)(2,1)S(1)}, bf16[2048]{0:T(1024)(128)(2,1)}, u32[]{:S(2)}) copy-start(bf16[2048]{0:T(1024)(128)(2,1)} %param.26) | copy-start | bytes 12292
  54.6 13.3 %copy-start.5 = (bf16[4,1024,256]{2,1,0:T(8,128)(2,1)S(1)}, bf16[4,1024,256]{2,1,0:T(8,128)(2,1)}, u32[]{:S(2)}) copy-start(bf16[4,1024,256]{2,1,0:T(8,128)(2,1)} %keys_ref.3) | copy-start | bytes 6291460
  59.5 10.6 %copy-start.6 = (bf16[4,1024,256]{2,1,0:T(8,128)(2,1)S(1)}, bf16[4,1024,256]{2,1,0:T(8,128)(2,1)}, u32[]{:S(2)}) copy-start(bf16[4,1024,256]{2,1,0:T(8,128)(2,1)} %values_ref.3) | copy-start | bytes 6291460
  59.5 10.6 %copy-start.7 = (bf16[2048,51]{0,1:T(8,128)(2,1)S(1)}, bf16[2048,51]{0,1:T(8,128)(2,1)}, u32[]{:S(2)}) copy-start(bf16[2048,51]{0,1:T(8,128)(2,1)} %param.27) | copy-start | bytes 626692
  59.5 10.6 %copy-start.9 = (s32[4]{0:T(128)S(1)}, s32[4]{0:T(128)}, u32[]{:S(2)}) copy-start(s32[4]{0:T(128)} %length_ref.3) | copy-start | bytes 52
  59.5 8.3 %collective-permute-start.7 = (bf16[16,2048]{1,0:T(8,128)(2,1)S(1)}, bf16[16,2048]{1,0:T(8,128)(2,1)S(1)}, u32[]{:S(2)}, u32[]{:S(2)}) collective-permute-start(bf16[16,2048]{1,0:T(8,128)(2,1)S(1)} %get-tuple-element.19), channel_id=1, source_target_pairs={{0,64},{4,68},{8,72},{12,76},{16,80},{20,84},{24,88},{28,92},{32,9... | collective-permute-start | bytes 196616 | tf_op jit(solution)/shard_map/ppermute | solution.py:391
  60.5 4.4 %collective-permute-start.3 = (f32[16,128]{1,0:T(8,128)S(1)}, f32[16,128]{1,0:T(8,128)S(1)}, u32[]{:S(2)}, u32[]{:S(2)}) collective-permute-start(f32[16,128]{1,0:T(8,128)S(1)} %get-tuple-element.18), channel_id=1, source_target_pairs={{0,64},{4,68},{8,72},{12,76},{16,80},{20,84},{24,88},{28,92},{32,9... | collective-permute-start | bytes 24584 | tf_op jit(solution)/shard_map/ppermute | solution.py:391
  64.9 3.8 %collective-permute-start.4 = (f32[16,128]{1,0:T(8,128)S(1)}, f32[16,128]{1,0:T(8,128)S(1)}, u32[]{:S(2)}, u32[]{:S(2)}) collective-permute-start(f32[16,128]{1,0:T(8,128)S(1)} %collective-permute-done.3.own_ref), channel_id=1, source_target_pairs={{0,1},{1,0},{2,3},{3,2},{4,5},{5,4},{6,7},{7,6},{8,9},{9,8},{10,11... | collective-permute-start | bytes 24584 | tf_op jit(solution)/shard_map/ppermute | solution.py:386
  66.2 2.5 %collective-permute-start.5 = (f32[16,128]{1,0:T(8,128)S(1)}, f32[16,128]{1,0:T(8,128)S(1)}, u32[]{:S(2)}, u32[]{:S(2)}) collective-permute-start(f32[16,128]{1,0:T(8,128)S(1)} %collective-permute-done.3.own_ref), channel_id=1, source_target_pairs={{0,2},{1,3},{2,0},{3,1},{4,6},{5,7},{6,4},{7,5},{8,10},{9,11},{10,... | collective-permute-start | bytes 24584 | tf_op jit(solution)/shard_map/ppermute | solution.py:386
  67.0 3.1 %collective-permute-start.6 = (f32[16,128]{1,0:T(8,128)S(1)}, f32[16,128]{1,0:T(8,128)S(1)}, u32[]{:S(2)}, u32[]{:S(2)}) collective-permute-start(f32[16,128]{1,0:T(8,128)S(1)} %collective-permute-done.3.own_ref), channel_id=1, source_target_pairs={{0,3},{1,2},{2,1},{3,0},{4,7},{5,6},{6,5},{7,4},{8,11},{9,10},{10,... | collective-permute-start | bytes 24584 | tf_op jit(solution)/shard_map/ppermute | solution.py:386
  71.5 3.1 %collective-permute-start.10 = (f32[16,128]{1,0:T(8,128)S(1)}, f32[16,128]{1,0:T(8,128)S(1)}, u32[]{:S(2)}, u32[]{:S(2)}) collective-permute-start(f32[16,128]{1,0:T(8,128)S(1)} %critic.1.own_ref), channel_id=1, source_target_pairs={{0,3},{1,2},{2,1},{3,0},{4,7},{5,6},{6,5},{7,4},{8,11},{9,10},{10,... | collective-permute-start | bytes 24584 | tf_op jit(solution)/shard_map/ppermute | solution.py:386
  72.4 2.3 %collective-permute-start.8 = (f32[16,128]{1,0:T(8,128)S(1)}, f32[16,128]{1,0:T(8,128)S(1)}, u32[]{:S(2)}, u32[]{:S(2)}) collective-permute-start(f32[16,128]{1,0:T(8,128)S(1)} %critic.1.own_ref), channel_id=1, source_target_pairs={{0,1},{1,0},{2,3},{3,2},{4,5},{5,4},{6,7},{7,6},{8,9},{9,8},{10,11... | collective-permute-start | bytes 24584 | tf_op jit(solution)/shard_map/ppermute | solution.py:386
  72.6 2.5 %collective-permute-start.9 = (f32[16,128]{1,0:T(8,128)S(1)}, f32[16,128]{1,0:T(8,128)S(1)}, u32[]{:S(2)}, u32[]{:S(2)}) collective-permute-start(f32[16,128]{1,0:T(8,128)S(1)} %critic.1.own_ref), channel_id=1, source_target_pairs={{0,2},{1,3},{2,0},{3,1},{4,6},{5,7},{6,4},{7,5},{8,10},{9,11},{10,... | collective-permute-start | bytes 24584 | tf_op jit(solution)/shard_map/ppermute | solution.py:386

commit v3 on v2

v3 whole, which is shorter than its diff:
```python
import functools
import math

import jax
import jax.numpy as jnp
from jax import lax
from jax.experimental import pallas as pl
from jax.experimental.pallas import tpu as pltpu
from jax.sharding import PartitionSpec as P

D = 8192
HEAD_DIM = 128
GROUP = 8
ATOMS = 51
LANES = 128
HALF = 64
MIB = 1024 * 1024

norm_eps = 1e-06
atom_span = 10.0
masked = -1e30
attn_scale = 1.0 / math.sqrt(HEAD_DIM)
log2_e = 1.0 / math.log(2.0)

SMEM = pl.BlockSpec(memory_space=pltpu.SMEM)
VMEM = pl.BlockSpec(memory_space=pltpu.VMEM)
HBM = pl.BlockSpec(memory_space=pltpu.HBM)
NT = (((1,), (1,)), ((), ()))


def kernel_call(body, outs, specs, scratch=(), limit=16, flops=0, moved=0, name=None):
    return pl.pallas_call(
        body,
        out_shape=outs,
        in_specs=specs,
        out_specs=jax.tree.map(lambda _: VMEM, outs),
        scratch_shapes=scratch,
        compiler_params=pltpu.CompilerParams(vmem_limit_bytes=limit * MIB),
        cost_estimate=pl.CostEstimate(flops=flops, bytes_accessed=moved, transcendentals=0),
        name=name,
    )


def array(shape, dtype):
    return jax.ShapeDtypeStruct(shape, dtype)


def in_hbm(x):
    return pltpu.with_memory_space_constraint(x, pltpu.HBM)


def pick_rows_kernel(token_ref, table_ref, out_ref, tiles_ref, sems):
    width = table_ref.shape[0]
    pieces = sems.shape[0]
    places = tiles_ref.shape[1] // pieces
    lane = lax.broadcasted_iota(jnp.int32, (width, LANES), 1)

    def token_of(place, half):
        destination = lax.shift_right_logical(place, 3)
        decode_step = jnp.bitwise_and(place, 3)
        row = jnp.bitwise_and(lax.shift_right_logical(place, 2), 1)
        return token_ref[destination, decode_step, row + 2 * half]

    for piece in range(pieces):

        def fetch(i, carry):
            place = piece * places + i
            for half in range(2):
                block = jnp.bitwise_and(token_of(place, half), ~(LANES - 1))
                pltpu.make_async_copy(
                    table_ref.at[:, pl.ds(pl.multiple_of(block, LANES), LANES)],
                    tiles_ref.at[half, place],
                    sems.at[piece],
                ).start()
            return carry

        lax.fori_loop(0, places, fetch, 0, unroll=8)

    empty = jnp.zeros((width, LANES), jnp.float32)
    pair = (empty, empty)
    for piece in range(pieces):
        part = tiles_ref.at[:, pl.ds(piece * places, places)]
        pltpu.make_async_copy(part, part, sems.at[piece]).wait()
        first_place = piece * places % LANES

        def step(i, carry):
            place = piece * places + i
            here = lane == first_place + i
            kept = []
            for half in range(2):
                shift = jnp.bitwise_and(place - token_of(place, half), LANES - 1)
                tile = pltpu.roll(tiles_ref[half, place].astype(jnp.float32), shift, 1)
                kept.append(jnp.where(here, tile, carry[half]))
            return tuple(kept)

        pair = lax.fori_loop(0, places, step, pair, unroll=min(places, 32))
        if first_place + places == LANES:
            both = jnp.concatenate(pair, axis=0)
            rows = pl.ds((piece + 1) * places - LANES, LANES)
            out_ref[rows, :] = both.T.astype(out_ref.dtype)
            pair = (empty, empty)


def pick_rows(tokens, table, pieces=8):
    width = table.shape[0]
    rows = tokens.size * width // LANES
    return kernel_call(
        pick_rows_kernel,
        array((rows, LANES), table.dtype),
        [SMEM, HBM],
        scratch=[
            pltpu.VMEM((2, rows, width, LANES), table.dtype),
            pltpu.SemaphoreType.DMA((pieces,)),
        ],
        limit=24,
        name="pick_rows",
    )(tokens, in_hbm(table))


def stage_kernel(source_ref, target_ref, sems):
    pieces = sems.shape[0]
    rows = target_ref.shape[0] // pieces
    copies = []
    for piece in range(pieces):
        part = pl.ds(piece * rows, rows)
        copies.append(
            pltpu.make_async_copy(source_ref.at[part], target_ref.at[part], sems.at[piece])
        )
    for copy in copies:
        copy.start()
    for copy in copies:
        copy.wait()


def staged(source, rows, pieces=4):
    shape = (rows, source.shape[1])
    return pl.pallas_call(
        stage_kernel,
        out_shape=pltpu.VMEM(shape, source.dtype),
        in_specs=[HBM],
        out_specs=VMEM,
        scratch_shapes=[pltpu.SemaphoreType.DMA((pieces,))],
        compiler_params=pltpu.CompilerParams(vmem_limit_bytes=MIB),
        cost_estimate=pl.CostEstimate(
            flops=0, bytes_accessed=4 * rows * shape[1], transcendentals=0
        ),
        name="stage_weights",
    )(in_hbm(source))


def project_kernel(
    tp_ref, blocks_ref, gain_ref, early_ref, key_ref, value_ref, x_ref, query_ref, *rest
):
    parts = rest[:4]
    gained_ref, placed_ref, sums_ref, late_ref, keys_ref, sems = rest[4:]
    count, width = x_ref.shape
    kv_width = key_ref.shape[1] // 4
    early = early_ref.shape[0]
    chunk = width - early
    copies = [pltpu.make_async_copy(value_ref.at[pl.ds(early, chunk)], late_ref, sems.at[0])]
    for at in range(width // chunk):
        rows = pl.ds(at * chunk, chunk)
        copies.append(
            pltpu.make_async_copy(key_ref.at[rows], keys_ref.at[rows], sems.at[at + 1])
        )
    for copy in copies:
        copy.start()
    left = lax.broadcasted_iota(jnp.int32, (8, LANES), 1) < HALF
    squares = jnp.zeros((count, LANES), jnp.float32)
    for k in range(width // LANES):
        pair = blocks_ref[pl.ds(16 * k, 16), :].astype(jnp.float32)
        one, two = pair[:8], pair[8:]
        low = jnp.where(left, one, pltpu.roll(two, HALF, 1))
        high = jnp.where(left, pltpu.roll(one, HALF, 1), two)
        x = jnp.concatenate([low, high], axis=0)
        squares += x * x
        columns = pl.ds(k * LANES, LANES)
        x_ref[:, columns] = x.astype(x_ref.dtype)
        gained = x * gain_ref[:, columns]
        gained_ref[:, columns] = gained.astype(gained_ref.dtype)
        head, group = divmod(k, GROUP)
        for row in range(4):
            placed_ref[4 * head + row, pl.ds(4 * group, 4), :] = gained[4 * row : 4 * row + 4]
    query_ref[...] = placed_ref[...].astype(query_ref.dtype)
    total = jnp.broadcast_to(jnp.sum(squares, axis=1, keepdims=True), (count, LANES))

    def product(rows, weight):
        return jnp.dot(gained_ref[:, rows], weight, preferred_element_type=jnp.float32)

    values = product(pl.ds(0, early), early_ref[...])
    copies[0].wait()
    sums_ref[1] = values + product(pl.ds(early, chunk), late_ref[...])
    keys = None
    for at in range(width // chunk):
        rows = pl.ds(at * chunk, chunk)
        copies[at + 1].wait()
        partial = product(rows, keys_ref[rows, :])
        keys = partial if keys is None else keys + partial
    sums_ref[0] = keys
    for by, part_ref in enumerate(parts):
        start = pl.multiple_of(jnp.bitwise_xor(tp_ref[0], by) * kv_width, kv_width)
        peer = pl.ds(start, kv_width)
        part_ref[:, :kv_width] = sums_ref[0, :, peer]
        part_ref[:, kv_width : 2 * kv_width] = sums_ref[1, :, peer]
        part_ref[:, 2 * kv_width :] = total


def project(tp, blocks, gain, key_weight, value_weight):
    width, kv_all = key_weight.shape
    count = blocks.shape[0] * LANES // width
    early = width * 3 // 4
    part = array((count, kv_all // 2 + LANES), jnp.float32)
    heads = width // (GROUP * HEAD_DIM)
    queries = (4 * heads, 4 * GROUP, HEAD_DIM)
    x, query, *parts = kernel_call(
        project_kernel,
        (array((count, width), jnp.bfloat16), array(queries, jnp.bfloat16)) + (part,) * 4,
        [SMEM] + [VMEM] * 3 + [HBM] * 2,
        scratch=[
            pltpu.VMEM((count, width), jnp.bfloat16),
            pltpu.VMEM(queries, jnp.float32),
            pltpu.VMEM((2, count, kv_all), jnp.float32),
            pltpu.VMEM((width - early, kv_all), key_weight.dtype),
            pltpu.VMEM((width, kv_all), key_weight.dtype),
            pltpu.SemaphoreType.DMA((1 + width // (width - early),)),
        ],
        flops=4 * count * width * kv_all,
        moved=4 * width * kv_all,
        name="project",
    )(
        tp,
        blocks,
        gain,
        staged(value_weight, early),
        in_hbm(key_weight),
        in_hbm(value_weight),
    )
    return x, query, parts


def masked_scores(query, keys, length, raw_ref, top_ref, at):
    raw = lax.dot_general(query, keys, NT, preferred_element_type=jnp.float32)
    visible = lax.broadcasted_iota(jnp.int32, raw.shape, 1) < length
    raw = jnp.where(visible, raw, masked)
    raw_ref[at] = raw
    top_ref[at] = jnp.broadcast_to(jnp.max(raw, axis=1, keepdims=True), top_ref.shape[1:])


def scores_kernel(length_ref, query_ref, keys_ref, raw_ref, top_ref):
    for at in range(query_ref.shape[0]):
        head, row = divmod(at, 4)
        keys = keys_ref[row, :, pl.ds(head * HEAD_DIM, HEAD_DIM)]
        masked_scores(query_ref[at], keys, length_ref[row], raw_ref, top_ref, at)


def policy_scores(lengths, query, keys):
    raw = array(query.shape[:2] + (keys.shape[1],), jnp.float32)
    return kernel_call(
        scores_kernel,
        (raw, array(query.shape, jnp.float32)),
        [SMEM, VMEM, VMEM],
        flops=2 * raw.size * HEAD_DIM,
        moved=2 * keys.size + 4 * raw.size,
        name="policy_scores",
    )(lengths, query, keys)


def spread_rows(inv, spread_ref):
    for row in range(4):
        for group in range(GROUP):
            spread_ref[row, pl.ds(4 * group, 4), :] = inv[4 * row : 4 * row + 4]


def widened(x, width):
    return jnp.concatenate([x] * (width // LANES), axis=1)


def policy_kernel(
    own_ref,
    one_ref,
    two_ref,
    three_ref,
    raw_ref,
    top_ref,
    query_ref,
    x_ref,
    values_ref,
    passed_ref,
    spread_ref,
    rows_ref,
):
    count, width = x_ref.shape
    kv_width = values_ref.shape[2]
    cache_size = values_ref.shape[1]
    total = own_ref[...] + (one_ref[...] + (two_ref[...] + three_ref[...]))
    inv = lax.rsqrt(total[:, 2 * kv_width :] * (1.0 / D) + norm_eps)
    wide = widened(inv, kv_width)
    new_key = (wide * total[:, :kv_width]).astype(jnp.bfloat16)
    new_value = (wide * total[:, kv_width : 2 * kv_width]).astype(jnp.bfloat16)
    spread_rows(inv * (attn_scale * log2_e), spread_ref)
    queries = query_ref.shape[1]
    at_query = lax.broadcasted_iota(jnp.int32, (4 * queries, count), 0)
    at_fresh = lax.broadcasted_iota(jnp.int32, (4 * queries, count), 1)
    mine = jnp.logical_and(
        lax.div(at_query, queries) == lax.shift_right_logical(at_fresh, 2),
        jnp.bitwise_and(at_fresh, 3) <= jnp.bitwise_and(at_query, 3),
    )
    for head in range(query_ref.shape[0] // 4):
        columns = slice(head * HEAD_DIM, (head + 1) * HEAD_DIM)
        all_queries = query_ref[pl.ds(4 * head, 4)].reshape(4 * queries, HEAD_DIM)
        fresh = lax.dot_general(
            all_queries, new_key[:, columns], NT, preferred_element_type=jnp.float32
        )
        fresh = jnp.where(mine, fresh, masked)
        fresh_top = jnp.max(fresh, axis=1, keepdims=True)
        fresh_weights, attended, inverses = [], [], []
        for row in range(4):
            at = 4 * head + row
            part = slice(row * queries, (row + 1) * queries)
            spread = spread_ref[row]
            highest = jnp.maximum(top_ref[at], fresh_top[part]) * spread
            weights = jnp.exp2(
                raw_ref[at] * widened(spread, cache_size) - widened(highest, cache_size)
            )
            extra = jnp.exp2(fresh[part] * spread[:, :count] - highest[:, :count])
            inverses.append(
                1.0
                / (jnp.sum(weights, axis=1, keepdims=True) + jnp.sum(extra, axis=1, keepdims=True))
            )
            fresh_weights.append(extra)
            attended.append(
                jnp.dot(
                    weights.astype(jnp.bfloat16),
                    values_ref[row, :, columns],
                    preferred_element_type=jnp.float32,
                )
            )
        fresh_weights = jnp.concatenate(fresh_weights, axis=0).astype(jnp.bfloat16)
        fresh_sum = jnp.dot(
            fresh_weights, new_value[:, columns], preferred_element_type=jnp.float32
        )
        for row in range(4):
            part = slice(row * queries, (row + 1) * queries)
            both = (attended[row] + fresh_sum[part]) * inverses[row]
            for group in range(GROUP):
                rows_ref[head * GROUP + group, pl.ds(4 * row, 4), :] = both[
                    4 * group : 4 * group + 4
                ]
    for k in range(width // LANES):
        columns = pl.ds(k * LANES, LANES)
        hidden = x_ref[:, columns].astype(jnp.float32) + rows_ref[k]
        passed_ref[:, columns] = hidden.astype(passed_ref.dtype)


def policy(parts, raw, top, query, x, values):
    count, width = x.shape
    return kernel_call(
        policy_kernel,
        array((count, width), jnp.bfloat16),
        [VMEM] * 9,
        scratch=[
            pltpu.VMEM((4, 4 * GROUP, LANES), jnp.float32),
            pltpu.VMEM((width // LANES, count, LANES), jnp.float32),
        ],
        flops=2 * raw.size * HEAD_DIM,
        moved=2 * values.size + 4 * raw.size,
        name="policy",
    )(*parts, raw, top, query, x, values)


def by_step_kernel(rows_ref, out_ref, wide_ref):
    for k in range(rows_ref.shape[1] // LANES):
        columns = pl.ds(k * LANES, LANES)
        wide_ref[k] = rows_ref[:, columns].astype(jnp.float32)
        for step in range(4):
            out_ref[step, :, columns] = wide_ref[k, pl.ds(step, 4, stride=4), :].astype(
                out_ref.dtype
            )


def by_step(rows):
    count, width = rows.shape
    return kernel_call(
        by_step_kernel,
        array((4, count // 4, width), rows.dtype),
        [VMEM],
        scratch=[pltpu.VMEM((width // LANES, count, LANES), jnp.float32)],
        moved=16 * rows.size,
        name="by_step",
    )(rows)


def squares_kernel(rows_ref, out_ref):
    squares = jnp.zeros(out_ref.shape, jnp.float32)
    for k in range(rows_ref.shape[1] // LANES):
        part = rows_ref[:, pl.ds(k * LANES, LANES)].astype(jnp.float32)
        squares += part * part
    out_ref[...] = jnp.broadcast_to(jnp.sum(squares, axis=1, keepdims=True), out_ref.shape)


def row_squares(rows):
    return kernel_call(
        squares_kernel, array((rows.shape[0], LANES), jnp.float32), [VMEM], name="row_squares"
    )(rows)


def critic_scores_kernel(
    length_ref, rows_ref, gain_ref, keys_ref, raw_ref, top_ref, placed_ref
):
    for k in range(rows_ref.shape[1] // LANES):
        columns = pl.ds(k * LANES, LANES)
        gained = rows_ref[:, columns].astype(jnp.float32) * gain_ref[:, columns]
        head, group = divmod(k, GROUP)
        for row in range(4):
            placed_ref[4 * head + row, pl.ds(4 * group, 4), :] = gained[4 * row : 4 * row + 4]
    for at in range(placed_ref.shape[0]):
        head, row = divmod(at, 4)
        keys = keys_ref[row, :, pl.ds(head * HEAD_DIM, HEAD_DIM)]
        query = placed_ref[at].astype(jnp.bfloat16)
        masked_scores(query, keys, length_ref[row], raw_ref, top_ref, at)


def critic_scores(lengths, rows, gain, keys):
    heads = keys.shape[2] // HEAD_DIM
    placed = (4 * heads, 4 * GROUP, HEAD_DIM)
    raw = array(placed[:2] + (keys.shape[1],), jnp.float32)
    return kernel_call(
        critic_scores_kernel,
        (raw, array(placed, jnp.float32)),
        [SMEM] + [VMEM] * 3,
        scratch=[pltpu.VMEM(placed, jnp.float32)],
        flops=2 * raw.size * HEAD_DIM,
        moved=2 * keys.size + 4 * raw.size,
        name="critic_scores",
    )(lengths, rows, gain, keys)


def critic_kernel(
    own_ref,
    one_ref,
    two_ref,
    three_ref,
    raw_ref,
    top_ref,
    rows_ref,
    gain_ref,
    values_ref,
    head_ref,
    out_ref,
    spread_ref,
    attended_ref,
    scaled_ref,
):
    count, width = rows_ref.shape
    cache_size = values_ref.shape[1]
    total = own_ref[...] + (one_ref[...] + (two_ref[...] + three_ref[...]))
    inv = lax.rsqrt(total * (1.0 / D) + norm_eps)
    spread_rows(inv * (attn_scale * log2_e), spread_ref)
    for at in range(raw_ref.shape[0]):
        head, row = divmod(at, 4)
        spread = spread_ref[row]
        weights = jnp.exp2(
            raw_ref[at] * widened(spread, cache_size) - widened(top_ref[at] * spread, cache_size)
        )
        inverse = 1.0 / jnp.sum(weights, axis=1, keepdims=True)
        attended = inverse * jnp.dot(
            weights.astype(jnp.bfloat16),
            values_ref[row, :, pl.ds(head * HEAD_DIM, HEAD_DIM)],
            preferred_element_type=jnp.float32,
        )
        for group in range(GROUP):
            attended_ref[head * GROUP + group, pl.ds(4 * row, 4), :] = attended[
                4 * group : 4 * group + 4
            ]
    squares = jnp.zeros((count, LANES), jnp.float32)
    for k in range(width // LANES):
        columns = pl.ds(k * LANES, LANES)
        combined = rows_ref[:, columns].astype(jnp.float32) + attended_ref[k]
        squares += combined * combined
        scaled_ref[:, columns] = (combined * gain_ref[:, columns]).astype(scaled_ref.dtype)
    logits = lax.dot_general(
        scaled_ref[...], head_ref[...], NT, preferred_element_type=jnp.float32
    )
    out_ref[...] = jnp.broadcast_to(jnp.sum(squares, axis=1, keepdims=True), (count, LANES))
    out_ref[:, :ATOMS] = logits


def critic(parts, raw, top, rows, gain, values, head):
    count, width = rows.shape
    return kernel_call(
        critic_kernel,
        array((count, LANES), jnp.float32),
        [VMEM] * 10,
        scratch=[
            pltpu.VMEM((4, 4 * GROUP, LANES), jnp.float32),
            pltpu.VMEM((width // LANES, count, LANES), jnp.float32),
            pltpu.VMEM((count, width), jnp.bfloat16),
        ],
        flops=2 * raw.size * HEAD_DIM,
        moved=2 * values.size + 4 * raw.size,
        name="critic",
    )(*parts, raw, top, rows, gain, values, head)


def expect_kernel(own_ref, one_ref, two_ref, three_ref, out_ref):
    total = own_ref[...] + (one_ref[...] + (two_ref[...] + three_ref[...]))
    lane = lax.broadcasted_iota(jnp.int32, total.shape, 1)
    at = lax.broadcasted_iota(jnp.int32, total.shape, 0)
    logits = lax.rsqrt(total[:, LANES - 1 :] * (1.0 / D) + norm_eps) * total
    real = lane < ATOMS
    logits = jnp.where(real, logits, masked)
    weights = jnp.exp(logits - jnp.max(logits, axis=1, keepdims=True))
    atoms = -atom_span + 2.0 * atom_span * lane.astype(jnp.float32) / (ATOMS - 1)
    value = jnp.sum(weights * atoms, axis=1, keepdims=True) / jnp.sum(
        weights, axis=1, keepdims=True
    )
    placed = jnp.where(lane == lax.shift_right_logical(at, 2), value, 0.0)
    rows = [
        jnp.sum(jnp.where(jnp.bitwise_and(at, 3) == step, placed, 0.0), axis=0, keepdims=True)
        for step in range(4)
    ]
    out_ref[...] = jnp.concatenate(rows, axis=0)[:, :4]


def expect(parts):
    return kernel_call(expect_kernel, array((4, 4), jnp.float32), [VMEM] * 4, name="expect")(*parts)


def swapped(shard, by):
    peers = lax.axis_size("tp")
    return lax.ppermute(shard, "tp", [(i, i ^ by) for i in range(peers)])


def passed_along(shard, axis, by):
    peers = lax.axis_size(axis)
    return lax.ppermute(shard, axis, [(i, (i + by) % peers) for i in range(peers)])


def with_peers(shard):
    return [shard] + [swapped(shard, by) for by in (1, 2, 3)]


def on_device(
    tokens,
    lengths,
    embedding,
    attn_gain,
    key_weight,
    value_weight,
    policy_keys,
    policy_values,
    critic_lengths,
    critic_gain,
    critic_keys,
    critic_values,
    value_gain,
    value_head,
):
    row_groups = lax.axis_size("rows")
    tp = lax.axis_index("tp").astype(jnp.int32).reshape(1)

    def as_row(gain):
        return gain.astype(jnp.float32).reshape(1, -1)

    table = embedding.transpose(1, 2, 0).reshape(embedding.shape[2], embedding.shape[0])
    all_tokens = lax.all_to_all(
        jnp.broadcast_to(tokens[None], (row_groups,) + tokens.shape), "rows", 0, 0
    )
    picked = pick_rows(all_tokens, table)
    blocks = lax.all_to_all(picked.reshape(row_groups, -1, LANES), "rows", 0, 0)
    x, query, parts = project(
        tp, blocks.reshape(picked.shape), as_row(attn_gain), key_weight, value_weight
    )
    arrived = parts[:1] + [swapped(parts[by], by) for by in (1, 2, 3)]
    raw, top = policy_scores(lengths, query, policy_keys)
    passed = policy(arrived, raw, top, query, x, policy_values)
    rows = passed_along(passed, "rows", row_groups // 2)
    hidden = by_step(passed)

    raw, top = critic_scores(critic_lengths, rows, as_row(critic_gain), critic_keys)
    logits = critic(
        with_peers(row_squares(rows)),
        raw,
        top,
        rows,
        as_row(value_gain),
        critic_values,
        value_head.T,
    )
    values = expect(with_peers(logits))
    return hidden, values


def solution(mesh):
    placed = (
        P(None, "rows"),
        P("rows"),
        P(None, "rows", "tp"),
        P("tp"),
        P("tp", None),
        P("tp", None),
        P("rows", None, "tp"),
        P("rows", None, "tp"),
        P("rows"),
        P("tp"),
        P("rows", None, "tp"),
        P("rows", None, "tp"),
        P("tp"),
        P("tp", None),
    )
    return jax.shard_map(
        on_device,
        mesh=mesh,
        in_specs=placed,
        out_specs=(P(None, "rows", "tp"), P(None, "rows")),
        check_vma=False,
    )
```

time: 76.3 us -> 69.8 us (0.915)
  local copies, waits for them, and re-layouts: 8.88 us -> 0.74 us
  Pallas kernels: 13.7 us -> 19.1 us
  waiting for transfers between devices: 16.1 us -> 13.7 us
  starting transfers between devices: 16.6 us -> 15.2 us
    unnamed x26 -> x20, local copies, waits for them, and re-layouts: 8.19 us -> 0.05 us
    pallas_call x5 -> x8, Pallas kernels: 11.5 us -> 15.3 us  [the longest x1 8.13 us: pick_rows(): kernel_call(pick_rows_kernel, array((rows, LANES), table.dtype), [SMEM, H...]
    all_to_all x1, waiting for transfers between devices: 8.89 us -> 6.98 us  [on_device(): blocks = lax.all_to_all(picked.reshape(row_groups, -1, LANES), 'rows', 0, 0)]
    ppermute x2 -> x1, starting transfers between devices: 2.97 us -> 1.07 us  [passed_along(): lax.ppermute(shard, axis, [(i, (i + by) % peers) for i in range(peers)])]
    ppermute x9, waiting for transfers between devices: 4.78 us -> 3.09 us  [swapped(): return lax.ppermute(shard, 'tp', [(i, i ^ by) for i in range(peers)])]
    pallas_call x1, Pallas kernels: 1.31 us -> 2.94 us  [project(): kernel_call(project_kernel, (array((count, width), jnp.bfloat16), array(q...]
    ppermute x2 -> x1, waiting for transfers between devices: 2.4 us -> 3.63 us  [passed_along(): lax.ppermute(shard, axis, [(i, (i + by) % peers) for i in range(peers)])]
  transfers between devices with their start and end apart: 12 -> 11, of which waited for: 7 -> 5; matrix products, arithmetic and copies ran while one was open for 0% -> 0% of each run, Pallas kernels for 2% -> 8%
where the time goes in v3:
time: 69.8 us; the launch traced here: 69.6 us
  blocking collectives  20 us (29%)
  Pallas kernels  19.1 us (27%)
  starting transfers between devices  15.2 us (22%)
  waiting for transfers between devices  13.7 us (20%)
  between operations  0.8 us (1%)
  local copies, waits for them, and re-layouts  0.74 us (1%)
    all_to_all x1, blocking collectives, on_device(): lax.all_to_all(jnp.broadcast_to(tokens[None], (row_groups,) + tokens.shap...  20 us
    ppermute x9, starting transfers between devices, swapped(): return lax.ppermute(shard, 'tp', [(i, i ^ by) for i in range(peers)])  10.3 us
    pallas_call x1, Pallas kernels, pick_rows(): kernel_call(pick_rows_kernel, array((rows, LANES), table.dtype), [SMEM, H...  8.13 us
    all_to_all x1, waiting for transfers between devices, on_device(): blocks = lax.all_to_all(picked.reshape(row_groups, -1, LANES), 'rows', 0, 0)  6.98 us
    all_to_all x1, starting transfers between devices, on_device(): blocks = lax.all_to_all(picked.reshape(row_groups, -1, LANES), 'rows', 0, 0)  3.87 us
    ppermute x1, waiting for transfers between devices, passed_along(): lax.ppermute(shard, axis, [(i, (i + by) % peers) for i in range(peers)])  3.63 us
    ppermute x9, waiting for transfers between devices, swapped(): return lax.ppermute(shard, 'tp', [(i, i ^ by) for i in range(peers)])  3.09 us
    pallas_call x1, Pallas kernels, project(): kernel_call(project_kernel, (array((count, width), jnp.bfloat16), array(q...  2.94 us
  transfers between devices with their start and end apart: 11, of which 5 were waited for; matrix products, arithmetic and copies ran while one was open for 0% of the time, Pallas kernels for 8%

profile of v3, /device:TPU:1, one launch (start us, length us, event | category | flops | bytes accessed | tf_op | source)
XLA Modules:
  0.0 69.6 jit_solution(16512657290558536545)
XLA Ops:
  0.6 0.7 broadcast_in_dim.2
  1.3 20.0 %all_to_all.10.token_ref = s32[32,4,4]{2,1,0:T(4,128)S(1)} all-to-all(s32[32,4,4]{2,1,0:T(4,128)S(1)} %broadcast_in_dim.2), channel_id=1, replica_groups=mesh['rows'=32,'tp'=4] {'rows'}, dimensions={0} | all-to-all | bytes 4096 | tf_op jit(solution)/shard_map/all_to_all | solution.py:566
  21.3 8.1 %pick_rows.1 = bf16[256,128]{1,0:T(8,128)(2,1)} custom-call(s32[32,4,4]{2,1,0:T(4,128)S(1)} %all_to_all.10.token_ref, bf16[64,76032]{1,0:T(8,128)(2,1)} %bitcast.15), custom_call_target="tpu_custom_call" | custom-call | tf_op jit(solution)/shard_map/pick_rows/pallas_call | solution.py:107
  29.4 3.9 %all-to-all-start.1 = ((bf16[32,8,128]{2,1,0:T(8,128)(2,1)}), bf16[32,8,128]{2,1,0:T(8,128)(2,1)S(1)}, u32[]{:S(2)}, u32[]{:S(2)}) async-start(bf16[32,8,128]{2,1,0:T(8,128)(2,1)} %bitcast.3), calls=%async_computation.1 | async-start | bytes 131072 | tf_op jit(solution)/shard_map/all_to_all | solution.py:570
  33.3 0.0 copy-start.7
  33.3 1.9 %stage_weights.1.early_ref = bf16[1536,1024]{1,0:T(8,128)(2,1)S(1)} custom-call(bf16[2048,1024]{1,0:T(8,128)(2,1)} %value_ref.1), custom_call_target="tpu_custom_call" | custom-call | bytes 6291456 | tf_op jit(solution)/shard_map/stage_weights/pallas_call | solution.py:137
  35.2 0.0 copy-done.7
  35.2 7.0 %all-to-all-done.1 = bf16[32,8,128]{2,1,0:T(8,128)(2,1)S(1)} async-done(((bf16[32,8,128]{2,1,0:T(8,128)(2,1)}), bf16[32,8,128]{2,1,0:T(8,128)(2,1)S(1)}, u32[]{:S(2)}, u32[]{:S(2)}) %all-to-all-start.1) | async-done | bytes 65568 | tf_op jit(solution)/shard_map/all_to_all | solution.py:570
  42.2 0.0 copy-start.2
  42.2 0.0 copy-start.5
  42.2 2.9 %project.1 = (bf16[16,2048]{1,0:T(8,128)(2,1)S(1)}, bf16[8,32,128]{2,1,0:T(8,128)(2,1)S(1)}, f32[16,640]{1,0:T(8,128)S(1)}, f32[16,640]{1,0:T(8,128)S(1)}, f32[16,640]{1,0:T(8,128)S(1)}, /*index=5*/f32[16,640]{1,0:T(8,128)S(1)}) custom-call(s32[1]{0:T(128)} %bitcast.tp_ref, bf16[256,128]{1,0:T(8,128)(2,1)S(1)} %bitcast.10, f32[1,2048]{1,0:T(1,128)S(1)} %bitcast.13, ...), custom_call_target="tpu_custom_call" | custom-call | flops 134217728 | bytes 8388608 | tf_op jit(solution)/shard_map/project/pallas_call | solution.py:215
  45.2 0.0 copy-start
  45.2 0.0 copy-start.8
  45.2 0.0 copy-start.9
  45.2 0.0 copy-start.3
  45.2 0.0 copy-start.6
  45.2 3.3 %collective-permute-start = (f32[16,640]{1,0:T(8,128)S(1)}, f32[16,640]{1,0:T(8,128)S(1)}, u32[]{:S(2)}, u32[]{:S(2)}) collective-permute-start(f32[16,640]{1,0:T(8,128)S(1)} %get-tuple-element.13), channel_id=1, source_target_pairs={{0,1},{1,0},{2,3},{3,2},{4,5},{5,4},{6,7},{7,6},{8,9},{9,8},{10,11... | collective-permute-start | bytes 122888 | tf_op jit(solution)/shard_map/ppermute | solution.py:531
  48.5 0.3 collective-permute-start.1
  48.8 1.4 %collective-permute-start.2 = (f32[16,640]{1,0:T(8,128)S(1)}, f32[16,640]{1,0:T(8,128)S(1)}, u32[]{:S(2)}, u32[]{:S(2)}) collective-permute-start(f32[16,640]{1,0:T(8,128)S(1)} %get-tuple-element.15), channel_id=1, source_target_pairs={{0,3},{1,2},{2,1},{3,0},{4,7},{5,6},{6,5},{7,4},{8,11},{9,10},{10,... | collective-permute-start | bytes 122888 | tf_op jit(solution)/shard_map/ppermute | solution.py:531
  50.2 0.0 copy-done.2
  50.2 0.0 copy-done.5
  50.2 1.4 %policy_scores.1 = (f32[8,32,1024]{2,1,0:T(8,128)S(1)}, f32[8,32,128]{2,1,0:T(8,128)S(1)}) custom-call(s32[4]{0:T(128)S(1)} %copy-done.5, bf16[8,32,128]{2,1,0:T(8,128)(2,1)S(1)} %get-tuple-element.16.query_ref, bf16[4,1024,256]{2,1,0:T(8,128)(2,1)S(1)} %copy-done.2), custom_call_target="tpu_custom_call" | custom-call | flops 67108864 | bytes 3145728 | tf_op jit(solution)/shard_map/policy_scores/pallas_call | solution.py:258
  51.7 0.0 copy-start.1
  51.7 0.0 copy-start.4
  51.7 0.0 collective-permute-done.one_ref
  51.7 0.0 collective-permute-done.1.two_ref
  51.7 1.1 %collective-permute-done.2.three_ref = f32[16,640]{1,0:T(8,128)S(1)} collective-permute-done((f32[16,640]{1,0:T(8,128)S(1)}, f32[16,640]{1,0:T(8,128)S(1)}, u32[]{:S(2)}, u32[]{:S(2)}) %collective-permute-start.2) | collective-permute-done | bytes 40992 | tf_op jit(solution)/shard_map/ppermute | solution.py:531
  52.8 0.0 copy-done
  52.8 1.0 %policy.1.rows_ref = bf16[16,2048]{1,0:T(8,128)(2,1)S(1)} custom-call(f32[16,640]{1,0:T(8,128)S(1)} %get-tuple-element.12.own_ref, f32[16,640]{1,0:T(8,128)S(1)} %collective-permute-done.one_ref, f32[16,640]{1,0:T(8,128)S(1)} %collective-permute-done.1.two_ref, f32[16,640]{1,0:T(8,128)S(1)} %collective-permute-done.2.three_ref, ...), custom_call_target="tpu_custom_call" | custom-call | flops 67108864 | bytes 3145728 | tf_op jit(solution)/shard_map/policy/pallas_call | solution.py:357
  53.7 1.1 %collective-permute-start.3 = (bf16[16,2048]{1,0:T(8,128)(2,1)S(1)}, bf16[16,2048]{1,0:T(8,128)(2,1)S(1)}, u32[]{:S(2)}, u32[]{:S(2)}) collective-permute-start(bf16[16,2048]{1,0:T(8,128)(2,1)S(1)} %policy.1.rows_ref), channel_id=1, source_target_pairs={{0,64},{4,68},{8,72},{12,76},{16,80},{20,84},{24,88},{28,92},{32,9... | collective-permute-start | bytes 196616 | tf_op jit(solution)/shard_map/ppermute | solution.py:536
  54.8 3.6 %collective-permute-done.3.rows_ref = bf16[16,2048]{1,0:T(8,128)(2,1)S(1)} collective-permute-done((bf16[16,2048]{1,0:T(8,128)(2,1)S(1)}, bf16[16,2048]{1,0:T(8,128)(2,1)S(1)}, u32[]{:S(2)}, u32[]{:S(2)}) %collective-permute-start.3) | collective-permute-done | bytes 65568 | tf_op jit(solution)/shard_map/ppermute | solution.py:536
  58.5 0.1 row_squares.1.own_ref
  58.5 1.4 %collective-permute-start.4 = (f32[16,128]{1,0:T(8,128)S(1)}, f32[16,128]{1,0:T(8,128)S(1)}, u32[]{:S(2)}, u32[]{:S(2)}) collective-permute-start(f32[16,128]{1,0:T(8,128)S(1)} %row_squares.1.own_ref), channel_id=1, source_target_pairs={{0,1},{1,0},{2,3},{3,2},{4,5},{5,4},{6,7},{7,6},{8,9},{9,8},{10,11... | collective-permute-start | bytes 24584 | tf_op jit(solution)/shard_map/ppermute | solution.py:531
  60.0 0.8 %collective-permute-start.5 = (f32[16,128]{1,0:T(8,128)S(1)}, f32[16,128]{1,0:T(8,128)S(1)}, u32[]{:S(2)}, u32[]{:S(2)}) collective-permute-start(f32[16,128]{1,0:T(8,128)S(1)} %row_squares.1.own_ref), channel_id=1, source_target_pairs={{0,2},{1,3},{2,0},{3,1},{4,6},{5,7},{6,4},{7,5},{8,10},{9,11},{10,... | collective-permute-start | bytes 24584 | tf_op jit(solution)/shard_map/ppermute | solution.py:531
  60.8 0.9 %collective-permute-start.6 = (f32[16,128]{1,0:T(8,128)S(1)}, f32[16,128]{1,0:T(8,128)S(1)}, u32[]{:S(2)}, u32[]{:S(2)}) collective-permute-start(f32[16,128]{1,0:T(8,128)S(1)} %row_squares.1.own_ref), channel_id=1, source_target_pairs={{0,3},{1,2},{2,1},{3,0},{4,7},{5,6},{6,5},{7,4},{8,11},{9,10},{10,... | collective-permute-start | bytes 24584 | tf_op jit(solution)/shard_map/ppermute | solution.py:531
  61.7 0.0 copy-done.8
  61.7 0.0 copy-done.9
  61.7 0.0 copy-done.3
  61.7 0.0 copy-done.6
  61.7 1.4 %critic_scores.1 = (f32[8,32,1024]{2,1,0:T(8,128)S(1)}, f32[8,32,128]{2,1,0:T(8,128)S(1)}) custom-call(s32[4]{0:T(128)S(1)} %copy-done.6, bf16[16,2048]{1,0:T(8,128)(2,1)S(1)} %collective-permute-done.3.rows_ref, f32[1,2048]{1,0:T(1,128)S(1)} %bitcast.14, bf16[4,1024,256]{2,1,0:T(8,128)(2,1)S(1)} %copy-done.3), custom_call_target="tpu_custom_call" | custom-call | flops 67108864 | bytes 3145728 | tf_op jit(solution)/shard_map/critic_scores/pallas_call | solution.py:427
  63.2 0.0 collective-permute-done.4.one_ref
  63.2 0.0 collective-permute-done.5.two_ref
  63.2 0.7 collective-permute-done.6.three_ref
  63.9 0.0 copy-done.1
  63.9 0.0 copy-done.4
  63.9 0.7 %critic.1.own_ref = f32[16,128]{1,0:T(8,128)S(1)} custom-call(f32[16,128]{1,0:T(8,128)S(1)} %row_squares.1.own_ref, f32[16,128]{1,0:T(8,128)S(1)} %collective-permute-done.4.one_ref, f32[16,128]{1,0:T(8,128)S(1)} %collective-permute-done.5.two_ref, f32[16,128]{1,0:T(8,128)S(1)} %collective-permute-done.6.three_ref, ...), custom_call_target="tpu_custom_call" | custom-call | flops 67108864 | bytes 3145728 | tf_op jit(solution)/shard_map/critic/pallas_call | solution.py:490
  64.6 0.4 collective-permute-start.7
  65.0 0.6 collective-permute-start.8
  65.6 1.1 %collective-permute-start.9 = (f32[16,128]{1,0:T(8,128)S(1)}, f32[16,128]{1,0:T(8,128)S(1)}, u32[]{:S(2)}, u32[]{:S(2)}) collective-permute-start(f32[16,128]{1,0:T(8,128)S(1)} %critic.1.own_ref), channel_id=1, source_target_pairs={{0,3},{1,2},{2,1},{3,0},{4,7},{5,6},{6,5},{7,4},{8,11},{9,10},{10,... | collective-permute-start | bytes 24584 | tf_op jit(solution)/shard_map/ppermute | solution.py:531
  66.8 0.7 by_step.1
  67.4 0.0 collective-permute-done.7.one_ref
  67.5 0.0 collective-permute-done.8.two_ref
  67.5 1.3 %collective-permute-done.9.three_ref = f32[16,128]{1,0:T(8,128)S(1)} collective-permute-done((f32[16,128]{1,0:T(8,128)S(1)}, f32[16,128]{1,0:T(8,128)S(1)}, u32[]{:S(2)}, u32[]{:S(2)}) %collective-permute-start.9) | collective-permute-done | bytes 8224 | tf_op jit(solution)/shard_map/ppermute | solution.py:531
  68.8 0.8 %expect.1 = f32[4,4]{1,0:T(4,128)} custom-call(f32[16,128]{1,0:T(8,128)S(1)} %critic.1.own_ref, f32[16,128]{1,0:T(8,128)S(1)} %collective-permute-done.7.one_ref, f32[16,128]{1,0:T(8,128)S(1)} %collective-permute-done.8.two_ref, f32[16,128]{1,0:T(8,128)S(1)} %collective-permute-done.9.three_ref), custom_call_target="tpu_custom_call" | custom-call | tf_op jit(solution)/shard_map/expect/pallas_call | solution.py:526
  (3 shorter events, 0.0 us)
Async XLA Ops:
  29.4 12.8 %all-to-all-start.1 = ((bf16[32,8,128]{2,1,0:T(8,128)(2,1)}), bf16[32,8,128]{2,1,0:T(8,128)(2,1)S(1)}, u32[]{:S(2)}, u32[]{:S(2)}) async-start(bf16[32,8,128]{2,1,0:T(8,128)(2,1)} %bitcast.3), calls=%async_computation.1 | async-start | bytes 131072 | tf_op jit(solution)/shard_map/all_to_all | solution.py:570
  33.3 1.9 %copy-start.7 = (bf16[2048]{0:T(1024)(128)(2,1)S(1)}, bf16[2048]{0:T(1024)(128)(2,1)}, u32[]{:S(2)}) copy-start(bf16[2048]{0:T(1024)(128)(2,1)} %param.17) | copy-start | bytes 12292
  42.2 8.0 %copy-start.2 = (bf16[4,1024,256]{2,1,0:T(8,128)(2,1)S(1)}, bf16[4,1024,256]{2,1,0:T(8,128)(2,1)}, u32[]{:S(2)}) copy-start(bf16[4,1024,256]{2,1,0:T(8,128)(2,1)} %keys_ref.2) | copy-start | bytes 6291460
  42.2 8.0 %copy-start.5 = (s32[4]{0:T(128)S(1)}, s32[4]{0:T(128)}, u32[]{:S(2)}) copy-start(s32[4]{0:T(128)} %length_ref.2) | copy-start | bytes 52
  45.2 7.6 %copy-start = (bf16[4,1024,256]{2,1,0:T(8,128)(2,1)S(1)}, bf16[4,1024,256]{2,1,0:T(8,128)(2,1)}, u32[]{:S(2)}) copy-start(bf16[4,1024,256]{2,1,0:T(8,128)(2,1)} %values_ref.2) | copy-start | bytes 6291460
  45.2 16.5 %copy-start.8 = (bf16[2048]{0:T(1024)(128)(2,1)S(1)}, bf16[2048]{0:T(1024)(128)(2,1)}, u32[]{:S(2)}) copy-start(bf16[2048]{0:T(1024)(128)(2,1)} %param.23) | copy-start | bytes 12292
  45.2 16.5 %copy-start.9 = (bf16[2048]{0:T(1024)(128)(2,1)S(1)}, bf16[2048]{0:T(1024)(128)(2,1)}, u32[]{:S(2)}) copy-start(bf16[2048]{0:T(1024)(128)(2,1)} %param.26) | copy-start | bytes 12292
  45.2 16.5 %copy-start.3 = (bf16[4,1024,256]{2,1,0:T(8,128)(2,1)S(1)}, bf16[4,1024,256]{2,1,0:T(8,128)(2,1)}, u32[]{:S(2)}) copy-start(bf16[4,1024,256]{2,1,0:T(8,128)(2,1)} %keys_ref.3) | copy-start | bytes 6291460
  45.2 16.5 %copy-start.6 = (s32[4]{0:T(128)S(1)}, s32[4]{0:T(128)}, u32[]{:S(2)}) copy-start(s32[4]{0:T(128)} %length_ref.3) | copy-start | bytes 52
  45.2 6.4 %collective-permute-start = (f32[16,640]{1,0:T(8,128)S(1)}, f32[16,640]{1,0:T(8,128)S(1)}, u32[]{:S(2)}, u32[]{:S(2)}) collective-permute-start(f32[16,640]{1,0:T(8,128)S(1)} %get-tuple-element.13), channel_id=1, source_target_pairs={{0,1},{1,0},{2,3},{3,2},{4,5},{5,4},{6,7},{7,6},{8,9},{9,8},{10,11... | collective-permute-start | bytes 122888 | tf_op jit(solution)/shard_map/ppermute | solution.py:531
  48.5 3.2 %collective-permute-start.1 = (f32[16,640]{1,0:T(8,128)S(1)}, f32[16,640]{1,0:T(8,128)S(1)}, u32[]{:S(2)}, u32[]{:S(2)}) collective-permute-start(f32[16,640]{1,0:T(8,128)S(1)} %get-tuple-element.14), channel_id=1, source_target_pairs={{0,2},{1,3},{2,0},{3,1},{4,6},{5,7},{6,4},{7,5},{8,10},{9,11},{10,... | collective-permute-start | bytes 122888 | tf_op jit(solution)/shard_map/ppermute | solution.py:531
  48.8 4.0 %collective-permute-start.2 = (f32[16,640]{1,0:T(8,128)S(1)}, f32[16,640]{1,0:T(8,128)S(1)}, u32[]{:S(2)}, u32[]{:S(2)}) collective-permute-start(f32[16,640]{1,0:T(8,128)S(1)} %get-tuple-element.15), channel_id=1, source_target_pairs={{0,3},{1,2},{2,1},{3,0},{4,7},{5,6},{6,5},{7,4},{8,11},{9,10},{10,... | collective-permute-start | bytes 122888 | tf_op jit(solution)/shard_map/ppermute | solution.py:531
  51.7 12.2 %copy-start.1 = (bf16[4,1024,256]{2,1,0:T(8,128)(2,1)S(1)}, bf16[4,1024,256]{2,1,0:T(8,128)(2,1)}, u32[]{:S(2)}) copy-start(bf16[4,1024,256]{2,1,0:T(8,128)(2,1)} %values_ref.3) | copy-start | bytes 6291460
  51.7 12.2 %copy-start.4 = (bf16[2048,51]{0,1:T(8,128)(2,1)S(1)}, bf16[2048,51]{0,1:T(8,128)(2,1)}, u32[]{:S(2)}) copy-start(bf16[2048,51]{0,1:T(8,128)(2,1)} %param.27) | copy-start | bytes 626692
  53.7 4.7 %collective-permute-start.3 = (bf16[16,2048]{1,0:T(8,128)(2,1)S(1)}, bf16[16,2048]{1,0:T(8,128)(2,1)S(1)}, u32[]{:S(2)}, u32[]{:S(2)}) collective-permute-start(bf16[16,2048]{1,0:T(8,128)(2,1)S(1)} %policy.1.rows_ref), channel_id=1, source_target_pairs={{0,64},{4,68},{8,72},{12,76},{16,80},{20,84},{24,88},{28,92},{32,9... | collective-permute-start | bytes 196616 | tf_op jit(solution)/shard_map/ppermute | solution.py:536
  58.5 4.6 %collective-permute-start.4 = (f32[16,128]{1,0:T(8,128)S(1)}, f32[16,128]{1,0:T(8,128)S(1)}, u32[]{:S(2)}, u32[]{:S(2)}) collective-permute-start(f32[16,128]{1,0:T(8,128)S(1)} %row_squares.1.own_ref), channel_id=1, source_target_pairs={{0,1},{1,0},{2,3},{3,2},{4,5},{5,4},{6,7},{7,6},{8,9},{9,8},{10,11... | collective-permute-start | bytes 24584 | tf_op jit(solution)/shard_map/ppermute | solution.py:531
  60.0 3.2 %collective-permute-start.5 = (f32[16,128]{1,0:T(8,128)S(1)}, f32[16,128]{1,0:T(8,128)S(1)}, u32[]{:S(2)}, u32[]{:S(2)}) collective-permute-start(f32[16,128]{1,0:T(8,128)S(1)} %row_squares.1.own_ref), channel_id=1, source_target_pairs={{0,2},{1,3},{2,0},{3,1},{4,6},{5,7},{6,4},{7,5},{8,10},{9,11},{10,... | collective-permute-start | bytes 24584 | tf_op jit(solution)/shard_map/ppermute | solution.py:531
  60.8 3.1 %collective-permute-start.6 = (f32[16,128]{1,0:T(8,128)S(1)}, f32[16,128]{1,0:T(8,128)S(1)}, u32[]{:S(2)}, u32[]{:S(2)}) collective-permute-start(f32[16,128]{1,0:T(8,128)S(1)} %row_squares.1.own_ref), channel_id=1, source_target_pairs={{0,3},{1,2},{2,1},{3,0},{4,7},{5,6},{6,5},{7,4},{8,11},{9,10},{10,... | collective-permute-start | bytes 24584 | tf_op jit(solution)/shard_map/ppermute | solution.py:531
  64.6 2.9 %collective-permute-start.7 = (f32[16,128]{1,0:T(8,128)S(1)}, f32[16,128]{1,0:T(8,128)S(1)}, u32[]{:S(2)}, u32[]{:S(2)}) collective-permute-start(f32[16,128]{1,0:T(8,128)S(1)} %critic.1.own_ref), channel_id=1, source_target_pairs={{0,1},{1,0},{2,3},{3,2},{4,5},{5,4},{6,7},{7,6},{8,9},{9,8},{10,11... | collective-permute-start | bytes 24584 | tf_op jit(solution)/shard_map/ppermute | solution.py:531
  65.0 2.5 %collective-permute-start.8 = (f32[16,128]{1,0:T(8,128)S(1)}, f32[16,128]{1,0:T(8,128)S(1)}, u32[]{:S(2)}, u32[]{:S(2)}) collective-permute-start(f32[16,128]{1,0:T(8,128)S(1)} %critic.1.own_ref), channel_id=1, source_target_pairs={{0,2},{1,3},{2,0},{3,1},{4,6},{5,7},{6,4},{7,5},{8,10},{9,11},{10,... | collective-permute-start | bytes 24584 | tf_op jit(solution)/shard_map/ppermute | solution.py:531
  65.6 3.1 %collective-permute-start.9 = (f32[16,128]{1,0:T(8,128)S(1)}, f32[16,128]{1,0:T(8,128)S(1)}, u32[]{:S(2)}, u32[]{:S(2)}) collective-permute-start(f32[16,128]{1,0:T(8,128)S(1)} %critic.1.own_ref), channel_id=1, source_target_pairs={{0,3},{1,2},{2,1},{3,0},{4,7},{5,6},{6,5},{7,4},{8,11},{9,10},{10,... | collective-permute-start | bytes 24584 | tf_op jit(solution)/shard_map/ppermute | solution.py:531

commit v4 on v3

--- a/solution.py
+++ b/solution.py
@@ -49,32 +49,42 @@
     return pltpu.with_memory_space_constraint(x, pltpu.HBM)
 
 
+def lay_out_kernel(token_ref, out_ref):
+    row = jnp.concatenate([token_ref[step : step + 1, :] for step in range(4)], axis=1)
+    out_ref[...] = jnp.broadcast_to(row[None], out_ref.shape)
+
+
+def laid_out(tokens, copies):
+    out = array((copies, 1, tokens.size), tokens.dtype)
+    return kernel_call(lay_out_kernel, out, [VMEM], name="lay_out")(tokens)
+
+
 def pick_rows_kernel(token_ref, table_ref, out_ref, tiles_ref, sems):
     width = table_ref.shape[0]
     pieces = sems.shape[0]
-    places = tiles_ref.shape[1] // pieces
+    destinations = token_ref.shape[0] // pieces
+    places = 8 * destinations
     lane = lax.broadcasted_iota(jnp.int32, (width, LANES), 1)
 
-    def token_of(place, half):
-        destination = lax.shift_right_logical(place, 3)
-        decode_step = jnp.bitwise_and(place, 3)
-        row = jnp.bitwise_and(lax.shift_right_logical(place, 2), 1)
-        return token_ref[destination, decode_step, row + 2 * half]
+    def token_of(destination, i, half):
+        m = 8 * half + i
+        return token_ref[destination, 0, 4 * (m % 4) + m // 4]
 
     for piece in range(pieces):
 
-        def fetch(i, carry):
-            place = piece * places + i
+        def fetch(at, carry):
+            destination = piece * destinations + at
             for half in range(2):
-                block = jnp.bitwise_and(token_of(place, half), ~(LANES - 1))
-                pltpu.make_async_copy(
-                    table_ref.at[:, pl.ds(pl.multiple_of(block, LANES), LANES)],
-                    tiles_ref.at[half, place],
-                    sems.at[piece],
-                ).start()
+                for i in range(8):
+                    block = jnp.bitwise_and(token_of(destination, i, half), ~(LANES - 1))
+                    pltpu.make_async_copy(
+                        table_ref.at[:, pl.ds(pl.multiple_of(block, LANES), LANES)],
+                        tiles_ref.at[half, 8 * destination + i],
+                        sems.at[piece],
+                    ).start()
             return carry
 
-        lax.fori_loop(0, places, fetch, 0, unroll=8)
+        lax.fori_loop(0, destinations, fetch, 0)
 
     empty = jnp.zeros((width, LANES), jnp.float32)
     pair = (empty, empty)
@@ -83,17 +93,19 @@
         pltpu.make_async_copy(part, part, sems.at[piece]).wait()
         first_place = piece * places % LANES
 
-        def step(i, carry):
-            place = piece * places + i
-            here = lane == first_place + i
-            kept = []
-            for half in range(2):
-                shift = jnp.bitwise_and(place - token_of(place, half), LANES - 1)
-                tile = pltpu.roll(tiles_ref[half, place].astype(jnp.float32), shift, 1)
-                kept.append(jnp.where(here, tile, carry[half]))
-            return tuple(kept)
-
-        pair = lax.fori_loop(0, places, step, pair, unroll=min(places, 32))
+        def step(at, carry):
+            destination = piece * destinations + at
+            pair = list(carry)
+            for i in range(8):
+                place = 8 * destination + i
+                here = lane == first_place + 8 * at + i
+                for half in range(2):
+                    shift = jnp.bitwise_and(place - token_of(destination, i, half), LANES - 1)
+                    tile = pltpu.roll(tiles_ref[half, place].astype(jnp.float32), shift, 1)
+                    pair[half] = jnp.where(here, tile, pair[half])
+            return tuple(pair)
+
+        pair = lax.fori_loop(0, destinations, step, pair, unroll=min(destinations, 4))
         if first_place + places == LANES:
             both = jnp.concatenate(pair, axis=0)
             rows = pl.ds((piece + 1) * places - LANES, LANES)
@@ -563,9 +575,7 @@
         return gain.astype(jnp.float32).reshape(1, -1)
 
     table = embedding.transpose(1, 2, 0).reshape(embedding.shape[2], embedding.shape[0])
-    all_tokens = lax.all_to_all(
-        jnp.broadcast_to(tokens[None], (row_groups,) + tokens.shape), "rows", 0, 0
-    )
+    all_tokens = lax.all_to_all(laid_out(tokens, row_groups), "rows", 0, 0)
     picked = pick_rows(all_tokens, table)
     blocks = lax.all_to_all(picked.reshape(row_groups, -1, LANES), "rows", 0, 0)
     x, query, parts = project(

time: 69.8 us -> 67.7 us (0.970)
  Pallas kernels: 19.1 us -> 17.2 us
    pallas_call x1, Pallas kernels: 8.13 us -> 6.13 us  [pick_rows(): kernel_call(pick_rows_kernel, array((rows, LANES), table.dtype), [SMEM, H...]
where the time goes in v4:
time: 67.7 us; the launch traced here: 67.5 us
  blocking collectives  19.8 us (29%)
  Pallas kernels  17.2 us (25%)
  starting transfers between devices  15.3 us (23%)
  waiting for transfers between devices  13.7 us (20%)
  between operations  0.81 us (1%)
  local copies, waits for them, and re-layouts  0.73 us (1%)
    all_to_all x1, blocking collectives, on_device(): all_tokens = lax.all_to_all(laid_out(tokens, row_groups), 'rows', 0, 0)  19.8 us
    ppermute x9, starting transfers between devices, swapped(): return lax.ppermute(shard, 'tp', [(i, i ^ by) for i in range(peers)])  10.3 us
    all_to_all x1, waiting for transfers between devices, on_device(): blocks = lax.all_to_all(picked.reshape(row_groups, -1, LANES), 'rows', 0, 0)  6.98 us
    pallas_call x1, Pallas kernels, pick_rows(): kernel_call(pick_rows_kernel, array((rows, LANES), table.dtype), [SMEM, H...  6.13 us
    all_to_all x1, starting transfers between devices, on_device(): blocks = lax.all_to_all(picked.reshape(row_groups, -1, LANES), 'rows', 0, 0)  3.87 us
    ppermute x1, waiting for transfers between devices, passed_along(): lax.ppermute(shard, axis, [(i, (i + by) % peers) for i in range(peers)])  3.63 us
    ppermute x9, waiting for transfers between devices, swapped(): return lax.ppermute(shard, 'tp', [(i, i ^ by) for i in range(peers)])  3.09 us
    pallas_call x1, Pallas kernels, project(): kernel_call(project_kernel, (array((count, width), jnp.bfloat16), array(q...  2.94 us
  transfers between devices with their start and end apart: 11, of which 5 were waited for; matrix products, arithmetic and copies ran while one was open for 0% of the time, Pallas kernels for 8%

profile of v4, /device:TPU:1, one launch (start us, length us, event | category | flops | bytes accessed | tf_op | source)
XLA Modules:
  0.0 67.5 jit_solution(15722359977913331786)
XLA Ops:
  0.6 0.0 copy-start.5
  0.6 0.7 copy-done.5
  1.3 0.1 lay_out.1
  1.4 19.8 %all_to_all.10.token_ref = s32[32,1,16]{2,1,0:T(1,128)S(1)} all-to-all(s32[32,1,16]{2,1,0:T(1,128)S(1)} %lay_out.1), channel_id=1, replica_groups=mesh['rows'=32,'tp'=4] {'rows'}, dimensions={0} | all-to-all | bytes 4096 | tf_op jit(solution)/shard_map/all_to_all | solution.py:578
  21.2 6.1 %pick_rows.1 = bf16[256,128]{1,0:T(8,128)(2,1)} custom-call(s32[32,1,16]{2,1,0:T(1,128)S(1)} %all_to_all.10.token_ref, bf16[64,76032]{1,0:T(8,128)(2,1)} %bitcast.15), custom_call_target="tpu_custom_call" | custom-call | tf_op jit(solution)/shard_map/pick_rows/pallas_call | solution.py:119
  27.3 3.9 %all-to-all-start.1 = ((bf16[32,8,128]{2,1,0:T(8,128)(2,1)}), bf16[32,8,128]{2,1,0:T(8,128)(2,1)S(1)}, u32[]{:S(2)}, u32[]{:S(2)}) async-start(bf16[32,8,128]{2,1,0:T(8,128)(2,1)} %bitcast.3), calls=%async_computation.1 | async-start | bytes 131072 | tf_op jit(solution)/shard_map/all_to_all | solution.py:580
  31.2 0.0 copy-start.8
  31.2 1.9 %stage_weights.1.early_ref = bf16[1536,1024]{1,0:T(8,128)(2,1)S(1)} custom-call(bf16[2048,1024]{1,0:T(8,128)(2,1)} %value_ref.1), custom_call_target="tpu_custom_call" | custom-call | bytes 6291456 | tf_op jit(solution)/shard_map/stage_weights/pallas_call | solution.py:149
  33.1 0.0 copy-done.8
  33.1 7.0 %all-to-all-done.1 = bf16[32,8,128]{2,1,0:T(8,128)(2,1)S(1)} async-done(((bf16[32,8,128]{2,1,0:T(8,128)(2,1)}), bf16[32,8,128]{2,1,0:T(8,128)(2,1)S(1)}, u32[]{:S(2)}, u32[]{:S(2)}) %all-to-all-start.1) | async-done | bytes 65568 | tf_op jit(solution)/shard_map/all_to_all | solution.py:580
  40.1 0.0 copy-start.2
  40.1 0.0 copy-start.6
  40.1 2.9 %project.1 = (bf16[16,2048]{1,0:T(8,128)(2,1)S(1)}, bf16[8,32,128]{2,1,0:T(8,128)(2,1)S(1)}, f32[16,640]{1,0:T(8,128)S(1)}, f32[16,640]{1,0:T(8,128)S(1)}, f32[16,640]{1,0:T(8,128)S(1)}, /*index=5*/f32[16,640]{1,0:T(8,128)S(1)}) custom-call(s32[1]{0:T(128)} %bitcast.tp_ref, bf16[256,128]{1,0:T(8,128)(2,1)S(1)} %bitcast.10, f32[1,2048]{1,0:T(1,128)S(1)} %bitcast.13, ...), custom_call_target="tpu_custom_call" | custom-call | flops 134217728 | bytes 8388608 | tf_op jit(solution)/shard_map/project/pallas_call | solution.py:227
  43.1 0.0 copy-start
  43.1 0.0 copy-start.9
  43.1 0.0 copy-start.10
  43.1 0.0 copy-start.3
  43.1 0.0 copy-start.7
  43.1 3.3 %collective-permute-start = (f32[16,640]{1,0:T(8,128)S(1)}, f32[16,640]{1,0:T(8,128)S(1)}, u32[]{:S(2)}, u32[]{:S(2)}) collective-permute-start(f32[16,640]{1,0:T(8,128)S(1)} %get-tuple-element.13), channel_id=1, source_target_pairs={{0,1},{1,0},{2,3},{3,2},{4,5},{5,4},{6,7},{7,6},{8,9},{9,8},{10,11... | collective-permute-start | bytes 122888 | tf_op jit(solution)/shard_map/ppermute | solution.py:543
  46.4 0.3 collective-permute-start.1
  46.7 1.4 %collective-permute-start.2 = (f32[16,640]{1,0:T(8,128)S(1)}, f32[16,640]{1,0:T(8,128)S(1)}, u32[]{:S(2)}, u32[]{:S(2)}) collective-permute-start(f32[16,640]{1,0:T(8,128)S(1)} %get-tuple-element.15), channel_id=1, source_target_pairs={{0,3},{1,2},{2,1},{3,0},{4,7},{5,6},{6,5},{7,4},{8,11},{9,10},{10,... | collective-permute-start | bytes 122888 | tf_op jit(solution)/shard_map/ppermute | solution.py:543
  48.1 0.0 copy-done.2
  48.1 0.0 copy-done.6
  48.1 1.4 %policy_scores.1 = (f32[8,32,1024]{2,1,0:T(8,128)S(1)}, f32[8,32,128]{2,1,0:T(8,128)S(1)}) custom-call(s32[4]{0:T(128)S(1)} %copy-done.6, bf16[8,32,128]{2,1,0:T(8,128)(2,1)S(1)} %get-tuple-element.16.query_ref, bf16[4,1024,256]{2,1,0:T(8,128)(2,1)S(1)} %copy-done.2), custom_call_target="tpu_custom_call" | custom-call | flops 67108864 | bytes 3145728 | tf_op jit(solution)/shard_map/policy_scores/pallas_call | solution.py:270
  49.6 0.0 copy-start.1
  49.6 0.0 copy-start.4
  49.6 0.0 collective-permute-done.one_ref
  49.6 0.0 collective-permute-done.1.two_ref
  49.6 1.1 %collective-permute-done.2.three_ref = f32[16,640]{1,0:T(8,128)S(1)} collective-permute-done((f32[16,640]{1,0:T(8,128)S(1)}, f32[16,640]{1,0:T(8,128)S(1)}, u32[]{:S(2)}, u32[]{:S(2)}) %collective-permute-start.2) | collective-permute-done | bytes 40992 | tf_op jit(solution)/shard_map/ppermute | solution.py:543
  50.7 0.0 copy-done
  50.7 1.0 %policy.1.rows_ref = bf16[16,2048]{1,0:T(8,128)(2,1)S(1)} custom-call(f32[16,640]{1,0:T(8,128)S(1)} %get-tuple-element.12.own_ref, f32[16,640]{1,0:T(8,128)S(1)} %collective-permute-done.one_ref, f32[16,640]{1,0:T(8,128)S(1)} %collective-permute-done.1.two_ref, f32[16,640]{1,0:T(8,128)S(1)} %collective-permute-done.2.three_ref, ...), custom_call_target="tpu_custom_call" | custom-call | flops 67108864 | bytes 3145728 | tf_op jit(solution)/shard_map/policy/pallas_call | solution.py:369
  51.6 1.1 %collective-permute-start.3 = (bf16[16,2048]{1,0:T(8,128)(2,1)S(1)}, bf16[16,2048]{1,0:T(8,128)(2,1)S(1)}, u32[]{:S(2)}, u32[]{:S(2)}) collective-permute-start(bf16[16,2048]{1,0:T(8,128)(2,1)S(1)} %policy.1.rows_ref), channel_id=1, source_target_pairs={{0,64},{4,68},{8,72},{12,76},{16,80},{20,84},{24,88},{28,92},{32,9... | collective-permute-start | bytes 196616 | tf_op jit(solution)/shard_map/ppermute | solution.py:548
  52.7 3.6 %collective-permute-done.3.rows_ref = bf16[16,2048]{1,0:T(8,128)(2,1)S(1)} collective-permute-done((bf16[16,2048]{1,0:T(8,128)(2,1)S(1)}, bf16[16,2048]{1,0:T(8,128)(2,1)S(1)}, u32[]{:S(2)}, u32[]{:S(2)}) %collective-permute-start.3) | collective-permute-done | bytes 65568 | tf_op jit(solution)/shard_map/ppermute | solution.py:548
  56.3 0.1 row_squares.1.own_ref
  56.4 1.4 %collective-permute-start.4 = (f32[16,128]{1,0:T(8,128)S(1)}, f32[16,128]{1,0:T(8,128)S(1)}, u32[]{:S(2)}, u32[]{:S(2)}) collective-permute-start(f32[16,128]{1,0:T(8,128)S(1)} %row_squares.1.own_ref), channel_id=1, source_target_pairs={{0,1},{1,0},{2,3},{3,2},{4,5},{5,4},{6,7},{7,6},{8,9},{9,8},{10,11... | collective-permute-start | bytes 24584 | tf_op jit(solution)/shard_map/ppermute | solution.py:543
  57.9 0.8 %collective-permute-start.5 = (f32[16,128]{1,0:T(8,128)S(1)}, f32[16,128]{1,0:T(8,128)S(1)}, u32[]{:S(2)}, u32[]{:S(2)}) collective-permute-start(f32[16,128]{1,0:T(8,128)S(1)} %row_squares.1.own_ref), channel_id=1, source_target_pairs={{0,2},{1,3},{2,0},{3,1},{4,6},{5,7},{6,4},{7,5},{8,10},{9,11},{10,... | collective-permute-start | bytes 24584 | tf_op jit(solution)/shard_map/ppermute | solution.py:543
  58.7 0.9 %collective-permute-start.6 = (f32[16,128]{1,0:T(8,128)S(1)}, f32[16,128]{1,0:T(8,128)S(1)}, u32[]{:S(2)}, u32[]{:S(2)}) collective-permute-start(f32[16,128]{1,0:T(8,128)S(1)} %row_squares.1.own_ref), channel_id=1, source_target_pairs={{0,3},{1,2},{2,1},{3,0},{4,7},{5,6},{6,5},{7,4},{8,11},{9,10},{10,... | collective-permute-start | bytes 24584 | tf_op jit(solution)/shard_map/ppermute | solution.py:543
  59.6 0.0 copy-done.9
  59.6 0.0 copy-done.10
  59.6 0.0 copy-done.3
  59.6 0.0 copy-done.7
  59.6 1.4 %critic_scores.1 = (f32[8,32,1024]{2,1,0:T(8,128)S(1)}, f32[8,32,128]{2,1,0:T(8,128)S(1)}) custom-call(s32[4]{0:T(128)S(1)} %copy-done.7, bf16[16,2048]{1,0:T(8,128)(2,1)S(1)} %collective-permute-done.3.rows_ref, f32[1,2048]{1,0:T(1,128)S(1)} %bitcast.14, bf16[4,1024,256]{2,1,0:T(8,128)(2,1)S(1)} %copy-done.3), custom_call_target="tpu_custom_call" | custom-call | flops 67108864 | bytes 3145728 | tf_op jit(solution)/shard_map/critic_scores/pallas_call | solution.py:439
  61.1 0.0 collective-permute-done.4.one_ref
  61.1 0.0 collective-permute-done.5.two_ref
  61.1 0.7 %collective-permute-done.6.three_ref = f32[16,128]{1,0:T(8,128)S(1)} collective-permute-done((f32[16,128]{1,0:T(8,128)S(1)}, f32[16,128]{1,0:T(8,128)S(1)}, u32[]{:S(2)}, u32[]{:S(2)}) %collective-permute-start.6) | collective-permute-done | bytes 8224 | tf_op jit(solution)/shard_map/ppermute | solution.py:543
  61.8 0.0 copy-done.1
  61.8 0.0 copy-done.4
  61.8 0.7 %critic.1.own_ref = f32[16,128]{1,0:T(8,128)S(1)} custom-call(f32[16,128]{1,0:T(8,128)S(1)} %row_squares.1.own_ref, f32[16,128]{1,0:T(8,128)S(1)} %collective-permute-done.4.one_ref, f32[16,128]{1,0:T(8,128)S(1)} %collective-permute-done.5.two_ref, f32[16,128]{1,0:T(8,128)S(1)} %collective-permute-done.6.three_ref, ...), custom_call_target="tpu_custom_call" | custom-call | flops 67108864 | bytes 3145728 | tf_op jit(solution)/shard_map/critic/pallas_call | solution.py:502
  62.5 0.4 collective-permute-start.7
  62.9 0.7 collective-permute-start.8
  63.5 1.1 %collective-permute-start.9 = (f32[16,128]{1,0:T(8,128)S(1)}, f32[16,128]{1,0:T(8,128)S(1)}, u32[]{:S(2)}, u32[]{:S(2)}) collective-permute-start(f32[16,128]{1,0:T(8,128)S(1)} %critic.1.own_ref), channel_id=1, source_target_pairs={{0,3},{1,2},{2,1},{3,0},{4,7},{5,6},{6,5},{7,4},{8,11},{9,10},{10,... | collective-permute-start | bytes 24584 | tf_op jit(solution)/shard_map/ppermute | solution.py:543
  64.7 0.7 by_step.1
  65.3 0.0 collective-permute-done.7.one_ref
  65.3 0.0 collective-permute-done.8.two_ref
  65.4 1.3 %collective-permute-done.9.three_ref = f32[16,128]{1,0:T(8,128)S(1)} collective-permute-done((f32[16,128]{1,0:T(8,128)S(1)}, f32[16,128]{1,0:T(8,128)S(1)}, u32[]{:S(2)}, u32[]{:S(2)}) %collective-permute-start.9) | collective-permute-done | bytes 8224 | tf_op jit(solution)/shard_map/ppermute | solution.py:543
  66.6 0.8 %expect.1 = f32[4,4]{1,0:T(4,128)} custom-call(f32[16,128]{1,0:T(8,128)S(1)} %critic.1.own_ref, f32[16,128]{1,0:T(8,128)S(1)} %collective-permute-done.7.one_ref, f32[16,128]{1,0:T(8,128)S(1)} %collective-permute-done.8.two_ref, f32[16,128]{1,0:T(8,128)S(1)} %collective-permute-done.9.three_ref), custom_call_target="tpu_custom_call" | custom-call | tf_op jit(solution)/shard_map/expect/pallas_call | solution.py:538
  (3 shorter events, 0.0 us)
Async XLA Ops:
  0.6 0.7 %copy-start.5 = (s32[4,4]{1,0:T(4,128)S(1)}, s32[4,4]{1,0:T(4,128)}, u32[]{:S(2)}) copy-start(s32[4,4]{1,0:T(4,128)} %token_ref.1) | copy-start | bytes 196
  27.3 12.8 %all-to-all-start.1 = ((bf16[32,8,128]{2,1,0:T(8,128)(2,1)}), bf16[32,8,128]{2,1,0:T(8,128)(2,1)S(1)}, u32[]{:S(2)}, u32[]{:S(2)}) async-start(bf16[32,8,128]{2,1,0:T(8,128)(2,1)} %bitcast.3), calls=%async_computation.1 | async-start | bytes 131072 | tf_op jit(solution)/shard_map/all_to_all | solution.py:580
  31.2 1.9 %copy-start.8 = (bf16[2048]{0:T(1024)(128)(2,1)S(1)}, bf16[2048]{0:T(1024)(128)(2,1)}, u32[]{:S(2)}) copy-start(bf16[2048]{0:T(1024)(128)(2,1)} %param.17) | copy-start | bytes 12292
  40.1 8.0 %copy-start.2 = (bf16[4,1024,256]{2,1,0:T(8,128)(2,1)S(1)}, bf16[4,1024,256]{2,1,0:T(8,128)(2,1)}, u32[]{:S(2)}) copy-start(bf16[4,1024,256]{2,1,0:T(8,128)(2,1)} %keys_ref.2) | copy-start | bytes 6291460
  40.1 8.0 %copy-start.6 = (s32[4]{0:T(128)S(1)}, s32[4]{0:T(128)}, u32[]{:S(2)}) copy-start(s32[4]{0:T(128)} %length_ref.2) | copy-start | bytes 52
  43.1 7.6 %copy-start = (bf16[4,1024,256]{2,1,0:T(8,128)(2,1)S(1)}, bf16[4,1024,256]{2,1,0:T(8,128)(2,1)}, u32[]{:S(2)}) copy-start(bf16[4,1024,256]{2,1,0:T(8,128)(2,1)} %values_ref.2) | copy-start | bytes 6291460
  43.1 16.5 %copy-start.9 = (bf16[2048]{0:T(1024)(128)(2,1)S(1)}, bf16[2048]{0:T(1024)(128)(2,1)}, u32[]{:S(2)}) copy-start(bf16[2048]{0:T(1024)(128)(2,1)} %param.23) | copy-start | bytes 12292
  43.1 16.5 %copy-start.10 = (bf16[2048]{0:T(1024)(128)(2,1)S(1)}, bf16[2048]{0:T(1024)(128)(2,1)}, u32[]{:S(2)}) copy-start(bf16[2048]{0:T(1024)(128)(2,1)} %param.26) | copy-start | bytes 12292
  43.1 16.5 %copy-start.3 = (bf16[4,1024,256]{2,1,0:T(8,128)(2,1)S(1)}, bf16[4,1024,256]{2,1,0:T(8,128)(2,1)}, u32[]{:S(2)}) copy-start(bf16[4,1024,256]{2,1,0:T(8,128)(2,1)} %keys_ref.3) | copy-start | bytes 6291460
  43.1 16.5 %copy-start.7 = (s32[4]{0:T(128)S(1)}, s32[4]{0:T(128)}, u32[]{:S(2)}) copy-start(s32[4]{0:T(128)} %length_ref.3) | copy-start | bytes 52
  43.1 6.4 %collective-permute-start = (f32[16,640]{1,0:T(8,128)S(1)}, f32[16,640]{1,0:T(8,128)S(1)}, u32[]{:S(2)}, u32[]{:S(2)}) collective-permute-start(f32[16,640]{1,0:T(8,128)S(1)} %get-tuple-element.13), channel_id=1, source_target_pairs={{0,1},{1,0},{2,3},{3,2},{4,5},{5,4},{6,7},{7,6},{8,9},{9,8},{10,11... | collective-permute-start | bytes 122888 | tf_op jit(solution)/shard_map/ppermute | solution.py:543
  46.4 3.2 %collective-permute-start.1 = (f32[16,640]{1,0:T(8,128)S(1)}, f32[16,640]{1,0:T(8,128)S(1)}, u32[]{:S(2)}, u32[]{:S(2)}) collective-permute-start(f32[16,640]{1,0:T(8,128)S(1)} %get-tuple-element.14), channel_id=1, source_target_pairs={{0,2},{1,3},{2,0},{3,1},{4,6},{5,7},{6,4},{7,5},{8,10},{9,11},{10,... | collective-permute-start | bytes 122888 | tf_op jit(solution)/shard_map/ppermute | solution.py:543
  46.7 4.0 %collective-permute-start.2 = (f32[16,640]{1,0:T(8,128)S(1)}, f32[16,640]{1,0:T(8,128)S(1)}, u32[]{:S(2)}, u32[]{:S(2)}) collective-permute-start(f32[16,640]{1,0:T(8,128)S(1)} %get-tuple-element.15), channel_id=1, source_target_pairs={{0,3},{1,2},{2,1},{3,0},{4,7},{5,6},{6,5},{7,4},{8,11},{9,10},{10,... | collective-permute-start | bytes 122888 | tf_op jit(solution)/shard_map/ppermute | solution.py:543
  49.6 12.2 %copy-start.1 = (bf16[4,1024,256]{2,1,0:T(8,128)(2,1)S(1)}, bf16[4,1024,256]{2,1,0:T(8,128)(2,1)}, u32[]{:S(2)}) copy-start(bf16[4,1024,256]{2,1,0:T(8,128)(2,1)} %values_ref.3) | copy-start | bytes 6291460
  49.6 12.2 %copy-start.4 = (bf16[2048,51]{0,1:T(8,128)(2,1)S(1)}, bf16[2048,51]{0,1:T(8,128)(2,1)}, u32[]{:S(2)}) copy-start(bf16[2048,51]{0,1:T(8,128)(2,1)} %param.27) | copy-start | bytes 626692
  51.6 4.7 %collective-permute-start.3 = (bf16[16,2048]{1,0:T(8,128)(2,1)S(1)}, bf16[16,2048]{1,0:T(8,128)(2,1)S(1)}, u32[]{:S(2)}, u32[]{:S(2)}) collective-permute-start(bf16[16,2048]{1,0:T(8,128)(2,1)S(1)} %policy.1.rows_ref), channel_id=1, source_target_pairs={{0,64},{4,68},{8,72},{12,76},{16,80},{20,84},{24,88},{28,92},{32,9... | collective-permute-start | bytes 196616 | tf_op jit(solution)/shard_map/ppermute | solution.py:548
  56.4 4.6 %collective-permute-start.4 = (f32[16,128]{1,0:T(8,128)S(1)}, f32[16,128]{1,0:T(8,128)S(1)}, u32[]{:S(2)}, u32[]{:S(2)}) collective-permute-start(f32[16,128]{1,0:T(8,128)S(1)} %row_squares.1.own_ref), channel_id=1, source_target_pairs={{0,1},{1,0},{2,3},{3,2},{4,5},{5,4},{6,7},{7,6},{8,9},{9,8},{10,11... | collective-permute-start | bytes 24584 | tf_op jit(solution)/shard_map/ppermute | solution.py:543
  57.9 3.2 %collective-permute-start.5 = (f32[16,128]{1,0:T(8,128)S(1)}, f32[16,128]{1,0:T(8,128)S(1)}, u32[]{:S(2)}, u32[]{:S(2)}) collective-permute-start(f32[16,128]{1,0:T(8,128)S(1)} %row_squares.1.own_ref), channel_id=1, source_target_pairs={{0,2},{1,3},{2,0},{3,1},{4,6},{5,7},{6,4},{7,5},{8,10},{9,11},{10,... | collective-permute-start | bytes 24584 | tf_op jit(solution)/shard_map/ppermute | solution.py:543
  58.7 3.1 %collective-permute-start.6 = (f32[16,128]{1,0:T(8,128)S(1)}, f32[16,128]{1,0:T(8,128)S(1)}, u32[]{:S(2)}, u32[]{:S(2)}) collective-permute-start(f32[16,128]{1,0:T(8,128)S(1)} %row_squares.1.own_ref), channel_id=1, source_target_pairs={{0,3},{1,2},{2,1},{3,0},{4,7},{5,6},{6,5},{7,4},{8,11},{9,10},{10,... | collective-permute-start | bytes 24584 | tf_op jit(solution)/shard_map/ppermute | solution.py:543
  62.5 2.9 %collective-permute-start.7 = (f32[16,128]{1,0:T(8,128)S(1)}, f32[16,128]{1,0:T(8,128)S(1)}, u32[]{:S(2)}, u32[]{:S(2)}) collective-permute-start(f32[16,128]{1,0:T(8,128)S(1)} %critic.1.own_ref), channel_id=1, source_target_pairs={{0,1},{1,0},{2,3},{3,2},{4,5},{5,4},{6,7},{7,6},{8,9},{9,8},{10,11... | collective-permute-start | bytes 24584 | tf_op jit(solution)/shard_map/ppermute | solution.py:543
  62.9 2.5 %collective-permute-start.8 = (f32[16,128]{1,0:T(8,128)S(1)}, f32[16,128]{1,0:T(8,128)S(1)}, u32[]{:S(2)}, u32[]{:S(2)}) collective-permute-start(f32[16,128]{1,0:T(8,128)S(1)} %critic.1.own_ref), channel_id=1, source_target_pairs={{0,2},{1,3},{2,0},{3,1},{4,6},{5,7},{6,4},{7,5},{8,10},{9,11},{10,... | collective-permute-start | bytes 24584 | tf_op jit(solution)/shard_map/ppermute | solution.py:543
  63.5 3.1 %collective-permute-start.9 = (f32[16,128]{1,0:T(8,128)S(1)}, f32[16,128]{1,0:T(8,128)S(1)}, u32[]{:S(2)}, u32[]{:S(2)}) collective-permute-start(f32[16,128]{1,0:T(8,128)S(1)} %critic.1.own_ref), channel_id=1, source_target_pairs={{0,3},{1,2},{2,1},{3,0},{4,7},{5,6},{6,5},{7,4},{8,11},{9,10},{10,... | collective-permute-start | bytes 24584 | tf_op jit(solution)/shard_map/ppermute | solution.py:543

commit v5 on v4

--- a/solution.py
+++ b/solution.py
@@ -33,7 +33,7 @@
         body,
         out_shape=outs,
         in_specs=specs,
-        out_specs=jax.tree.map(lambda _: VMEM, outs),
+        out_specs=tuple(VMEM for _ in outs) if isinstance(outs, tuple) else VMEM,
         scratch_shapes=scratch,
         compiler_params=pltpu.CompilerParams(vmem_limit_bytes=limit * MIB),
         cost_estimate=pl.CostEstimate(flops=flops, bytes_accessed=moved, transcendentals=0),
@@ -59,7 +59,9 @@
     return kernel_call(lay_out_kernel, out, [VMEM], name="lay_out")(tokens)
 
 
-def pick_rows_kernel(token_ref, table_ref, out_ref, tiles_ref, sems):
+def pick_rows_kernel(
+    token_ref, table_ref, weight_ref, out_ref, early_ref, tiles_ref, sems, early_sem
+):
     width = table_ref.shape[0]
     pieces = sems.shape[0]
     destinations = token_ref.shape[0] // pieces
@@ -86,6 +88,10 @@
 
         lax.fori_loop(0, destinations, fetch, 0)
 
+    early = pltpu.make_async_copy(
+        weight_ref.at[pl.ds(0, early_ref.shape[0])], early_ref, early_sem
+    )
+    early.start()
     empty = jnp.zeros((width, LANES), jnp.float32)
     pair = (empty, empty)
     for piece in range(pieces):
@@ -111,62 +117,35 @@
             rows = pl.ds((piece + 1) * places - LANES, LANES)
             out_ref[rows, :] = both.T.astype(out_ref.dtype)
             pair = (empty, empty)
-
-
-def pick_rows(tokens, table, pieces=8):
+    early.wait()
+
+
+def pick_rows(tokens, table, weight, pieces=8):
     width = table.shape[0]
     rows = tokens.size * width // LANES
+    early = (weight.shape[0] * 3 // 4, weight.shape[1])
     return kernel_call(
         pick_rows_kernel,
-        array((rows, LANES), table.dtype),
-        [SMEM, HBM],
+        (array((rows, LANES), table.dtype), pltpu.VMEM(early, weight.dtype)),
+        [SMEM, HBM, HBM],
         scratch=[
             pltpu.VMEM((2, rows, width, LANES), table.dtype),
             pltpu.SemaphoreType.DMA((pieces,)),
+            pltpu.SemaphoreType.DMA,
         ],
         limit=24,
         name="pick_rows",
-    )(tokens, in_hbm(table))
-
-
-def stage_kernel(source_ref, target_ref, sems):
-    pieces = sems.shape[0]
-    rows = target_ref.shape[0] // pieces
-    copies = []
-    for piece in range(pieces):
-        part = pl.ds(piece * rows, rows)
-        copies.append(
-            pltpu.make_async_copy(source_ref.at[part], target_ref.at[part], sems.at[piece])
-        )
-    for copy in copies:
-        copy.start()
-    for copy in copies:
-        copy.wait()
-
-
-def staged(source, rows, pieces=4):
-    shape = (rows, source.shape[1])
-    return pl.pallas_call(
-        stage_kernel,
-        out_shape=pltpu.VMEM(shape, source.dtype),
-        in_specs=[HBM],
-        out_specs=VMEM,
-        scratch_shapes=[pltpu.SemaphoreType.DMA((pieces,))],
-        compiler_params=pltpu.CompilerParams(vmem_limit_bytes=MIB),
-        cost_estimate=pl.CostEstimate(
-            flops=0, bytes_accessed=4 * rows * shape[1], transcendentals=0
-        ),
-        name="stage_weights",
-    )(in_hbm(source))
+    )(tokens, in_hbm(table), in_hbm(weight))
 
 
 def project_kernel(
-    tp_ref, blocks_ref, gain_ref, early_ref, key_ref, value_ref, x_ref, query_ref, *rest
+    blocks_ref, gain_ref, early_ref, key_ref, value_ref, x_ref, query_ref, *rest
 ):
     parts = rest[:4]
     gained_ref, placed_ref, sums_ref, late_ref, keys_ref, sems = rest[4:]
     count, width = x_ref.shape
     kv_width = key_ref.shape[1] // 4
+    tp = lax.axis_index("tp")
     early = early_ref.shape[0]
     chunk = width - early
     copies = [pltpu.make_async_copy(value_ref.at[pl.ds(early, chunk)], late_ref, sems.at[0])]
@@ -188,7 +167,7 @@
         squares += x * x
         columns = pl.ds(k * LANES, LANES)
         x_ref[:, columns] = x.astype(x_ref.dtype)
-        gained = x * gain_ref[:, columns]
+        gained = x * gain_ref[k : k + 1, :].astype(jnp.float32)
         gained_ref[:, columns] = gained.astype(gained_ref.dtype)
         head, group = divmod(k, GROUP)
         for row in range(4):
@@ -210,24 +189,24 @@
         keys = partial if keys is None else keys + partial
     sums_ref[0] = keys
     for by, part_ref in enumerate(parts):
-        start = pl.multiple_of(jnp.bitwise_xor(tp_ref[0], by) * kv_width, kv_width)
+        start = pl.multiple_of(jnp.bitwise_xor(tp, by) * kv_width, kv_width)
         peer = pl.ds(start, kv_width)
         part_ref[:, :kv_width] = sums_ref[0, :, peer]
         part_ref[:, kv_width : 2 * kv_width] = sums_ref[1, :, peer]
         part_ref[:, 2 * kv_width :] = total
 
 
-def project(tp, blocks, gain, key_weight, value_weight):
+def project(blocks, gain, early_values, key_weight, value_weight):
     width, kv_all = key_weight.shape
     count = blocks.shape[0] * LANES // width
-    early = width * 3 // 4
+    early = early_values.shape[0]
     part = array((count, kv_all // 2 + LANES), jnp.float32)
     heads = width // (GROUP * HEAD_DIM)
     queries = (4 * heads, 4 * GROUP, HEAD_DIM)
     x, query, *parts = kernel_call(
         project_kernel,
         (array((count, width), jnp.bfloat16), array(queries, jnp.bfloat16)) + (part,) * 4,
-        [SMEM] + [VMEM] * 3 + [HBM] * 2,
+        [VMEM] * 3 + [HBM] * 2,
         scratch=[
             pltpu.VMEM((count, width), jnp.bfloat16),
             pltpu.VMEM(queries, jnp.float32),
@@ -240,10 +219,9 @@
         moved=4 * width * kv_all,
         name="project",
     )(
-        tp,
         blocks,
         gain,
-        staged(value_weight, early),
+        early_values,
         in_hbm(key_weight),
         in_hbm(value_weight),
     )
@@ -421,7 +399,7 @@
 ):
     for k in range(rows_ref.shape[1] // LANES):
         columns = pl.ds(k * LANES, LANES)
-        gained = rows_ref[:, columns].astype(jnp.float32) * gain_ref[:, columns]
+        gained = rows_ref[:, columns].astype(jnp.float32) * gain_ref[k : k + 1, :].astype(jnp.float32)
         head, group = divmod(k, GROUP)
         for row in range(4):
             placed_ref[4 * head + row, pl.ds(4 * group, 4), :] = gained[4 * row : 4 * row + 4]
@@ -489,7 +467,9 @@
         columns = pl.ds(k * LANES, LANES)
         combined = rows_ref[:, columns].astype(jnp.float32) + attended_ref[k]
         squares += combined * combined
-        scaled_ref[:, columns] = (combined * gain_ref[:, columns]).astype(scaled_ref.dtype)
+        scaled_ref[:, columns] = (combined * gain_ref[k : k + 1, :].astype(jnp.float32)).astype(
+            scaled_ref.dtype
+        )
     logits = lax.dot_general(
         scaled_ref[...], head_ref[...], NT, preferred_element_type=jnp.float32
     )
@@ -569,17 +549,16 @@
     value_head,
 ):
     row_groups = lax.axis_size("rows")
-    tp = lax.axis_index("tp").astype(jnp.int32).reshape(1)
-
-    def as_row(gain):
-        return gain.astype(jnp.float32).reshape(1, -1)
+
+    def as_rows(gain):
+        return gain.reshape(-1, LANES)
 
     table = embedding.transpose(1, 2, 0).reshape(embedding.shape[2], embedding.shape[0])
     all_tokens = lax.all_to_all(laid_out(tokens, row_groups), "rows", 0, 0)
-    picked = pick_rows(all_tokens, table)
+    picked, early_values = pick_rows(all_tokens, table, value_weight)
     blocks = lax.all_to_all(picked.reshape(row_groups, -1, LANES), "rows", 0, 0)
     x, query, parts = project(
-        tp, blocks.reshape(picked.shape), as_row(attn_gain), key_weight, value_weight
+        blocks.reshape(picked.shape), as_rows(attn_gain), early_values, key_weight, value_weight
     )
     arrived = parts[:1] + [swapped(parts[by], by) for by in (1, 2, 3)]
     raw, top = policy_scores(lengths, query, policy_keys)
@@ -587,13 +566,13 @@
     rows = passed_along(passed, "rows", row_groups // 2)
     hidden = by_step(passed)
 
-    raw, top = critic_scores(critic_lengths, rows, as_row(critic_gain), critic_keys)
+    raw, top = critic_scores(critic_lengths, rows, as_rows(critic_gain), critic_keys)
     logits = critic(
         with_peers(row_squares(rows)),
         raw,
         top,
         rows,
-        as_row(value_gain),
+        as_rows(value_gain),
         critic_values,
         value_head.T,
     )

time: 67.7 us -> 65.8 us (0.972)
  blocking collectives: 19.8 us -> 31.7 us
  waiting for transfers between devices: 13.7 us -> 6.11 us
  starting transfers between devices: 15.3 us -> 11.3 us
  Pallas kernels: 17.2 us -> 15 us
    all_to_all x0 -> x1, blocking collectives: none -> 11.9 us  [on_device(): blocks = lax.all_to_all(picked.reshape(row_groups, -1, LANES), 'rows', 0, 0)]
    all_to_all x1 -> x0, waiting for transfers between devices: 6.98 us -> none  [on_device(): blocks = lax.all_to_all(picked.reshape(row_groups, -1, LANES), 'rows', 0, 0)]
    all_to_all x1 -> x0, starting transfers between devices: 3.87 us -> none  [on_device(): blocks = lax.all_to_all(picked.reshape(row_groups, -1, LANES), 'rows', 0, 0)]
    pallas_call x2 -> x1, Pallas kernels: 8.01 us -> 5.78 us  [pick_rows(): kernel_call(pick_rows_kernel, (array((rows, LANES), table.dtype), pltpu.V...]
  transfers between devices with their start and end apart: 11 -> 10, of which waited for: 5 -> 5; matrix products, arithmetic and copies ran while one was open for 0% -> 0% of each run, Pallas kernels for 8% -> 5%
where the time goes in v5:
time: 65.8 us; the launch traced here: 65.6 us
  blocking collectives  31.7 us (48%)
  Pallas kernels  15 us (23%)
  starting transfers between devices  11.3 us (17%)
  waiting for transfers between devices  6.11 us (9%)
  between operations  0.76 us (1%)
  local copies, waits for them, and re-layouts  0.72 us (1%)
    all_to_all x1, blocking collectives, on_device(): all_tokens = lax.all_to_all(laid_out(tokens, row_groups), 'rows', 0, 0)  19.8 us
    all_to_all x1, blocking collectives, on_device(): blocks = lax.all_to_all(picked.reshape(row_groups, -1, LANES), 'rows', 0, 0)  11.9 us
    ppermute x9, starting transfers between devices, swapped(): return lax.ppermute(shard, 'tp', [(i, i ^ by) for i in range(peers)])  10.3 us
    pallas_call x1, Pallas kernels, pick_rows(): kernel_call(pick_rows_kernel, (array((rows, LANES), table.dtype), pltpu.V...  5.78 us
    ppermute x1, waiting for transfers between devices, passed_along(): lax.ppermute(shard, axis, [(i, (i + by) % peers) for i in range(peers)])  3.63 us
    pallas_call x1, Pallas kernels, project(): kernel_call(project_kernel, (array((count, width), jnp.bfloat16), array(q...  2.94 us
    ppermute x9, waiting for transfers between devices, swapped(): return lax.ppermute(shard, 'tp', [(i, i ^ by) for i in range(peers)])  2.48 us
    pallas_call x1, Pallas kernels, critic_scores(): kernel_call(critic_scores_kernel, (raw, array(placed, jnp.float32)), [SME...  1.45 us
  transfers between devices with their start and end apart: 10, of which 5 were waited for; matrix products, arithmetic and copies ran while one was open for 0% of the time, Pallas kernels for 5%

profile of v5, /device:TPU:1, one launch (start us, length us, event | category | flops | bytes accessed | tf_op | source)
XLA Modules:
  0.0 65.6 jit_solution(17799280972856924933)
XLA Ops:
  0.6 0.0 copy-start.8
  0.6 0.7 %copy-done.8 = s32[4,4]{1,0:T(4,128)S(1)} copy-done((s32[4,4]{1,0:T(4,128)S(1)}, s32[4,4]{1,0:T(4,128)}, u32[]{:S(2)}) %copy-start.8) | copy-done | bytes 88
  1.3 0.1 lay_out.1
  1.4 19.8 %all_to_all.10.token_ref = s32[32,1,16]{2,1,0:T(1,128)S(1)} all-to-all(s32[32,1,16]{2,1,0:T(1,128)S(1)} %lay_out.1), channel_id=1, replica_groups=mesh['rows'=32,'tp'=4] {'rows'}, dimensions={0} | all-to-all | bytes 4096 | tf_op jit(solution)/shard_map/all_to_all | solution.py:557
  21.2 0.0 copy-start.5
  21.2 5.8 %pick_rows.1 = (bf16[256,128]{1,0:T(8,128)(2,1)S(1)}, bf16[1536,1024]{1,0:T(8,128)(2,1)S(1)}) custom-call(s32[32,1,16]{2,1,0:T(1,128)S(1)} %all_to_all.10.token_ref, bf16[64,76032]{1,0:T(8,128)(2,1)} %bitcast.15, bf16[2048,1024]{1,0:T(8,128)(2,1)} %value_ref.1), custom_call_target="tpu_custom_call" | custom-call | tf_op jit(solution)/shard_map/pick_rows/pallas_call | solution.py:127
  27.0 11.9 %all_to_all.11 = bf16[32,8,128]{2,1,0:T(8,128)(2,1)S(1)} all-to-all(bf16[32,8,128]{2,1,0:T(8,128)(2,1)S(1)} %bitcast.11), channel_id=1, replica_groups=mesh['rows'=32,'tp'=4] {'rows'}, dimensions={0} | all-to-all | bytes 131072 | tf_op jit(solution)/shard_map/all_to_all | solution.py:559
  38.9 0.0 copy-done.5
  38.9 0.0 copy-start.1
  38.9 0.0 copy-start.9
  38.9 2.9 %project.1 = (bf16[16,2048]{1,0:T(8,128)(2,1)S(1)}, bf16[8,32,128]{2,1,0:T(8,128)(2,1)S(1)}, f32[16,640]{1,0:T(8,128)S(1)}, f32[16,640]{1,0:T(8,128)S(1)}, f32[16,640]{1,0:T(8,128)S(1)}, /*index=5*/f32[16,640]{1,0:T(8,128)S(1)}) custom-call(bf16[256,128]{1,0:T(8,128)(2,1)S(1)} %bitcast.9, bf16[16,128]{1,0:T(8,128)(2,1)S(1)} %bitcast.12, ...), custom_call_target="tpu_custom_call" | custom-call | flops 134217728 | bytes 8388608 | tf_op jit(solution)/shard_map/project/pallas_call | solution.py:206
  41.8 0.0 copy-start
  41.8 0.0 copy-start.2
  41.9 0.0 copy-start.6
  41.9 0.0 copy-start.10
  41.9 3.6 %collective-permute-start = (f32[16,640]{1,0:T(8,128)S(1)}, f32[16,640]{1,0:T(8,128)S(1)}, u32[]{:S(2)}, u32[]{:S(2)}) collective-permute-start(f32[16,640]{1,0:T(8,128)S(1)} %get-tuple-element.17), channel_id=1, source_target_pairs={{0,1},{1,0},{2,3},{3,2},{4,5},{5,4},{6,7},{7,6},{8,9},{9,8},{10,11... | collective-permute-start | bytes 122888 | tf_op jit(solution)/shard_map/ppermute | solution.py:523
  45.5 0.3 collective-permute-start.1
  45.8 1.4 %collective-permute-start.2 = (f32[16,640]{1,0:T(8,128)S(1)}, f32[16,640]{1,0:T(8,128)S(1)}, u32[]{:S(2)}, u32[]{:S(2)}) collective-permute-start(f32[16,640]{1,0:T(8,128)S(1)} %get-tuple-element.19), channel_id=1, source_target_pairs={{0,3},{1,2},{2,1},{3,0},{4,7},{5,6},{6,5},{7,4},{8,11},{9,10},{10,... | collective-permute-start | bytes 122888 | tf_op jit(solution)/shard_map/ppermute | solution.py:523
  47.2 0.0 copy-done.1
  47.2 0.0 copy-done.9
  47.2 1.4 %policy_scores.1 = (f32[8,32,1024]{2,1,0:T(8,128)S(1)}, f32[8,32,128]{2,1,0:T(8,128)S(1)}) custom-call(s32[4]{0:T(128)S(1)} %copy-done.9, bf16[8,32,128]{2,1,0:T(8,128)(2,1)S(1)} %get-tuple-element.20.query_ref, bf16[4,1024,256]{2,1,0:T(8,128)(2,1)S(1)} %copy-done.1), custom_call_target="tpu_custom_call" | custom-call | flops 67108864 | bytes 3145728 | tf_op jit(solution)/shard_map/policy_scores/pallas_call | solution.py:248
  48.6 0.0 copy-start.3
  48.6 0.0 copy-start.4
  48.6 0.0 copy-start.7
  48.6 0.0 collective-permute-done.one_ref
  48.7 0.0 collective-permute-done.1.two_ref
  48.7 1.1 %collective-permute-done.2.three_ref = f32[16,640]{1,0:T(8,128)S(1)} collective-permute-done((f32[16,640]{1,0:T(8,128)S(1)}, f32[16,640]{1,0:T(8,128)S(1)}, u32[]{:S(2)}, u32[]{:S(2)}) %collective-permute-start.2) | collective-permute-done | bytes 40992 | tf_op jit(solution)/shard_map/ppermute | solution.py:523
  49.7 0.0 copy-done
  49.7 1.0 %policy.1.rows_ref = bf16[16,2048]{1,0:T(8,128)(2,1)S(1)} custom-call(f32[16,640]{1,0:T(8,128)S(1)} %get-tuple-element.16.own_ref, f32[16,640]{1,0:T(8,128)S(1)} %collective-permute-done.one_ref, f32[16,640]{1,0:T(8,128)S(1)} %collective-permute-done.1.two_ref, f32[16,640]{1,0:T(8,128)S(1)} %collective-permute-done.2.three_ref, ...), custom_call_target="tpu_custom_call" | custom-call | flops 67108864 | bytes 3145728 | tf_op jit(solution)/shard_map/policy/pallas_call | solution.py:347
  50.7 1.1 %collective-permute-start.3 = (bf16[16,2048]{1,0:T(8,128)(2,1)S(1)}, bf16[16,2048]{1,0:T(8,128)(2,1)S(1)}, u32[]{:S(2)}, u32[]{:S(2)}) collective-permute-start(bf16[16,2048]{1,0:T(8,128)(2,1)S(1)} %policy.1.rows_ref), channel_id=1, source_target_pairs={{0,64},{4,68},{8,72},{12,76},{16,80},{20,84},{24,88},{28,92},{32,9... | collective-permute-start | bytes 196616 | tf_op jit(solution)/shard_map/ppermute | solution.py:528
  51.8 3.6 %collective-permute-done.3.rows_ref = bf16[16,2048]{1,0:T(8,128)(2,1)S(1)} collective-permute-done((bf16[16,2048]{1,0:T(8,128)(2,1)S(1)}, bf16[16,2048]{1,0:T(8,128)(2,1)S(1)}, u32[]{:S(2)}, u32[]{:S(2)}) %collective-permute-start.3) | collective-permute-done | bytes 65568 | tf_op jit(solution)/shard_map/ppermute | solution.py:528
  55.4 0.1 row_squares.1.own_ref
  55.5 2.1 %collective-permute-start.6 = (f32[16,128]{1,0:T(8,128)S(1)}, f32[16,128]{1,0:T(8,128)S(1)}, u32[]{:S(2)}, u32[]{:S(2)}) collective-permute-start(f32[16,128]{1,0:T(8,128)S(1)} %row_squares.1.own_ref), channel_id=1, source_target_pairs={{0,3},{1,2},{2,1},{3,0},{4,7},{5,6},{6,5},{7,4},{8,11},{9,10},{10,... | collective-permute-start | bytes 24584 | tf_op jit(solution)/shard_map/ppermute | solution.py:523
  57.6 0.7 collective-permute-start.5
  58.3 0.0 collective-permute-start.4
  58.3 0.0 copy-done.2
  58.3 0.0 copy-done.6
  58.3 0.0 copy-done.10
  58.3 1.4 %critic_scores.1 = (f32[8,32,1024]{2,1,0:T(8,128)S(1)}, f32[8,32,128]{2,1,0:T(8,128)S(1)}) custom-call(s32[4]{0:T(128)S(1)} %copy-done.10, bf16[16,2048]{1,0:T(8,128)(2,1)S(1)} %collective-permute-done.3.rows_ref, bf16[16,128]{1,0:T(8,128)(2,1)S(1)} %bitcast.13, bf16[4,1024,256]{2,1,0:T(8,128)(2,1)S(1)} %copy-done.2), custom_call_target="tpu_custom_call" | custom-call | flops 67108864 | bytes 3145728 | tf_op jit(solution)/shard_map/critic_scores/pallas_call | solution.py:417
  59.8 0.0 collective-permute-done.6.three_ref
  59.8 0.5 collective-permute-done.5.two_ref
  60.3 0.0 collective-permute-done.4.one_ref
  60.3 0.0 copy-done.3
  60.3 0.0 copy-done.4
  60.3 0.0 copy-done.7
  60.3 0.7 %critic.1.own_ref = f32[16,128]{1,0:T(8,128)S(1)} custom-call(f32[16,128]{1,0:T(8,128)S(1)} %row_squares.1.own_ref, f32[16,128]{1,0:T(8,128)S(1)} %collective-permute-done.4.one_ref, f32[16,128]{1,0:T(8,128)S(1)} %collective-permute-done.5.two_ref, f32[16,128]{1,0:T(8,128)S(1)} %collective-permute-done.6.three_ref, ...), custom_call_target="tpu_custom_call" | custom-call | flops 67108864 | bytes 3145728 | tf_op jit(solution)/shard_map/critic/pallas_call | solution.py:482
  61.0 1.2 %collective-permute-start.9 = (f32[16,128]{1,0:T(8,128)S(1)}, f32[16,128]{1,0:T(8,128)S(1)}, u32[]{:S(2)}, u32[]{:S(2)}) collective-permute-start(f32[16,128]{1,0:T(8,128)S(1)} %critic.1.own_ref), channel_id=1, source_target_pairs={{0,3},{1,2},{2,1},{3,0},{4,7},{5,6},{6,5},{7,4},{8,11},{9,10},{10,... | collective-permute-start | bytes 24584 | tf_op jit(solution)/shard_map/ppermute | solution.py:523
  62.2 0.6 collective-permute-start.8
  62.8 0.4 collective-permute-start.7
  63.2 0.7 %by_step.1 = bf16[4,4,2048]{2,1,0:T(4,128)(2,1)} custom-call(bf16[16,2048]{1,0:T(8,128)(2,1)S(1)} %policy.1.rows_ref), custom_call_target="tpu_custom_call" | custom-call | bytes 524288 | tf_op jit(solution)/shard_map/by_step/pallas_call | solution.py:373
  63.9 0.3 collective-permute-done.9.three_ref
  64.1 0.6 collective-permute-done.8.two_ref
  64.7 0.0 collective-permute-done.7.one_ref
  64.7 0.8 %expect.1 = f32[4,4]{1,0:T(4,128)} custom-call(f32[16,128]{1,0:T(8,128)S(1)} %critic.1.own_ref, f32[16,128]{1,0:T(8,128)S(1)} %collective-permute-done.7.one_ref, f32[16,128]{1,0:T(8,128)S(1)} %collective-permute-done.8.two_ref, f32[16,128]{1,0:T(8,128)S(1)} %collective-permute-done.9.three_ref), custom_call_target="tpu_custom_call" | custom-call | tf_op jit(solution)/shard_map/expect/pallas_call | solution.py:518
Async XLA Ops:
  0.6 0.7 %copy-start.8 = (s32[4,4]{1,0:T(4,128)S(1)}, s32[4,4]{1,0:T(4,128)}, u32[]{:S(2)}) copy-start(s32[4,4]{1,0:T(4,128)} %token_ref.1) | copy-start | bytes 196
  21.2 17.7 %copy-start.5 = (bf16[2048]{0:T(1024)(128)(2,1)S(1)}, bf16[2048]{0:T(1024)(128)(2,1)}, u32[]{:S(2)}) copy-start(bf16[2048]{0:T(1024)(128)(2,1)} %param.17) | copy-start | bytes 12292
  38.9 8.3 %copy-start.1 = (bf16[4,1024,256]{2,1,0:T(8,128)(2,1)S(1)}, bf16[4,1024,256]{2,1,0:T(8,128)(2,1)}, u32[]{:S(2)}) copy-start(bf16[4,1024,256]{2,1,0:T(8,128)(2,1)} %keys_ref.2) | copy-start | bytes 6291460
  38.9 8.3 %copy-start.9 = (s32[4]{0:T(128)S(1)}, s32[4]{0:T(128)}, u32[]{:S(2)}) copy-start(s32[4]{0:T(128)} %length_ref.2) | copy-start | bytes 52
  41.8 7.9 %copy-start = (bf16[4,1024,256]{2,1,0:T(8,128)(2,1)S(1)}, bf16[4,1024,256]{2,1,0:T(8,128)(2,1)}, u32[]{:S(2)}) copy-start(bf16[4,1024,256]{2,1,0:T(8,128)(2,1)} %values_ref.2) | copy-start | bytes 6291460
  41.8 16.5 %copy-start.2 = (bf16[4,1024,256]{2,1,0:T(8,128)(2,1)S(1)}, bf16[4,1024,256]{2,1,0:T(8,128)(2,1)}, u32[]{:S(2)}) copy-start(bf16[4,1024,256]{2,1,0:T(8,128)(2,1)} %keys_ref.3) | copy-start | bytes 6291460
  41.9 16.4 %copy-start.6 = (bf16[2048]{0:T(1024)(128)(2,1)S(1)}, bf16[2048]{0:T(1024)(128)(2,1)}, u32[]{:S(2)}) copy-start(bf16[2048]{0:T(1024)(128)(2,1)} %param.23) | copy-start | bytes 12292
  41.9 16.4 %copy-start.10 = (s32[4]{0:T(128)S(1)}, s32[4]{0:T(128)}, u32[]{:S(2)}) copy-start(s32[4]{0:T(128)} %length_ref.3) | copy-start | bytes 52
  41.9 6.8 %collective-permute-start = (f32[16,640]{1,0:T(8,128)S(1)}, f32[16,640]{1,0:T(8,128)S(1)}, u32[]{:S(2)}, u32[]{:S(2)}) collective-permute-start(f32[16,640]{1,0:T(8,128)S(1)} %get-tuple-element.17), channel_id=1, source_target_pairs={{0,1},{1,0},{2,3},{3,2},{4,5},{5,4},{6,7},{7,6},{8,9},{9,8},{10,11... | collective-permute-start | bytes 122888 | tf_op jit(solution)/shard_map/ppermute | solution.py:523
  45.5 3.2 %collective-permute-start.1 = (f32[16,640]{1,0:T(8,128)S(1)}, f32[16,640]{1,0:T(8,128)S(1)}, u32[]{:S(2)}, u32[]{:S(2)}) collective-permute-start(f32[16,640]{1,0:T(8,128)S(1)} %get-tuple-element.18), channel_id=1, source_target_pairs={{0,2},{1,3},{2,0},{3,1},{4,6},{5,7},{6,4},{7,5},{8,10},{9,11},{10,... | collective-permute-start | bytes 122888 | tf_op jit(solution)/shard_map/ppermute | solution.py:523
  45.8 4.0 %collective-permute-start.2 = (f32[16,640]{1,0:T(8,128)S(1)}, f32[16,640]{1,0:T(8,128)S(1)}, u32[]{:S(2)}, u32[]{:S(2)}) collective-permute-start(f32[16,640]{1,0:T(8,128)S(1)} %get-tuple-element.19), channel_id=1, source_target_pairs={{0,3},{1,2},{2,1},{3,0},{4,7},{5,6},{6,5},{7,4},{8,11},{9,10},{10,... | collective-permute-start | bytes 122888 | tf_op jit(solution)/shard_map/ppermute | solution.py:523
  48.6 11.7 %copy-start.3 = (bf16[4,1024,256]{2,1,0:T(8,128)(2,1)S(1)}, bf16[4,1024,256]{2,1,0:T(8,128)(2,1)}, u32[]{:S(2)}) copy-start(bf16[4,1024,256]{2,1,0:T(8,128)(2,1)} %values_ref.3) | copy-start | bytes 6291460
  48.6 11.7 %copy-start.4 = (bf16[2048,51]{0,1:T(8,128)(2,1)S(1)}, bf16[2048,51]{0,1:T(8,128)(2,1)}, u32[]{:S(2)}) copy-start(bf16[2048,51]{0,1:T(8,128)(2,1)} %param.27) | copy-start | bytes 626692
  48.6 11.7 %copy-start.7 = (bf16[2048]{0:T(1024)(128)(2,1)S(1)}, bf16[2048]{0:T(1024)(128)(2,1)}, u32[]{:S(2)}) copy-start(bf16[2048]{0:T(1024)(128)(2,1)} %param.26) | copy-start | bytes 12292
  50.7 4.7 %collective-permute-start.3 = (bf16[16,2048]{1,0:T(8,128)(2,1)S(1)}, bf16[16,2048]{1,0:T(8,128)(2,1)S(1)}, u32[]{:S(2)}, u32[]{:S(2)}) collective-permute-start(bf16[16,2048]{1,0:T(8,128)(2,1)S(1)} %policy.1.rows_ref), channel_id=1, source_target_pairs={{0,64},{4,68},{8,72},{12,76},{16,80},{20,84},{24,88},{28,92},{32,9... | collective-permute-start | bytes 196616 | tf_op jit(solution)/shard_map/ppermute | solution.py:528
  55.5 4.3 %collective-permute-start.6 = (f32[16,128]{1,0:T(8,128)S(1)}, f32[16,128]{1,0:T(8,128)S(1)}, u32[]{:S(2)}, u32[]{:S(2)}) collective-permute-start(f32[16,128]{1,0:T(8,128)S(1)} %row_squares.1.own_ref), channel_id=1, source_target_pairs={{0,3},{1,2},{2,1},{3,0},{4,7},{5,6},{6,5},{7,4},{8,11},{9,10},{10,... | collective-permute-start | bytes 24584 | tf_op jit(solution)/shard_map/ppermute | solution.py:523
  57.6 2.7 %collective-permute-start.5 = (f32[16,128]{1,0:T(8,128)S(1)}, f32[16,128]{1,0:T(8,128)S(1)}, u32[]{:S(2)}, u32[]{:S(2)}) collective-permute-start(f32[16,128]{1,0:T(8,128)S(1)} %row_squares.1.own_ref), channel_id=1, source_target_pairs={{0,2},{1,3},{2,0},{3,1},{4,6},{5,7},{6,4},{7,5},{8,10},{9,11},{10,... | collective-permute-start | bytes 24584 | tf_op jit(solution)/shard_map/ppermute | solution.py:523
  58.3 2.0 %collective-permute-start.4 = (f32[16,128]{1,0:T(8,128)S(1)}, f32[16,128]{1,0:T(8,128)S(1)}, u32[]{:S(2)}, u32[]{:S(2)}) collective-permute-start(f32[16,128]{1,0:T(8,128)S(1)} %row_squares.1.own_ref), channel_id=1, source_target_pairs={{0,1},{1,0},{2,3},{3,2},{4,5},{5,4},{6,7},{7,6},{8,9},{9,8},{10,11... | collective-permute-start | bytes 24584 | tf_op jit(solution)/shard_map/ppermute | solution.py:523
  61.0 3.1 %collective-permute-start.9 = (f32[16,128]{1,0:T(8,128)S(1)}, f32[16,128]{1,0:T(8,128)S(1)}, u32[]{:S(2)}, u32[]{:S(2)}) collective-permute-start(f32[16,128]{1,0:T(8,128)S(1)} %critic.1.own_ref), channel_id=1, source_target_pairs={{0,3},{1,2},{2,1},{3,0},{4,7},{5,6},{6,5},{7,4},{8,11},{9,10},{10,... | collective-permute-start | bytes 24584 | tf_op jit(solution)/shard_map/ppermute | solution.py:523
  62.2 2.5 %collective-permute-start.8 = (f32[16,128]{1,0:T(8,128)S(1)}, f32[16,128]{1,0:T(8,128)S(1)}, u32[]{:S(2)}, u32[]{:S(2)}) collective-permute-start(f32[16,128]{1,0:T(8,128)S(1)} %critic.1.own_ref), channel_id=1, source_target_pairs={{0,2},{1,3},{2,0},{3,1},{4,6},{5,7},{6,4},{7,5},{8,10},{9,11},{10,... | collective-permute-start | bytes 24584 | tf_op jit(solution)/shard_map/ppermute | solution.py:523
  62.8 1.9 %collective-permute-start.7 = (f32[16,128]{1,0:T(8,128)S(1)}, f32[16,128]{1,0:T(8,128)S(1)}, u32[]{:S(2)}, u32[]{:S(2)}) collective-permute-start(f32[16,128]{1,0:T(8,128)S(1)} %critic.1.own_ref), channel_id=1, source_target_pairs={{0,1},{1,0},{2,3},{3,2},{4,5},{5,4},{6,7},{7,6},{8,9},{9,8},{10,11... | collective-permute-start | bytes 24584 | tf_op jit(solution)/shard_map/ppermute | solution.py:523

commit v6 on v5

--- a/solution.py
+++ b/solution.py
@@ -19,6 +19,7 @@
 norm_eps = 1e-06
 atom_span = 10.0
 masked = -1e30
+shrink = 2.0**-64
 attn_scale = 1.0 / math.sqrt(HEAD_DIM)
 log2_e = 1.0 / math.log(2.0)
 
@@ -172,7 +173,7 @@
         head, group = divmod(k, GROUP)
         for row in range(4):
             placed_ref[4 * head + row, pl.ds(4 * group, 4), :] = gained[4 * row : 4 * row + 4]
-    query_ref[...] = placed_ref[...].astype(query_ref.dtype)
+    query_ref[...] = (placed_ref[...] * shrink).astype(query_ref.dtype)
     total = jnp.broadcast_to(jnp.sum(squares, axis=1, keepdims=True), (count, LANES))
 
     def product(rows, weight):
@@ -188,24 +189,31 @@
         partial = product(rows, keys_ref[rows, :])
         keys = partial if keys is None else keys + partial
     sums_ref[0] = keys
+    head = total.astype(jnp.bfloat16)
+    tail = jnp.where(total < 3e38, total - head.astype(jnp.float32), 0.0).astype(jnp.bfloat16)
     for by, part_ref in enumerate(parts):
         start = pl.multiple_of(jnp.bitwise_xor(tp, by) * kv_width, kv_width)
         peer = pl.ds(start, kv_width)
-        part_ref[:, :kv_width] = sums_ref[0, :, peer]
-        part_ref[:, kv_width : 2 * kv_width] = sums_ref[1, :, peer]
-        part_ref[:, 2 * kv_width :] = total
+        part_ref[:, :kv_width] = sums_ref[0, :, peer].astype(part_ref.dtype)
+        part_ref[:, kv_width : 2 * kv_width] = sums_ref[1, :, peer].astype(part_ref.dtype)
+        if by == 0:
+            part_ref[:, 2 * kv_width :] = total
+        else:
+            part_ref[:, 2 * kv_width : 2 * kv_width + LANES] = head
+            part_ref[:, 2 * kv_width + LANES :] = tail
 
 
 def project(blocks, gain, early_values, key_weight, value_weight):
     width, kv_all = key_weight.shape
     count = blocks.shape[0] * LANES // width
     early = early_values.shape[0]
-    part = array((count, kv_all // 2 + LANES), jnp.float32)
+    own = array((count, kv_all // 2 + LANES), jnp.float32)
+    part = array((count, kv_all // 2 + 2 * LANES), jnp.bfloat16)
     heads = width // (GROUP * HEAD_DIM)
     queries = (4 * heads, 4 * GROUP, HEAD_DIM)
     x, query, *parts = kernel_call(
         project_kernel,
-        (array((count, width), jnp.bfloat16), array(queries, jnp.bfloat16)) + (part,) * 4,
+        (array((count, width), jnp.bfloat16), array(queries, jnp.bfloat16), own) + (part,) * 3,
         [VMEM] * 3 + [HBM] * 2,
         scratch=[
             pltpu.VMEM((count, width), jnp.bfloat16),
@@ -265,6 +273,10 @@
     return jnp.concatenate([x] * (width // LANES), axis=1)
 
 
+def masked_weights(raw, spread, highest):
+    return jnp.where(raw > 0.5 * masked, jnp.exp2(raw * spread - highest), 0.0)
+
+
 def policy_kernel(
     own_ref,
     one_ref,
@@ -282,12 +294,16 @@
     count, width = x_ref.shape
     kv_width = values_ref.shape[2]
     cache_size = values_ref.shape[1]
-    total = own_ref[...] + (one_ref[...] + (two_ref[...] + three_ref[...]))
+    total = own_ref[...]
+    for part_ref in (one_ref, two_ref, three_ref):
+        part = part_ref[...].astype(jnp.float32)
+        squares = part[:, 2 * kv_width : 2 * kv_width + LANES] + part[:, 2 * kv_width + LANES :]
+        total = total + jnp.concatenate([part[:, : 2 * kv_width], squares], axis=1)
     inv = lax.rsqrt(total[:, 2 * kv_width :] * (1.0 / D) + norm_eps)
     wide = widened(inv, kv_width)
     new_key = (wide * total[:, :kv_width]).astype(jnp.bfloat16)
     new_value = (wide * total[:, kv_width : 2 * kv_width]).astype(jnp.bfloat16)
-    spread_rows(inv * (attn_scale * log2_e), spread_ref)
+    spread_rows(inv * (attn_scale * log2_e / shrink), spread_ref)
     queries = query_ref.shape[1]
     at_query = lax.broadcasted_iota(jnp.int32, (4 * queries, count), 0)
     at_fresh = lax.broadcasted_iota(jnp.int32, (4 * queries, count), 1)
@@ -309,10 +325,10 @@
             part = slice(row * queries, (row + 1) * queries)
             spread = spread_ref[row]
             highest = jnp.maximum(top_ref[at], fresh_top[part]) * spread
-            weights = jnp.exp2(
-                raw_ref[at] * widened(spread, cache_size) - widened(highest, cache_size)
+            weights = masked_weights(
+                raw_ref[at], widened(spread, cache_size), widened(highest, cache_size)
             )
-            extra = jnp.exp2(fresh[part] * spread[:, :count] - highest[:, :count])
+            extra = masked_weights(fresh[part], spread[:, :count], highest[:, :count])
             inverses.append(
                 1.0
                 / (jnp.sum(weights, axis=1, keepdims=True) + jnp.sum(extra, axis=1, keepdims=True))
@@ -406,7 +422,7 @@
     for at in range(placed_ref.shape[0]):
         head, row = divmod(at, 4)
         keys = keys_ref[row, :, pl.ds(head * HEAD_DIM, HEAD_DIM)]
-        query = placed_ref[at].astype(jnp.bfloat16)
+        query = (placed_ref[at] * shrink).astype(jnp.bfloat16)
         masked_scores(query, keys, length_ref[row], raw_ref, top_ref, at)
 
 
@@ -445,12 +461,14 @@
     cache_size = values_ref.shape[1]
     total = own_ref[...] + (one_ref[...] + (two_ref[...] + three_ref[...]))
     inv = lax.rsqrt(total * (1.0 / D) + norm_eps)
-    spread_rows(inv * (attn_scale * log2_e), spread_ref)
+    spread_rows(inv * (attn_scale * log2_e / shrink), spread_ref)
     for at in range(raw_ref.shape[0]):
         head, row = divmod(at, 4)
         spread = spread_ref[row]
-        weights = jnp.exp2(
-            raw_ref[at] * widened(spread, cache_size) - widened(top_ref[at] * spread, cache_size)
+        weights = masked_weights(
+            raw_ref[at],
+            widened(spread, cache_size),
+            widened(top_ref[at] * spread, cache_size),
         )
         inverse = 1.0 / jnp.sum(weights, axis=1, keepdims=True)
         attended = inverse * jnp.dot(

time: 65.8 us -> 65.6 us (level)
  no operation moved by 1% of the time
where the time goes in v6:
time: 65.6 us; the launch traced here: 65.3 us
  blocking collectives  31.7 us (48%)
  Pallas kernels  15.1 us (23%)
  starting transfers between devices  11.5 us (18%)
  waiting for transfers between devices  5.59 us (9%)
  between operations  0.76 us (1%)
  local copies, waits for them, and re-layouts  0.72 us (1%)
    all_to_all x1, blocking collectives, on_device(): all_tokens = lax.all_to_all(laid_out(tokens, row_groups), 'rows', 0, 0)  19.8 us
    all_to_all x1, blocking collectives, on_device(): blocks = lax.all_to_all(picked.reshape(row_groups, -1, LANES), 'rows', 0, 0)  11.9 us
    ppermute x9, starting transfers between devices, swapped(): return lax.ppermute(shard, 'tp', [(i, i ^ by) for i in range(peers)])  10.4 us
    pallas_call x1, Pallas kernels, pick_rows(): kernel_call(pick_rows_kernel, (array((rows, LANES), table.dtype), pltpu.V...  5.78 us
    ppermute x1, waiting for transfers between devices, passed_along(): lax.ppermute(shard, axis, [(i, (i + by) % peers) for i in range(peers)])  3.63 us
    pallas_call x1, Pallas kernels, project(): kernel_call(project_kernel, (array((count, width), jnp.bfloat16), array(q...  2.94 us
    ppermute x9, waiting for transfers between devices, swapped(): return lax.ppermute(shard, 'tp', [(i, i ^ by) for i in range(peers)])  1.96 us
    pallas_call x1, Pallas kernels, critic_scores(): kernel_call(critic_scores_kernel, (raw, array(placed, jnp.float32)), [SME...  1.45 us
  transfers between devices with their start and end apart: 10, of which 5 were waited for; matrix products, arithmetic and copies ran while one was open for 0% of the time, Pallas kernels for 5%

profile of v6, /device:TPU:1, one launch (start us, length us, event | category | flops | bytes accessed | tf_op | source)
XLA Modules:
  0.0 65.3 jit_solution(16883632404374419873)
XLA Ops:
  0.6 0.0 copy-start.8
  0.6 0.7 %copy-done.8 = s32[4,4]{1,0:T(4,128)S(1)} copy-done((s32[4,4]{1,0:T(4,128)S(1)}, s32[4,4]{1,0:T(4,128)}, u32[]{:S(2)}) %copy-start.8) | copy-done | bytes 88
  1.3 0.1 lay_out.1
  1.4 19.8 %all_to_all.10.token_ref = s32[32,1,16]{2,1,0:T(1,128)S(1)} all-to-all(s32[32,1,16]{2,1,0:T(1,128)S(1)} %lay_out.1), channel_id=1, replica_groups=mesh['rows'=32,'tp'=4] {'rows'}, dimensions={0} | all-to-all | bytes 4096 | tf_op jit(solution)/shard_map/all_to_all | solution.py:575
  21.2 0.0 copy-start.5
  21.2 5.8 %pick_rows.1 = (bf16[256,128]{1,0:T(8,128)(2,1)S(1)}, bf16[1536,1024]{1,0:T(8,128)(2,1)S(1)}) custom-call(s32[32,1,16]{2,1,0:T(1,128)S(1)} %all_to_all.10.token_ref, bf16[64,76032]{1,0:T(8,128)(2,1)} %bitcast.15, bf16[2048,1024]{1,0:T(8,128)(2,1)} %value_ref.1), custom_call_target="tpu_custom_call" | custom-call | tf_op jit(solution)/shard_map/pick_rows/pallas_call | solution.py:128
  27.0 11.9 %all_to_all.11 = bf16[32,8,128]{2,1,0:T(8,128)(2,1)S(1)} all-to-all(bf16[32,8,128]{2,1,0:T(8,128)(2,1)S(1)} %bitcast.11), channel_id=1, replica_groups=mesh['rows'=32,'tp'=4] {'rows'}, dimensions={0} | all-to-all | bytes 131072 | tf_op jit(solution)/shard_map/all_to_all | solution.py:577
  38.9 0.0 copy-done.5
  38.9 0.0 copy-start.1
  38.9 0.0 copy-start.9
  38.9 2.9 %project.1 = (bf16[16,2048]{1,0:T(8,128)(2,1)S(1)}, bf16[8,32,128]{2,1,0:T(8,128)(2,1)S(1)}, f32[16,640]{1,0:T(8,128)S(1)}, bf16[16,768]{1,0:T(8,128)(2,1)S(1)},...) custom-call(bf16[256,128]{1,0:T(8,128)(2,1)S(1)} %bitcast.9, bf16[16,128]{1,0:T(8,128)(2,1)S(1)} %bitcast.12, ...), custom_call_target="tpu_custom_call" | custom-call | flops 134217728 | bytes 8388608 | tf_op jit(solution)/shard_map/project/pallas_call | solution.py:214
  41.8 0.0 copy-start
  41.8 0.0 copy-start.2
  41.9 0.0 copy-start.6
  41.9 0.0 copy-start.10
  41.9 3.6 %collective-permute-start = (bf16[16,768]{1,0:T(8,128)(2,1)S(1)}, bf16[16,768]{1,0:T(8,128)(2,1)S(1)}, u32[]{:S(2)}, u32[]{:S(2)}) collective-permute-start(bf16[16,768]{1,0:T(8,128)(2,1)S(1)} %get-tuple-element.17), channel_id=1, source_target_pairs={{0,1},{1,0},{2,3},{3,2},{4,5},{5,4},{6,7},{7,6},{8,9},{9,8},{10,11... | collective-permute-start | bytes 73736 | tf_op jit(solution)/shard_map/ppermute | solution.py:541
  45.5 0.3 collective-permute-start.1
  45.8 1.4 %collective-permute-start.2 = (bf16[16,768]{1,0:T(8,128)(2,1)S(1)}, bf16[16,768]{1,0:T(8,128)(2,1)S(1)}, u32[]{:S(2)}, u32[]{:S(2)}) collective-permute-start(bf16[16,768]{1,0:T(8,128)(2,1)S(1)} %get-tuple-element.19), channel_id=1, source_target_pairs={{0,3},{1,2},{2,1},{3,0},{4,7},{5,6},{6,5},{7,4},{8,11},{9,10},{10,... | collective-permute-start | bytes 73736 | tf_op jit(solution)/shard_map/ppermute | solution.py:541
  47.2 0.0 copy-done.1
  47.2 0.0 copy-done.9
  47.2 1.4 %policy_scores.1 = (f32[8,32,1024]{2,1,0:T(8,128)S(1)}, f32[8,32,128]{2,1,0:T(8,128)S(1)}) custom-call(s32[4]{0:T(128)S(1)} %copy-done.9, bf16[8,32,128]{2,1,0:T(8,128)(2,1)S(1)} %get-tuple-element.20.query_ref, bf16[4,1024,256]{2,1,0:T(8,128)(2,1)S(1)} %copy-done.1), custom_call_target="tpu_custom_call" | custom-call | flops 67108864 | bytes 3145728 | tf_op jit(solution)/shard_map/policy_scores/pallas_call | solution.py:256
  48.6 0.0 copy-start.3
  48.6 0.0 copy-start.4
  48.6 0.0 copy-start.7
  48.6 0.0 collective-permute-done.one_ref
  48.7 0.0 collective-permute-done.1.two_ref
  48.7 0.6 collective-permute-done.2.three_ref
  49.3 0.0 copy-done
  49.3 1.1 %policy.1.rows_ref = bf16[16,2048]{1,0:T(8,128)(2,1)S(1)} custom-call(f32[16,640]{1,0:T(8,128)S(1)} %get-tuple-element.16.own_ref, bf16[16,768]{1,0:T(8,128)(2,1)S(1)} %collective-permute-done.one_ref, bf16[16,768]{1,0:T(8,128)(2,1)S(1)} %collective-permute-done.1.two_ref, bf16[16,768]{1,0:T(8,128)(2,1)S(1)} %collective-permute-done.2.three_ref, ...), custom_call_target="tpu_custom_call" | custom-call | flops 67108864 | bytes 3145728 | tf_op jit(solution)/shard_map/policy/pallas_call | solution.py:363
  50.3 1.1 %collective-permute-start.3 = (bf16[16,2048]{1,0:T(8,128)(2,1)S(1)}, bf16[16,2048]{1,0:T(8,128)(2,1)S(1)}, u32[]{:S(2)}, u32[]{:S(2)}) collective-permute-start(bf16[16,2048]{1,0:T(8,128)(2,1)S(1)} %policy.1.rows_ref), channel_id=1, source_target_pairs={{0,64},{4,68},{8,72},{12,76},{16,80},{20,84},{24,88},{28,92},{32,9... | collective-permute-start | bytes 196616 | tf_op jit(solution)/shard_map/ppermute | solution.py:546
  51.4 3.6 %collective-permute-done.3.rows_ref = bf16[16,2048]{1,0:T(8,128)(2,1)S(1)} collective-permute-done((bf16[16,2048]{1,0:T(8,128)(2,1)S(1)}, bf16[16,2048]{1,0:T(8,128)(2,1)S(1)}, u32[]{:S(2)}, u32[]{:S(2)}) %collective-permute-start.3) | collective-permute-done | bytes 65568 | tf_op jit(solution)/shard_map/ppermute | solution.py:546
  55.0 0.1 row_squares.1.own_ref
  55.1 2.3 %collective-permute-start.6 = (f32[16,128]{1,0:T(8,128)S(1)}, f32[16,128]{1,0:T(8,128)S(1)}, u32[]{:S(2)}, u32[]{:S(2)}) collective-permute-start(f32[16,128]{1,0:T(8,128)S(1)} %row_squares.1.own_ref), channel_id=1, source_target_pairs={{0,3},{1,2},{2,1},{3,0},{4,7},{5,6},{6,5},{7,4},{8,11},{9,10},{10,... | collective-permute-start | bytes 24584 | tf_op jit(solution)/shard_map/ppermute | solution.py:541
  57.5 0.6 collective-permute-start.5
  58.0 0.0 collective-permute-start.4
  58.0 0.0 copy-done.2
  58.0 0.0 copy-done.6
  58.0 0.0 copy-done.10
  58.1 1.4 %critic_scores.1 = (f32[8,32,1024]{2,1,0:T(8,128)S(1)}, f32[8,32,128]{2,1,0:T(8,128)S(1)}) custom-call(s32[4]{0:T(128)S(1)} %copy-done.10, bf16[16,2048]{1,0:T(8,128)(2,1)S(1)} %collective-permute-done.3.rows_ref, bf16[16,128]{1,0:T(8,128)(2,1)S(1)} %bitcast.13, bf16[4,1024,256]{2,1,0:T(8,128)(2,1)S(1)} %copy-done.2), custom_call_target="tpu_custom_call" | custom-call | flops 67108864 | bytes 3145728 | tf_op jit(solution)/shard_map/critic_scores/pallas_call | solution.py:433
  59.5 0.0 collective-permute-done.6.three_ref
  59.5 0.5 collective-permute-done.5.two_ref
  60.0 0.0 collective-permute-done.4.one_ref
  60.0 0.0 copy-done.3
  60.0 0.0 copy-done.4
  60.0 0.0 copy-done.7
  60.1 0.8 %critic.1.own_ref = f32[16,128]{1,0:T(8,128)S(1)} custom-call(f32[16,128]{1,0:T(8,128)S(1)} %row_squares.1.own_ref, f32[16,128]{1,0:T(8,128)S(1)} %collective-permute-done.4.one_ref, f32[16,128]{1,0:T(8,128)S(1)} %collective-permute-done.5.two_ref, f32[16,128]{1,0:T(8,128)S(1)} %collective-permute-done.6.three_ref, ...), custom_call_target="tpu_custom_call" | custom-call | flops 67108864 | bytes 3145728 | tf_op jit(solution)/shard_map/critic/pallas_call | solution.py:500
  60.8 1.2 %collective-permute-start.9 = (f32[16,128]{1,0:T(8,128)S(1)}, f32[16,128]{1,0:T(8,128)S(1)}, u32[]{:S(2)}, u32[]{:S(2)}) collective-permute-start(f32[16,128]{1,0:T(8,128)S(1)} %critic.1.own_ref), channel_id=1, source_target_pairs={{0,3},{1,2},{2,1},{3,0},{4,7},{5,6},{6,5},{7,4},{8,11},{9,10},{10,... | collective-permute-start | bytes 24584 | tf_op jit(solution)/shard_map/ppermute | solution.py:541
  62.0 0.6 collective-permute-start.8
  62.6 0.4 collective-permute-start.7
  63.0 0.7 %by_step.1 = bf16[4,4,2048]{2,1,0:T(4,128)(2,1)} custom-call(bf16[16,2048]{1,0:T(8,128)(2,1)S(1)} %policy.1.rows_ref), custom_call_target="tpu_custom_call" | custom-call | bytes 524288 | tf_op jit(solution)/shard_map/by_step/pallas_call | solution.py:389
  63.7 0.2 collective-permute-done.9.three_ref
  63.9 0.6 collective-permute-done.8.two_ref
  64.5 0.0 collective-permute-done.7.one_ref
  64.5 0.8 %expect.1 = f32[4,4]{1,0:T(4,128)} custom-call(f32[16,128]{1,0:T(8,128)S(1)} %critic.1.own_ref, f32[16,128]{1,0:T(8,128)S(1)} %collective-permute-done.7.one_ref, f32[16,128]{1,0:T(8,128)S(1)} %collective-permute-done.8.two_ref, f32[16,128]{1,0:T(8,128)S(1)} %collective-permute-done.9.three_ref), custom_call_target="tpu_custom_call" | custom-call | tf_op jit(solution)/shard_map/expect/pallas_call | solution.py:536
Async XLA Ops:
  0.6 0.7 %copy-start.8 = (s32[4,4]{1,0:T(4,128)S(1)}, s32[4,4]{1,0:T(4,128)}, u32[]{:S(2)}) copy-start(s32[4,4]{1,0:T(4,128)} %token_ref.1) | copy-start | bytes 196
  21.2 17.7 %copy-start.5 = (bf16[2048]{0:T(1024)(128)(2,1)S(1)}, bf16[2048]{0:T(1024)(128)(2,1)}, u32[]{:S(2)}) copy-start(bf16[2048]{0:T(1024)(128)(2,1)} %param.17) | copy-start | bytes 12292
  38.9 8.3 %copy-start.1 = (bf16[4,1024,256]{2,1,0:T(8,128)(2,1)S(1)}, bf16[4,1024,256]{2,1,0:T(8,128)(2,1)}, u32[]{:S(2)}) copy-start(bf16[4,1024,256]{2,1,0:T(8,128)(2,1)} %keys_ref.2) | copy-start | bytes 6291460
  38.9 8.3 %copy-start.9 = (s32[4]{0:T(128)S(1)}, s32[4]{0:T(128)}, u32[]{:S(2)}) copy-start(s32[4]{0:T(128)} %length_ref.2) | copy-start | bytes 52
  41.8 7.4 %copy-start = (bf16[4,1024,256]{2,1,0:T(8,128)(2,1)S(1)}, bf16[4,1024,256]{2,1,0:T(8,128)(2,1)}, u32[]{:S(2)}) copy-start(bf16[4,1024,256]{2,1,0:T(8,128)(2,1)} %values_ref.2) | copy-start | bytes 6291460
  41.8 16.2 %copy-start.2 = (bf16[4,1024,256]{2,1,0:T(8,128)(2,1)S(1)}, bf16[4,1024,256]{2,1,0:T(8,128)(2,1)}, u32[]{:S(2)}) copy-start(bf16[4,1024,256]{2,1,0:T(8,128)(2,1)} %keys_ref.3) | copy-start | bytes 6291460
  41.9 16.2 %copy-start.6 = (bf16[2048]{0:T(1024)(128)(2,1)S(1)}, bf16[2048]{0:T(1024)(128)(2,1)}, u32[]{:S(2)}) copy-start(bf16[2048]{0:T(1024)(128)(2,1)} %param.23) | copy-start | bytes 12292
  41.9 16.2 %copy-start.10 = (s32[4]{0:T(128)S(1)}, s32[4]{0:T(128)}, u32[]{:S(2)}) copy-start(s32[4]{0:T(128)} %length_ref.3) | copy-start | bytes 52
  41.9 6.8 %collective-permute-start = (bf16[16,768]{1,0:T(8,128)(2,1)S(1)}, bf16[16,768]{1,0:T(8,128)(2,1)S(1)}, u32[]{:S(2)}, u32[]{:S(2)}) collective-permute-start(bf16[16,768]{1,0:T(8,128)(2,1)S(1)} %get-tuple-element.17), channel_id=1, source_target_pairs={{0,1},{1,0},{2,3},{3,2},{4,5},{5,4},{6,7},{7,6},{8,9},{9,8},{10,11... | collective-permute-start | bytes 73736 | tf_op jit(solution)/shard_map/ppermute | solution.py:541
  45.5 3.2 %collective-permute-start.1 = (bf16[16,768]{1,0:T(8,128)(2,1)S(1)}, bf16[16,768]{1,0:T(8,128)(2,1)S(1)}, u32[]{:S(2)}, u32[]{:S(2)}) collective-permute-start(bf16[16,768]{1,0:T(8,128)(2,1)S(1)} %get-tuple-element.18), channel_id=1, source_target_pairs={{0,2},{1,3},{2,0},{3,1},{4,6},{5,7},{6,4},{7,5},{8,10},{9,11},{10,... | collective-permute-start | bytes 73736 | tf_op jit(solution)/shard_map/ppermute | solution.py:541
  45.8 3.5 %collective-permute-start.2 = (bf16[16,768]{1,0:T(8,128)(2,1)S(1)}, bf16[16,768]{1,0:T(8,128)(2,1)S(1)}, u32[]{:S(2)}, u32[]{:S(2)}) collective-permute-start(bf16[16,768]{1,0:T(8,128)(2,1)S(1)} %get-tuple-element.19), channel_id=1, source_target_pairs={{0,3},{1,2},{2,1},{3,0},{4,7},{5,6},{6,5},{7,4},{8,11},{9,10},{10,... | collective-permute-start | bytes 73736 | tf_op jit(solution)/shard_map/ppermute | solution.py:541
  48.6 11.4 %copy-start.3 = (bf16[4,1024,256]{2,1,0:T(8,128)(2,1)S(1)}, bf16[4,1024,256]{2,1,0:T(8,128)(2,1)}, u32[]{:S(2)}) copy-start(bf16[4,1024,256]{2,1,0:T(8,128)(2,1)} %values_ref.3) | copy-start | bytes 6291460
  48.6 11.4 %copy-start.4 = (bf16[2048,51]{0,1:T(8,128)(2,1)S(1)}, bf16[2048,51]{0,1:T(8,128)(2,1)}, u32[]{:S(2)}) copy-start(bf16[2048,51]{0,1:T(8,128)(2,1)} %param.27) | copy-start | bytes 626692
  48.6 11.4 %copy-start.7 = (bf16[2048]{0:T(1024)(128)(2,1)S(1)}, bf16[2048]{0:T(1024)(128)(2,1)}, u32[]{:S(2)}) copy-start(bf16[2048]{0:T(1024)(128)(2,1)} %param.26) | copy-start | bytes 12292
  50.3 4.7 %collective-permute-start.3 = (bf16[16,2048]{1,0:T(8,128)(2,1)S(1)}, bf16[16,2048]{1,0:T(8,128)(2,1)S(1)}, u32[]{:S(2)}, u32[]{:S(2)}) collective-permute-start(bf16[16,2048]{1,0:T(8,128)(2,1)S(1)} %policy.1.rows_ref), channel_id=1, source_target_pairs={{0,64},{4,68},{8,72},{12,76},{16,80},{20,84},{24,88},{28,92},{32,9... | collective-permute-start | bytes 196616 | tf_op jit(solution)/shard_map/ppermute | solution.py:546
  55.1 4.4 %collective-permute-start.6 = (f32[16,128]{1,0:T(8,128)S(1)}, f32[16,128]{1,0:T(8,128)S(1)}, u32[]{:S(2)}, u32[]{:S(2)}) collective-permute-start(f32[16,128]{1,0:T(8,128)S(1)} %row_squares.1.own_ref), channel_id=1, source_target_pairs={{0,3},{1,2},{2,1},{3,0},{4,7},{5,6},{6,5},{7,4},{8,11},{9,10},{10,... | collective-permute-start | bytes 24584 | tf_op jit(solution)/shard_map/ppermute | solution.py:541
  57.5 2.6 %collective-permute-start.5 = (f32[16,128]{1,0:T(8,128)S(1)}, f32[16,128]{1,0:T(8,128)S(1)}, u32[]{:S(2)}, u32[]{:S(2)}) collective-permute-start(f32[16,128]{1,0:T(8,128)S(1)} %row_squares.1.own_ref), channel_id=1, source_target_pairs={{0,2},{1,3},{2,0},{3,1},{4,6},{5,7},{6,4},{7,5},{8,10},{9,11},{10,... | collective-permute-start | bytes 24584 | tf_op jit(solution)/shard_map/ppermute | solution.py:541
  58.0 2.0 %collective-permute-start.4 = (f32[16,128]{1,0:T(8,128)S(1)}, f32[16,128]{1,0:T(8,128)S(1)}, u32[]{:S(2)}, u32[]{:S(2)}) collective-permute-start(f32[16,128]{1,0:T(8,128)S(1)} %row_squares.1.own_ref), channel_id=1, source_target_pairs={{0,1},{1,0},{2,3},{3,2},{4,5},{5,4},{6,7},{7,6},{8,9},{9,8},{10,11... | collective-permute-start | bytes 24584 | tf_op jit(solution)/shard_map/ppermute | solution.py:541
  60.8 3.1 %collective-permute-start.9 = (f32[16,128]{1,0:T(8,128)S(1)}, f32[16,128]{1,0:T(8,128)S(1)}, u32[]{:S(2)}, u32[]{:S(2)}) collective-permute-start(f32[16,128]{1,0:T(8,128)S(1)} %critic.1.own_ref), channel_id=1, source_target_pairs={{0,3},{1,2},{2,1},{3,0},{4,7},{5,6},{6,5},{7,4},{8,11},{9,10},{10,... | collective-permute-start | bytes 24584 | tf_op jit(solution)/shard_map/ppermute | solution.py:541
  62.0 2.5 %collective-permute-start.8 = (f32[16,128]{1,0:T(8,128)S(1)}, f32[16,128]{1,0:T(8,128)S(1)}, u32[]{:S(2)}, u32[]{:S(2)}) collective-permute-start(f32[16,128]{1,0:T(8,128)S(1)} %critic.1.own_ref), channel_id=1, source_target_pairs={{0,2},{1,3},{2,0},{3,1},{4,6},{5,7},{6,4},{7,5},{8,10},{9,11},{10,... | collective-permute-start | bytes 24584 | tf_op jit(solution)/shard_map/ppermute | solution.py:541
  62.6 1.9 %collective-permute-start.7 = (f32[16,128]{1,0:T(8,128)S(1)}, f32[16,128]{1,0:T(8,128)S(1)}, u32[]{:S(2)}, u32[]{:S(2)}) collective-permute-start(f32[16,128]{1,0:T(8,128)S(1)} %critic.1.own_ref), channel_id=1, source_target_pairs={{0,1},{1,0},{2,3},{3,2},{4,5},{5,4},{6,7},{7,6},{8,9},{9,8},{10,11... | collective-permute-start | bytes 24584 | tf_op jit(solution)/shard_map/ppermute | solution.py:541

commit v7 on v6

--- a/solution.py
+++ b/solution.py
@@ -288,6 +288,7 @@
     x_ref,
     values_ref,
     passed_ref,
+    squares_ref,
     spread_ref,
     rows_ref,
 ):
@@ -352,17 +353,21 @@
                 rows_ref[head * GROUP + group, pl.ds(4 * row, 4), :] = both[
                     4 * group : 4 * group + 4
                 ]
+    squares = jnp.zeros((count, LANES), jnp.float32)
     for k in range(width // LANES):
         columns = pl.ds(k * LANES, LANES)
-        hidden = x_ref[:, columns].astype(jnp.float32) + rows_ref[k]
-        passed_ref[:, columns] = hidden.astype(passed_ref.dtype)
+        hidden = (x_ref[:, columns].astype(jnp.float32) + rows_ref[k]).astype(passed_ref.dtype)
+        passed_ref[:, columns] = hidden
+        hidden = hidden.astype(jnp.float32)
+        squares += hidden * hidden
+    squares_ref[...] = jnp.broadcast_to(jnp.sum(squares, axis=1, keepdims=True), squares_ref.shape)
 
 
 def policy(parts, raw, top, query, x, values):
     count, width = x.shape
     return kernel_call(
         policy_kernel,
-        array((count, width), jnp.bfloat16),
+        (array((count, width), jnp.bfloat16), array((count, LANES), jnp.float32)),
         [VMEM] * 9,
         scratch=[
             pltpu.VMEM((4, 4 * GROUP, LANES), jnp.float32),
@@ -396,18 +401,21 @@
     )(rows)
 
 
-def squares_kernel(rows_ref, out_ref):
+def squares_kernel(rows_ref, other_ref, _, out_ref):
     squares = jnp.zeros(out_ref.shape, jnp.float32)
     for k in range(rows_ref.shape[1] // LANES):
         part = rows_ref[:, pl.ds(k * LANES, LANES)].astype(jnp.float32)
         squares += part * part
-    out_ref[...] = jnp.broadcast_to(jnp.sum(squares, axis=1, keepdims=True), out_ref.shape)
-
-
-def row_squares(rows):
+    out_ref[...] = other_ref[...] + jnp.sum(squares, axis=1, keepdims=True)
+
+
+def row_squares(rows, other, after):
     return kernel_call(
-        squares_kernel, array((rows.shape[0], LANES), jnp.float32), [VMEM], name="row_squares"
-    )(rows)
+        squares_kernel,
+        array(other.shape, jnp.float32),
+        [VMEM, VMEM, pl.BlockSpec(memory_space=pl.ANY)],
+        name="row_squares",
+    )(rows, other, after)
 
 
 def critic_scores_kernel(
@@ -442,10 +450,8 @@
 
 
 def critic_kernel(
-    own_ref,
-    one_ref,
-    two_ref,
-    three_ref,
+    near_ref,
+    far_ref,
     raw_ref,
     top_ref,
     rows_ref,
@@ -459,8 +465,7 @@
 ):
     count, width = rows_ref.shape
     cache_size = values_ref.shape[1]
-    total = own_ref[...] + (one_ref[...] + (two_ref[...] + three_ref[...]))
-    inv = lax.rsqrt(total * (1.0 / D) + norm_eps)
+    inv = lax.rsqrt((near_ref[...] + far_ref[...]) * (1.0 / D) + norm_eps)
     spread_rows(inv * (attn_scale * log2_e / shrink), spread_ref)
     for at in range(raw_ref.shape[0]):
         head, row = divmod(at, 4)
@@ -500,7 +505,7 @@
     return kernel_call(
         critic_kernel,
         array((count, LANES), jnp.float32),
-        [VMEM] * 10,
+        [VMEM] * 8,
         scratch=[
             pltpu.VMEM((4, 4 * GROUP, LANES), jnp.float32),
             pltpu.VMEM((width // LANES, count, LANES), jnp.float32),
@@ -544,6 +549,17 @@
 def passed_along(shard, axis, by):
     peers = lax.axis_size(axis)
     return lax.ppermute(shard, axis, [(i, (i + by) % peers) for i in range(peers)])
+
+
+def crossed(shard, by_rows, by_tp):
+    peers = lax.axis_size("tp")
+    groups = lax.axis_size("rows")
+    pairs = [
+        (r * peers + t, (r + by_rows) % groups * peers + (t ^ by_tp))
+        for r in range(groups)
+        for t in range(peers)
+    ]
+    return lax.ppermute(shard, ("rows", "tp"), pairs)
 
 
 def with_peers(shard):
@@ -580,13 +596,15 @@
     )
     arrived = parts[:1] + [swapped(parts[by], by) for by in (1, 2, 3)]
     raw, top = policy_scores(lengths, query, policy_keys)
-    passed = policy(arrived, raw, top, query, x, policy_values)
+    passed, squares = policy(arrived, raw, top, query, x, policy_values)
     rows = passed_along(passed, "rows", row_groups // 2)
+    squares = crossed(squares, row_groups // 2, 2)
     hidden = by_step(passed)
 
     raw, top = critic_scores(critic_lengths, rows, as_rows(critic_gain), critic_keys)
+    near = row_squares(rows, squares, top)
     logits = critic(
-        with_peers(row_squares(rows)),
+        (near, swapped(near, 1)),
         raw,
         top,
         rows,

time: 65.6 us -> 64.6 us (0.985)
  waiting for transfers between devices: 5.59 us -> 3.26 us
  starting transfers between devices: 11.5 us -> 12.7 us
    ppermute x0 -> x1, starting transfers between devices: none -> 2.62 us  [crossed(): return lax.ppermute(shard, ('rows', 'tp'), pairs)]
    ppermute x1, waiting for transfers between devices: 3.63 us -> 1.01 us  [passed_along(): lax.ppermute(shard, axis, [(i, (i + by) % peers) for i in range(peers)])]
    ppermute x9 -> x7, starting transfers between devices: 10.4 us -> 9.11 us  [swapped(): return lax.ppermute(shard, 'tp', [(i, i ^ by) for i in range(peers)])]
    ppermute x9 -> x7, waiting for transfers between devices: 1.96 us -> 2.24 us  [swapped(): return lax.ppermute(shard, 'tp', [(i, i ^ by) for i in range(peers)])]
  transfers between devices with their start and end apart: 10 -> 9, of which waited for: 5 -> 5; matrix products, arithmetic and copies ran while one was open for 0% -> 0% of each run, Pallas kernels for 5% -> 6%
where the time goes in v7:
time: 64.6 us; the launch traced here: 64.4 us
  blocking collectives  31.7 us (49%)
  Pallas kernels  15.3 us (24%)
  starting transfers between devices  12.7 us (20%)
  waiting for transfers between devices  3.26 us (5%)
  between operations  0.74 us (1%)
  local copies, waits for them, and re-layouts  0.72 us (1%)
    all_to_all x1, blocking collectives, on_device(): all_tokens = lax.all_to_all(laid_out(tokens, row_groups), 'rows', 0, 0)  19.8 us
    all_to_all x1, blocking collectives, on_device(): blocks = lax.all_to_all(picked.reshape(row_groups, -1, LANES), 'rows', 0, 0)  11.9 us
    ppermute x7, starting transfers between devices, swapped(): return lax.ppermute(shard, 'tp', [(i, i ^ by) for i in range(peers)])  9.11 us
    pallas_call x1, Pallas kernels, pick_rows(): kernel_call(pick_rows_kernel, (array((rows, LANES), table.dtype), pltpu.V...  5.78 us
    pallas_call x1, Pallas kernels, project(): kernel_call(project_kernel, (array((count, width), jnp.bfloat16), array(q...  2.94 us
    ppermute x1, starting transfers between devices, crossed(): return lax.ppermute(shard, ('rows', 'tp'), pairs)  2.62 us
    ppermute x7, waiting for transfers between devices, swapped(): return lax.ppermute(shard, 'tp', [(i, i ^ by) for i in range(peers)])  2.24 us
    pallas_call x1, Pallas kernels, critic_scores(): kernel_call(critic_scores_kernel, (raw, array(placed, jnp.float32)), [SME...  1.45 us
  transfers between devices with their start and end apart: 9, of which 5 were waited for; matrix products, arithmetic and copies ran while one was open for 0% of the time, Pallas kernels for 6%

profile of v7, /device:TPU:1, one launch (start us, length us, event | category | flops | bytes accessed | tf_op | source)
XLA Modules:
  0.0 64.4 jit_solution(4107875496507915216)
XLA Ops:
  0.6 0.0 copy-start.8
  0.6 0.7 %copy-done.8 = s32[4,4]{1,0:T(4,128)S(1)} copy-done((s32[4,4]{1,0:T(4,128)S(1)}, s32[4,4]{1,0:T(4,128)}, u32[]{:S(2)}) %copy-start.8) | copy-done | bytes 88
  1.3 0.1 lay_out.1
  1.4 19.8 %all_to_all.10.token_ref = s32[32,1,16]{2,1,0:T(1,128)S(1)} all-to-all(s32[32,1,16]{2,1,0:T(1,128)S(1)} %lay_out.1), channel_id=1, replica_groups=mesh['rows'=32,'tp'=4] {'rows'}, dimensions={0} | all-to-all | bytes 4096 | tf_op jit(solution)/shard_map/all_to_all | solution.py:591
  21.2 0.0 copy-start.5
  21.2 5.8 %pick_rows.1 = (bf16[256,128]{1,0:T(8,128)(2,1)S(1)}, bf16[1536,1024]{1,0:T(8,128)(2,1)S(1)}) custom-call(s32[32,1,16]{2,1,0:T(1,128)S(1)} %all_to_all.10.token_ref, bf16[64,76032]{1,0:T(8,128)(2,1)} %bitcast.15, bf16[2048,1024]{1,0:T(8,128)(2,1)} %value_ref.1), custom_call_target="tpu_custom_call" | custom-call | tf_op jit(solution)/shard_map/pick_rows/pallas_call | solution.py:128
  27.0 11.9 %all_to_all.11 = bf16[32,8,128]{2,1,0:T(8,128)(2,1)S(1)} all-to-all(bf16[32,8,128]{2,1,0:T(8,128)(2,1)S(1)} %bitcast.11), channel_id=1, replica_groups=mesh['rows'=32,'tp'=4] {'rows'}, dimensions={0} | all-to-all | bytes 131072 | tf_op jit(solution)/shard_map/all_to_all | solution.py:593
  38.9 0.0 copy-done.5
  38.9 0.0 copy-start.1
  38.9 0.0 copy-start.9
  38.9 2.9 %project.1 = (bf16[16,2048]{1,0:T(8,128)(2,1)S(1)}, bf16[8,32,128]{2,1,0:T(8,128)(2,1)S(1)}, f32[16,640]{1,0:T(8,128)S(1)}, bf16[16,768]{1,0:T(8,128)(2,1)S(1)},...) custom-call(bf16[256,128]{1,0:T(8,128)(2,1)S(1)} %bitcast.9, bf16[16,128]{1,0:T(8,128)(2,1)S(1)} %bitcast.12, ...), custom_call_target="tpu_custom_call" | custom-call | flops 134217728 | bytes 8388608 | tf_op jit(solution)/shard_map/project/pallas_call | solution.py:214
  41.8 0.0 copy-start
  41.8 0.0 copy-start.2
  41.9 0.0 copy-start.6
  41.9 0.0 copy-start.10
  41.9 3.6 %collective-permute-start = (bf16[16,768]{1,0:T(8,128)(2,1)S(1)}, bf16[16,768]{1,0:T(8,128)(2,1)S(1)}, u32[]{:S(2)}, u32[]{:S(2)}) collective-permute-start(bf16[16,768]{1,0:T(8,128)(2,1)S(1)} %get-tuple-element.19), channel_id=1, source_target_pairs={{0,1},{1,0},{2,3},{3,2},{4,5},{5,4},{6,7},{7,6},{8,9},{9,8},{10,11... | collective-permute-start | bytes 73736 | tf_op jit(solution)/shard_map/ppermute | solution.py:546
  45.5 0.3 collective-permute-start.1
  45.8 1.4 %collective-permute-start.2 = (bf16[16,768]{1,0:T(8,128)(2,1)S(1)}, bf16[16,768]{1,0:T(8,128)(2,1)S(1)}, u32[]{:S(2)}, u32[]{:S(2)}) collective-permute-start(bf16[16,768]{1,0:T(8,128)(2,1)S(1)} %get-tuple-element.21), channel_id=1, source_target_pairs={{0,3},{1,2},{2,1},{3,0},{4,7},{5,6},{6,5},{7,4},{8,11},{9,10},{10,... | collective-permute-start | bytes 73736 | tf_op jit(solution)/shard_map/ppermute | solution.py:546
  47.2 0.0 copy-done.1
  47.2 0.0 copy-done.9
  47.2 1.4 %policy_scores.1 = (f32[8,32,1024]{2,1,0:T(8,128)S(1)}, f32[8,32,128]{2,1,0:T(8,128)S(1)}) custom-call(s32[4]{0:T(128)S(1)} %copy-done.9, bf16[8,32,128]{2,1,0:T(8,128)(2,1)S(1)} %get-tuple-element.22.query_ref, bf16[4,1024,256]{2,1,0:T(8,128)(2,1)S(1)} %copy-done.1), custom_call_target="tpu_custom_call" | custom-call | flops 67108864 | bytes 3145728 | tf_op jit(solution)/shard_map/policy_scores/pallas_call | solution.py:256
  48.6 0.0 copy-start.3
  48.6 0.0 copy-start.4
  48.6 0.0 copy-start.7
  48.6 0.0 collective-permute-done.one_ref
  48.7 0.0 collective-permute-done.1.two_ref
  48.7 0.6 collective-permute-done.2.three_ref
  49.3 0.0 copy-done
  49.3 1.2 %policy.1 = (bf16[16,2048]{1,0:T(8,128)(2,1)S(1)}, f32[16,128]{1,0:T(8,128)S(1)}) custom-call(f32[16,640]{1,0:T(8,128)S(1)} %get-tuple-element.18.own_ref, bf16[16,768]{1,0:T(8,128)(2,1)S(1)} %collective-permute-done.one_ref, bf16[16,768]{1,0:T(8,128)(2,1)S(1)} %collective-permute-done.1.two_ref, bf16[16,768]{1,0:T(8,128)(2,1)S(1)} %collective-permute-done.2.three_ref, ...), custom_call_target="tpu_custom_call" | custom-call | flops 67108864 | bytes 3145728 | tf_op jit(solution)/shard_map/policy/pallas_call | solution.py:368
  50.5 1.0 %collective-permute-start.3 = (bf16[16,2048]{1,0:T(8,128)(2,1)S(1)}, bf16[16,2048]{1,0:T(8,128)(2,1)S(1)}, u32[]{:S(2)}, u32[]{:S(2)}) collective-permute-start(bf16[16,2048]{1,0:T(8,128)(2,1)S(1)} %get-tuple-element.26.rows_ref), channel_id=1, source_target_pairs={{0,64},{4,68},{8,72},{12,76},{16,80},{20,84},{24,88},{28,92},{32,9... | collective-permute-start | bytes 196616 | tf_op jit(solution)/shard_map/ppermute | solution.py:551
  51.5 2.6 %collective-permute-start.4 = (f32[16,128]{1,0:T(8,128)S(1)}, f32[16,128]{1,0:T(8,128)S(1)}, u32[]{:S(2)}, u32[]{:S(2)}) collective-permute-start(f32[16,128]{1,0:T(8,128)S(1)} %get-tuple-element.27), channel_id=1, source_target_pairs={{0,66},{1,67},{2,64},{3,65},{4,70},{5,71},{6,68},{7,69},{8,74},{9,... | collective-permute-start | bytes 24584 | tf_op jit(solution)/shard_map/ppermute | solution.py:562
  54.1 1.0 %collective-permute-done.3.rows_ref = bf16[16,2048]{1,0:T(8,128)(2,1)S(1)} collective-permute-done((bf16[16,2048]{1,0:T(8,128)(2,1)S(1)}, bf16[16,2048]{1,0:T(8,128)(2,1)S(1)}, u32[]{:S(2)}, u32[]{:S(2)}) %collective-permute-start.3) | collective-permute-done | bytes 65568 | tf_op jit(solution)/shard_map/ppermute | solution.py:551
  55.1 0.0 copy-done.2
  55.1 0.0 copy-done.6
  55.1 0.0 copy-done.10
  55.1 1.5 %critic_scores.1 = (f32[8,32,1024]{2,1,0:T(8,128)S(1)}, f32[8,32,128]{2,1,0:T(8,128)S(1)}) custom-call(s32[4]{0:T(128)S(1)} %copy-done.10, bf16[16,2048]{1,0:T(8,128)(2,1)S(1)} %collective-permute-done.3.rows_ref, bf16[16,128]{1,0:T(8,128)(2,1)S(1)} %bitcast.13, bf16[4,1024,256]{2,1,0:T(8,128)(2,1)S(1)} %copy-done.2), custom_call_target="tpu_custom_call" | custom-call | flops 67108864 | bytes 3145728 | tf_op jit(solution)/shard_map/critic_scores/pallas_call | solution.py:441
  56.6 0.0 collective-permute-done.4.other_ref
  56.6 0.1 row_squares.1.near_ref
  56.7 1.6 %collective-permute-start.5 = (f32[16,128]{1,0:T(8,128)S(1)}, f32[16,128]{1,0:T(8,128)S(1)}, u32[]{:S(2)}, u32[]{:S(2)}) collective-permute-start(f32[16,128]{1,0:T(8,128)S(1)} %row_squares.1.near_ref), channel_id=1, source_target_pairs={{0,1},{1,0},{2,3},{3,2},{4,5},{5,4},{6,7},{7,6},{8,9},{9,8},{10,11... | collective-permute-start | bytes 24584 | tf_op jit(solution)/shard_map/ppermute | solution.py:546
  58.3 0.8 %collective-permute-done.5.far_ref = f32[16,128]{1,0:T(8,128)S(1)} collective-permute-done((f32[16,128]{1,0:T(8,128)S(1)}, f32[16,128]{1,0:T(8,128)S(1)}, u32[]{:S(2)}, u32[]{:S(2)}) %collective-permute-start.5) | collective-permute-done | bytes 8224 | tf_op jit(solution)/shard_map/ppermute | solution.py:546
  59.1 0.0 copy-done.3
  59.1 0.0 copy-done.4
  59.1 0.0 copy-done.7
  59.1 0.8 %critic.1.own_ref = f32[16,128]{1,0:T(8,128)S(1)} custom-call(f32[16,128]{1,0:T(8,128)S(1)} %row_squares.1.near_ref, f32[16,128]{1,0:T(8,128)S(1)} %collective-permute-done.5.far_ref, f32[8,32,1024]{2,1,0:T(8,128)S(1)} %get-tuple-element.29.raw_ref, f32[8,32,128]{2,1,0:T(8,128)S(1)} %get-tuple-element.28._.top_ref, ...), custom_call_target="tpu_custom_call" | custom-call | flops 67108864 | bytes 3145728 | tf_op jit(solution)/shard_map/critic/pallas_call | solution.py:505
  59.9 1.2 %collective-permute-start.8 = (f32[16,128]{1,0:T(8,128)S(1)}, f32[16,128]{1,0:T(8,128)S(1)}, u32[]{:S(2)}, u32[]{:S(2)}) collective-permute-start(f32[16,128]{1,0:T(8,128)S(1)} %critic.1.own_ref), channel_id=1, source_target_pairs={{0,3},{1,2},{2,1},{3,0},{4,7},{5,6},{6,5},{7,4},{8,11},{9,10},{10,... | collective-permute-start | bytes 24584 | tf_op jit(solution)/shard_map/ppermute | solution.py:546
  61.1 0.6 collective-permute-start.7
  61.7 0.4 collective-permute-start.6
  62.1 0.7 %by_step.1 = bf16[4,4,2048]{2,1,0:T(4,128)(2,1)} custom-call(bf16[16,2048]{1,0:T(8,128)(2,1)S(1)} %get-tuple-element.26.rows_ref), custom_call_target="tpu_custom_call" | custom-call | bytes 524288 | tf_op jit(solution)/shard_map/by_step/pallas_call | solution.py:394
  62.8 0.3 collective-permute-done.8.three_ref
  63.1 0.5 collective-permute-done.7.two_ref
  63.6 0.0 collective-permute-done.6.one_ref
  63.6 0.8 %expect.1 = f32[4,4]{1,0:T(4,128)} custom-call(f32[16,128]{1,0:T(8,128)S(1)} %critic.1.own_ref, f32[16,128]{1,0:T(8,128)S(1)} %collective-permute-done.6.one_ref, f32[16,128]{1,0:T(8,128)S(1)} %collective-permute-done.7.two_ref, f32[16,128]{1,0:T(8,128)S(1)} %collective-permute-done.8.three_ref), custom_call_target="tpu_custom_call" | custom-call | tf_op jit(solution)/shard_map/expect/pallas_call | solution.py:541
Async XLA Ops:
  0.6 0.7 %copy-start.8 = (s32[4,4]{1,0:T(4,128)S(1)}, s32[4,4]{1,0:T(4,128)}, u32[]{:S(2)}) copy-start(s32[4,4]{1,0:T(4,128)} %token_ref.1) | copy-start | bytes 196
  21.2 17.7 %copy-start.5 = (bf16[2048]{0:T(1024)(128)(2,1)S(1)}, bf16[2048]{0:T(1024)(128)(2,1)}, u32[]{:S(2)}) copy-start(bf16[2048]{0:T(1024)(128)(2,1)} %param.17) | copy-start | bytes 12292
  38.9 8.3 %copy-start.1 = (bf16[4,1024,256]{2,1,0:T(8,128)(2,1)S(1)}, bf16[4,1024,256]{2,1,0:T(8,128)(2,1)}, u32[]{:S(2)}) copy-start(bf16[4,1024,256]{2,1,0:T(8,128)(2,1)} %keys_ref.2) | copy-start | bytes 6291460
  38.9 8.3 %copy-start.9 = (s32[4]{0:T(128)S(1)}, s32[4]{0:T(128)}, u32[]{:S(2)}) copy-start(s32[4]{0:T(128)} %length_ref.2) | copy-start | bytes 52
  41.8 7.4 %copy-start = (bf16[4,1024,256]{2,1,0:T(8,128)(2,1)S(1)}, bf16[4,1024,256]{2,1,0:T(8,128)(2,1)}, u32[]{:S(2)}) copy-start(bf16[4,1024,256]{2,1,0:T(8,128)(2,1)} %values_ref.2) | copy-start | bytes 6291460
  41.8 13.3 %copy-start.2 = (bf16[4,1024,256]{2,1,0:T(8,128)(2,1)S(1)}, bf16[4,1024,256]{2,1,0:T(8,128)(2,1)}, u32[]{:S(2)}) copy-start(bf16[4,1024,256]{2,1,0:T(8,128)(2,1)} %keys_ref.3) | copy-start | bytes 6291460
  41.9 13.3 %copy-start.6 = (bf16[2048]{0:T(1024)(128)(2,1)S(1)}, bf16[2048]{0:T(1024)(128)(2,1)}, u32[]{:S(2)}) copy-start(bf16[2048]{0:T(1024)(128)(2,1)} %param.23) | copy-start | bytes 12292
  41.9 13.2 %copy-start.10 = (s32[4]{0:T(128)S(1)}, s32[4]{0:T(128)}, u32[]{:S(2)}) copy-start(s32[4]{0:T(128)} %length_ref.3) | copy-start | bytes 52
  41.9 6.8 %collective-permute-start = (bf16[16,768]{1,0:T(8,128)(2,1)S(1)}, bf16[16,768]{1,0:T(8,128)(2,1)S(1)}, u32[]{:S(2)}, u32[]{:S(2)}) collective-permute-start(bf16[16,768]{1,0:T(8,128)(2,1)S(1)} %get-tuple-element.19), channel_id=1, source_target_pairs={{0,1},{1,0},{2,3},{3,2},{4,5},{5,4},{6,7},{7,6},{8,9},{9,8},{10,11... | collective-permute-start | bytes 73736 | tf_op jit(solution)/shard_map/ppermute | solution.py:546
  45.5 3.2 %collective-permute-start.1 = (bf16[16,768]{1,0:T(8,128)(2,1)S(1)}, bf16[16,768]{1,0:T(8,128)(2,1)S(1)}, u32[]{:S(2)}, u32[]{:S(2)}) collective-permute-start(bf16[16,768]{1,0:T(8,128)(2,1)S(1)} %get-tuple-element.20), channel_id=1, source_target_pairs={{0,2},{1,3},{2,0},{3,1},{4,6},{5,7},{6,4},{7,5},{8,10},{9,11},{10,... | collective-permute-start | bytes 73736 | tf_op jit(solution)/shard_map/ppermute | solution.py:546
  45.8 3.5 %collective-permute-start.2 = (bf16[16,768]{1,0:T(8,128)(2,1)S(1)}, bf16[16,768]{1,0:T(8,128)(2,1)S(1)}, u32[]{:S(2)}, u32[]{:S(2)}) collective-permute-start(bf16[16,768]{1,0:T(8,128)(2,1)S(1)} %get-tuple-element.21), channel_id=1, source_target_pairs={{0,3},{1,2},{2,1},{3,0},{4,7},{5,6},{6,5},{7,4},{8,11},{9,10},{10,... | collective-permute-start | bytes 73736 | tf_op jit(solution)/shard_map/ppermute | solution.py:546
  48.6 10.5 %copy-start.3 = (bf16[4,1024,256]{2,1,0:T(8,128)(2,1)S(1)}, bf16[4,1024,256]{2,1,0:T(8,128)(2,1)}, u32[]{:S(2)}) copy-start(bf16[4,1024,256]{2,1,0:T(8,128)(2,1)} %values_ref.3) | copy-start | bytes 6291460
  48.6 10.5 %copy-start.4 = (bf16[2048,51]{0,1:T(8,128)(2,1)S(1)}, bf16[2048,51]{0,1:T(8,128)(2,1)}, u32[]{:S(2)}) copy-start(bf16[2048,51]{0,1:T(8,128)(2,1)} %param.27) | copy-start | bytes 626692
  48.6 10.5 %copy-start.7 = (bf16[2048]{0:T(1024)(128)(2,1)S(1)}, bf16[2048]{0:T(1024)(128)(2,1)}, u32[]{:S(2)}) copy-start(bf16[2048]{0:T(1024)(128)(2,1)} %param.26) | copy-start | bytes 12292
  50.5 4.6 %collective-permute-start.3 = (bf16[16,2048]{1,0:T(8,128)(2,1)S(1)}, bf16[16,2048]{1,0:T(8,128)(2,1)S(1)}, u32[]{:S(2)}, u32[]{:S(2)}) collective-permute-start(bf16[16,2048]{1,0:T(8,128)(2,1)S(1)} %get-tuple-element.26.rows_ref), channel_id=1, source_target_pairs={{0,64},{4,68},{8,72},{12,76},{16,80},{20,84},{24,88},{28,92},{32,9... | collective-permute-start | bytes 196616 | tf_op jit(solution)/shard_map/ppermute | solution.py:551
  51.5 5.1 %collective-permute-start.4 = (f32[16,128]{1,0:T(8,128)S(1)}, f32[16,128]{1,0:T(8,128)S(1)}, u32[]{:S(2)}, u32[]{:S(2)}) collective-permute-start(f32[16,128]{1,0:T(8,128)S(1)} %get-tuple-element.27), channel_id=1, source_target_pairs={{0,66},{1,67},{2,64},{3,65},{4,70},{5,71},{6,68},{7,69},{8,74},{9,... | collective-permute-start | bytes 24584 | tf_op jit(solution)/shard_map/ppermute | solution.py:562
  56.7 2.5 %collective-permute-start.5 = (f32[16,128]{1,0:T(8,128)S(1)}, f32[16,128]{1,0:T(8,128)S(1)}, u32[]{:S(2)}, u32[]{:S(2)}) collective-permute-start(f32[16,128]{1,0:T(8,128)S(1)} %row_squares.1.near_ref), channel_id=1, source_target_pairs={{0,1},{1,0},{2,3},{3,2},{4,5},{5,4},{6,7},{7,6},{8,9},{9,8},{10,11... | collective-permute-start | bytes 24584 | tf_op jit(solution)/shard_map/ppermute | solution.py:546
  59.9 3.1 %collective-permute-start.8 = (f32[16,128]{1,0:T(8,128)S(1)}, f32[16,128]{1,0:T(8,128)S(1)}, u32[]{:S(2)}, u32[]{:S(2)}) collective-permute-start(f32[16,128]{1,0:T(8,128)S(1)} %critic.1.own_ref), channel_id=1, source_target_pairs={{0,3},{1,2},{2,1},{3,0},{4,7},{5,6},{6,5},{7,4},{8,11},{9,10},{10,... | collective-permute-start | bytes 24584 | tf_op jit(solution)/shard_map/ppermute | solution.py:546
  61.1 2.5 %collective-permute-start.7 = (f32[16,128]{1,0:T(8,128)S(1)}, f32[16,128]{1,0:T(8,128)S(1)}, u32[]{:S(2)}, u32[]{:S(2)}) collective-permute-start(f32[16,128]{1,0:T(8,128)S(1)} %critic.1.own_ref), channel_id=1, source_target_pairs={{0,2},{1,3},{2,0},{3,1},{4,6},{5,7},{6,4},{7,5},{8,10},{9,11},{10,... | collective-permute-start | bytes 24584 | tf_op jit(solution)/shard_map/ppermute | solution.py:546
  61.7 1.9 %collective-permute-start.6 = (f32[16,128]{1,0:T(8,128)S(1)}, f32[16,128]{1,0:T(8,128)S(1)}, u32[]{:S(2)}, u32[]{:S(2)}) collective-permute-start(f32[16,128]{1,0:T(8,128)S(1)} %critic.1.own_ref), channel_id=1, source_target_pairs={{0,1},{1,0},{2,3},{3,2},{4,5},{5,4},{6,7},{7,6},{8,9},{9,8},{10,11... | collective-permute-start | bytes 24584 | tf_op jit(solution)/shard_map/ppermute | solution.py:546

commit v8 on v7

--- a/solution.py
+++ b/solution.py
@@ -401,21 +401,26 @@
     )(rows)
 
 
-def squares_kernel(rows_ref, other_ref, _, out_ref):
+def add_kernel(one_ref, two_ref, out_ref):
+    out_ref[...] = one_ref[...] + two_ref[...]
+
+
+def added(one, two):
+    return kernel_call(add_kernel, array(one.shape, one.dtype), [VMEM] * 2, name="add")(one, two)
+
+
+def squares_kernel(rows_ref, out_ref):
     squares = jnp.zeros(out_ref.shape, jnp.float32)
     for k in range(rows_ref.shape[1] // LANES):
         part = rows_ref[:, pl.ds(k * LANES, LANES)].astype(jnp.float32)
         squares += part * part
-    out_ref[...] = other_ref[...] + jnp.sum(squares, axis=1, keepdims=True)
-
-
-def row_squares(rows, other, after):
+    out_ref[...] = jnp.broadcast_to(jnp.sum(squares, axis=1, keepdims=True), out_ref.shape)
+
+
+def row_squares(rows):
     return kernel_call(
-        squares_kernel,
-        array(other.shape, jnp.float32),
-        [VMEM, VMEM, pl.BlockSpec(memory_space=pl.ANY)],
-        name="row_squares",
-    )(rows, other, after)
+        squares_kernel, array((rows.shape[0], LANES), jnp.float32), [VMEM], name="row_squares"
+    )(rows)
 
 
 def critic_scores_kernel(
@@ -450,6 +455,7 @@
 
 
 def critic_kernel(
+    own_ref,
     near_ref,
     far_ref,
     raw_ref,
@@ -465,7 +471,8 @@
 ):
     count, width = rows_ref.shape
     cache_size = values_ref.shape[1]
-    inv = lax.rsqrt((near_ref[...] + far_ref[...]) * (1.0 / D) + norm_eps)
+    total = (own_ref[...] + near_ref[...]) + far_ref[...]
+    inv = lax.rsqrt(total * (1.0 / D) + norm_eps)
     spread_rows(inv * (attn_scale * log2_e / shrink), spread_ref)
     for at in range(raw_ref.shape[0]):
         head, row = divmod(at, 4)
@@ -505,7 +512,7 @@
     return kernel_call(
         critic_kernel,
         array((count, LANES), jnp.float32),
-        [VMEM] * 8,
+        [VMEM] * 9,
         scratch=[
             pltpu.VMEM((4, 4 * GROUP, LANES), jnp.float32),
             pltpu.VMEM((width // LANES, count, LANES), jnp.float32),
@@ -598,13 +605,13 @@
     raw, top = policy_scores(lengths, query, policy_keys)
     passed, squares = policy(arrived, raw, top, query, x, policy_values)
     rows = passed_along(passed, "rows", row_groups // 2)
-    squares = crossed(squares, row_groups // 2, 2)
+    far = crossed(added(squares, swapped(squares, 1)), row_groups // 2, 2)
     hidden = by_step(passed)
 
     raw, top = critic_scores(critic_lengths, rows, as_rows(critic_gain), critic_keys)
-    near = row_squares(rows, squares, top)
+    own = row_squares(rows)
     logits = critic(
-        (near, swapped(near, 1)),
+        (own, swapped(own, 1), far),
         raw,
         top,
         rows,

time: 64.6 us -> 64.6 us (level)
    ppermute x1, waiting for transfers between devices: 1.01 us -> 0.01 us  [passed_along(): lax.ppermute(shard, axis, [(i, (i + by) % peers) for i in range(peers)])]
    ppermute x7 -> x8, waiting for transfers between devices: 2.24 us -> 2.8 us  [swapped(): return lax.ppermute(shard, 'tp', [(i, i ^ by) for i in range(peers)])]
    ppermute x7 -> x8, starting transfers between devices: 9.11 us -> 9.6 us  [swapped(): return lax.ppermute(shard, 'tp', [(i, i ^ by) for i in range(peers)])]
  transfers between devices with their start and end apart: 9 -> 10, of which waited for: 5 -> 4; matrix products, arithmetic and copies ran while one was open for 0% -> 0% of each run, Pallas kernels for 6% -> 6%
where the time goes in v8:
time: 64.6 us; the launch traced here: 64.4 us
  blocking collectives  31.7 us (49%)
  Pallas kernels  15.3 us (24%)
  starting transfers between devices  13.2 us (20%)
  waiting for transfers between devices  2.81 us (4%)
  between operations  0.76 us (1%)
  local copies, waits for them, and re-layouts  0.72 us (1%)
    all_to_all x1, blocking collectives, on_device(): all_tokens = lax.all_to_all(laid_out(tokens, row_groups), 'rows', 0, 0)  19.8 us
    all_to_all x1, blocking collectives, on_device(): blocks = lax.all_to_all(picked.reshape(row_groups, -1, LANES), 'rows', 0, 0)  11.9 us
    ppermute x8, starting transfers between devices, swapped(): return lax.ppermute(shard, 'tp', [(i, i ^ by) for i in range(peers)])  9.6 us
    pallas_call x1, Pallas kernels, pick_rows(): kernel_call(pick_rows_kernel, (array((rows, LANES), table.dtype), pltpu.V...  5.78 us
    pallas_call x1, Pallas kernels, project(): kernel_call(project_kernel, (array((count, width), jnp.bfloat16), array(q...  2.94 us
    ppermute x8, waiting for transfers between devices, swapped(): return lax.ppermute(shard, 'tp', [(i, i ^ by) for i in range(peers)])  2.8 us
    ppermute x1, starting transfers between devices, crossed(): return lax.ppermute(shard, ('rows', 'tp'), pairs)  2.58 us
    pallas_call x1, Pallas kernels, critic_scores(): kernel_call(critic_scores_kernel, (raw, array(placed, jnp.float32)), [SME...  1.45 us
  transfers between devices with their start and end apart: 10, of which 4 were waited for; matrix products, arithmetic and copies ran while one was open for 0% of the time, Pallas kernels for 6%

profile of v8, /device:TPU:1, one launch (start us, length us, event | category | flops | bytes accessed | tf_op | source)
XLA Modules:
  0.0 64.4 jit_solution(300089078856298179)
XLA Ops:
  0.6 0.0 copy-start.8
  0.6 0.7 %copy-done.8 = s32[4,4]{1,0:T(4,128)S(1)} copy-done((s32[4,4]{1,0:T(4,128)S(1)}, s32[4,4]{1,0:T(4,128)}, u32[]{:S(2)}) %copy-start.8) | copy-done | bytes 88
  1.3 0.1 lay_out.1
  1.4 19.8 %all_to_all.10.token_ref = s32[32,1,16]{2,1,0:T(1,128)S(1)} all-to-all(s32[32,1,16]{2,1,0:T(1,128)S(1)} %lay_out.1), channel_id=1, replica_groups=mesh['rows'=32,'tp'=4] {'rows'}, dimensions={0} | all-to-all | bytes 4096 | tf_op jit(solution)/shard_map/all_to_all | solution.py:598
  21.2 0.0 copy-start.5
  21.2 5.8 %pick_rows.1 = (bf16[256,128]{1,0:T(8,128)(2,1)S(1)}, bf16[1536,1024]{1,0:T(8,128)(2,1)S(1)}) custom-call(s32[32,1,16]{2,1,0:T(1,128)S(1)} %all_to_all.10.token_ref, bf16[64,76032]{1,0:T(8,128)(2,1)} %bitcast.15, bf16[2048,1024]{1,0:T(8,128)(2,1)} %value_ref.1), custom_call_target="tpu_custom_call" | custom-call | tf_op jit(solution)/shard_map/pick_rows/pallas_call | solution.py:128
  27.0 11.9 %all_to_all.11 = bf16[32,8,128]{2,1,0:T(8,128)(2,1)S(1)} all-to-all(bf16[32,8,128]{2,1,0:T(8,128)(2,1)S(1)} %bitcast.11), channel_id=1, replica_groups=mesh['rows'=32,'tp'=4] {'rows'}, dimensions={0} | all-to-all | bytes 131072 | tf_op jit(solution)/shard_map/all_to_all | solution.py:600
  38.9 0.0 copy-done.5
  38.9 0.0 copy-start.1
  38.9 0.0 copy-start.9
  38.9 2.9 %project.1 = (bf16[16,2048]{1,0:T(8,128)(2,1)S(1)}, bf16[8,32,128]{2,1,0:T(8,128)(2,1)S(1)}, f32[16,640]{1,0:T(8,128)S(1)}, bf16[16,768]{1,0:T(8,128)(2,1)S(1)},...) custom-call(bf16[256,128]{1,0:T(8,128)(2,1)S(1)} %bitcast.9, bf16[16,128]{1,0:T(8,128)(2,1)S(1)} %bitcast.12, ...), custom_call_target="tpu_custom_call" | custom-call | flops 134217728 | bytes 8388608 | tf_op jit(solution)/shard_map/project/pallas_call | solution.py:214
  41.8 0.0 copy-start
  41.8 0.0 copy-start.2
  41.9 0.0 copy-start.6
  41.9 0.0 copy-start.10
  41.9 3.6 %collective-permute-start = (bf16[16,768]{1,0:T(8,128)(2,1)S(1)}, bf16[16,768]{1,0:T(8,128)(2,1)S(1)}, u32[]{:S(2)}, u32[]{:S(2)}) collective-permute-start(bf16[16,768]{1,0:T(8,128)(2,1)S(1)} %get-tuple-element.19), channel_id=1, source_target_pairs={{0,1},{1,0},{2,3},{3,2},{4,5},{5,4},{6,7},{7,6},{8,9},{9,8},{10,11... | collective-permute-start | bytes 73736 | tf_op jit(solution)/shard_map/ppermute | solution.py:553
  45.5 0.3 collective-permute-start.1
  45.8 1.4 %collective-permute-start.2 = (bf16[16,768]{1,0:T(8,128)(2,1)S(1)}, bf16[16,768]{1,0:T(8,128)(2,1)S(1)}, u32[]{:S(2)}, u32[]{:S(2)}) collective-permute-start(bf16[16,768]{1,0:T(8,128)(2,1)S(1)} %get-tuple-element.21), channel_id=1, source_target_pairs={{0,3},{1,2},{2,1},{3,0},{4,7},{5,6},{6,5},{7,4},{8,11},{9,10},{10,... | collective-permute-start | bytes 73736 | tf_op jit(solution)/shard_map/ppermute | solution.py:553
  47.2 0.0 copy-done.1
  47.2 0.0 copy-done.9
  47.2 1.4 %policy_scores.1 = (f32[8,32,1024]{2,1,0:T(8,128)S(1)}, f32[8,32,128]{2,1,0:T(8,128)S(1)}) custom-call(s32[4]{0:T(128)S(1)} %copy-done.9, bf16[8,32,128]{2,1,0:T(8,128)(2,1)S(1)} %get-tuple-element.22.query_ref, bf16[4,1024,256]{2,1,0:T(8,128)(2,1)S(1)} %copy-done.1), custom_call_target="tpu_custom_call" | custom-call | flops 67108864 | bytes 3145728 | tf_op jit(solution)/shard_map/policy_scores/pallas_call | solution.py:256
  48.6 0.0 copy-start.3
  48.6 0.0 copy-start.4
  48.6 0.0 copy-start.7
  48.6 0.0 collective-permute-done.one_ref
  48.7 0.0 collective-permute-done.1.two_ref
  48.7 0.6 collective-permute-done.2.three_ref
  49.3 0.0 copy-done
  49.3 1.2 %policy.1 = (bf16[16,2048]{1,0:T(8,128)(2,1)S(1)}, f32[16,128]{1,0:T(8,128)S(1)}) custom-call(f32[16,640]{1,0:T(8,128)S(1)} %get-tuple-element.18.own_ref, bf16[16,768]{1,0:T(8,128)(2,1)S(1)} %collective-permute-done.one_ref, bf16[16,768]{1,0:T(8,128)(2,1)S(1)} %collective-permute-done.1.two_ref, bf16[16,768]{1,0:T(8,128)(2,1)S(1)} %collective-permute-done.2.three_ref, ...), custom_call_target="tpu_custom_call" | custom-call | flops 67108864 | bytes 3145728 | tf_op jit(solution)/shard_map/policy/pallas_call | solution.py:368
  50.5 1.0 %collective-permute-start.3 = (bf16[16,2048]{1,0:T(8,128)(2,1)S(1)}, bf16[16,2048]{1,0:T(8,128)(2,1)S(1)}, u32[]{:S(2)}, u32[]{:S(2)}) collective-permute-start(bf16[16,2048]{1,0:T(8,128)(2,1)S(1)} %get-tuple-element.26.rows_ref), channel_id=1, source_target_pairs={{0,64},{4,68},{8,72},{12,76},{16,80},{20,84},{24,88},{28,92},{32,9... | collective-permute-start | bytes 196616 | tf_op jit(solution)/shard_map/ppermute | solution.py:558
  51.5 0.7 %collective-permute-start.5 = (f32[16,128]{1,0:T(8,128)S(1)}, f32[16,128]{1,0:T(8,128)S(1)}, u32[]{:S(2)}, u32[]{:S(2)}) collective-permute-start(f32[16,128]{1,0:T(8,128)S(1)} %get-tuple-element.27.one_ref), channel_id=1, source_target_pairs={{0,1},{1,0},{2,3},{3,2},{4,5},{5,4},{6,7},{7,6},{8,9},{9,8},{10,11... | collective-permute-start | bytes 24584 | tf_op jit(solution)/shard_map/ppermute | solution.py:553
  52.2 0.8 %collective-permute-done.5.two_ref = f32[16,128]{1,0:T(8,128)S(1)} collective-permute-done((f32[16,128]{1,0:T(8,128)S(1)}, f32[16,128]{1,0:T(8,128)S(1)}, u32[]{:S(2)}, u32[]{:S(2)}) %collective-permute-start.5) | collective-permute-done | bytes 8224 | tf_op jit(solution)/shard_map/ppermute | solution.py:553
  53.0 2.6 %collective-permute-start.6 = (f32[16,128]{1,0:T(8,128)S(1)}, f32[16,128]{1,0:T(8,128)S(1)}, u32[]{:S(2)}, u32[]{:S(2)}) collective-permute-start(f32[16,128]{1,0:T(8,128)S(1)} %add.1), channel_id=1, source_target_pairs={{0,66},{1,67},{2,64},{3,65},{4,70},{5,71},{6,68},{7,69},{8,74},{9,... | collective-permute-start | bytes 24584 | tf_op jit(solution)/shard_map/ppermute | solution.py:569
  55.6 0.0 collective-permute-done.3.rows_ref
  55.6 0.1 row_squares.1.own_ref
  55.7 1.1 %collective-permute-start.4 = (f32[16,128]{1,0:T(8,128)S(1)}, f32[16,128]{1,0:T(8,128)S(1)}, u32[]{:S(2)}, u32[]{:S(2)}) collective-permute-start(f32[16,128]{1,0:T(8,128)S(1)} %row_squares.1.own_ref), channel_id=1, source_target_pairs={{0,1},{1,0},{2,3},{3,2},{4,5},{5,4},{6,7},{7,6},{8,9},{9,8},{10,11... | collective-permute-start | bytes 24584 | tf_op jit(solution)/shard_map/ppermute | solution.py:553
  56.8 0.0 copy-done.2
  56.8 0.0 copy-done.6
  56.8 0.0 copy-done.10
  56.8 1.5 %critic_scores.1 = (f32[8,32,1024]{2,1,0:T(8,128)S(1)}, f32[8,32,128]{2,1,0:T(8,128)S(1)}) custom-call(s32[4]{0:T(128)S(1)} %copy-done.10, bf16[16,2048]{1,0:T(8,128)(2,1)S(1)} %collective-permute-done.3.rows_ref, bf16[16,128]{1,0:T(8,128)(2,1)S(1)} %bitcast.13, bf16[4,1024,256]{2,1,0:T(8,128)(2,1)S(1)} %copy-done.2), custom_call_target="tpu_custom_call" | custom-call | flops 67108864 | bytes 3145728 | tf_op jit(solution)/shard_map/critic_scores/pallas_call | solution.py:446
  58.2 0.0 collective-permute-done.6.far_ref
  58.2 0.0 collective-permute-done.4.near_ref
  58.2 0.0 copy-done.3
  58.2 0.0 copy-done.4
  58.2 0.0 copy-done.7
  58.3 0.8 %critic.1.own_ref = f32[16,128]{1,0:T(8,128)S(1)} custom-call(f32[16,128]{1,0:T(8,128)S(1)} %row_squares.1.own_ref, f32[16,128]{1,0:T(8,128)S(1)} %collective-permute-done.4.near_ref, f32[16,128]{1,0:T(8,128)S(1)} %collective-permute-done.6.far_ref, f32[8,32,1024]{2,1,0:T(8,128)S(1)} %get-tuple-element.28.raw_ref, ...), custom_call_target="tpu_custom_call" | custom-call | flops 67108864 | bytes 3145728 | tf_op jit(solution)/shard_map/critic/pallas_call | solution.py:512
  59.0 1.9 %collective-permute-start.9 = (f32[16,128]{1,0:T(8,128)S(1)}, f32[16,128]{1,0:T(8,128)S(1)}, u32[]{:S(2)}, u32[]{:S(2)}) collective-permute-start(f32[16,128]{1,0:T(8,128)S(1)} %critic.1.own_ref), channel_id=1, source_target_pairs={{0,3},{1,2},{2,1},{3,0},{4,7},{5,6},{6,5},{7,4},{8,11},{9,10},{10,... | collective-permute-start | bytes 24584 | tf_op jit(solution)/shard_map/ppermute | solution.py:553
  61.0 0.6 collective-permute-start.8
  61.6 0.0 collective-permute-start.7
  61.6 0.7 %by_step.1 = bf16[4,4,2048]{2,1,0:T(4,128)(2,1)} custom-call(bf16[16,2048]{1,0:T(8,128)(2,1)S(1)} %get-tuple-element.26.rows_ref), custom_call_target="tpu_custom_call" | custom-call | bytes 524288 | tf_op jit(solution)/shard_map/by_step/pallas_call | solution.py:394
  62.2 0.1 collective-permute-done.9.three_ref
  62.3 1.3 %collective-permute-done.8.two_ref = f32[16,128]{1,0:T(8,128)S(1)} collective-permute-done((f32[16,128]{1,0:T(8,128)S(1)}, f32[16,128]{1,0:T(8,128)S(1)}, u32[]{:S(2)}, u32[]{:S(2)}) %collective-permute-start.8) | collective-permute-done | bytes 8224 | tf_op jit(solution)/shard_map/ppermute | solution.py:553
  63.6 0.0 collective-permute-done.7.one_ref
  63.6 0.8 %expect.1 = f32[4,4]{1,0:T(4,128)} custom-call(f32[16,128]{1,0:T(8,128)S(1)} %critic.1.own_ref, f32[16,128]{1,0:T(8,128)S(1)} %collective-permute-done.7.one_ref, f32[16,128]{1,0:T(8,128)S(1)} %collective-permute-done.8.two_ref, f32[16,128]{1,0:T(8,128)S(1)} %collective-permute-done.9.three_ref), custom_call_target="tpu_custom_call" | custom-call | tf_op jit(solution)/shard_map/expect/pallas_call | solution.py:548
  (1 shorter events, 0.0 us)
Async XLA Ops:
  0.6 0.7 %copy-start.8 = (s32[4,4]{1,0:T(4,128)S(1)}, s32[4,4]{1,0:T(4,128)}, u32[]{:S(2)}) copy-start(s32[4,4]{1,0:T(4,128)} %token_ref.1) | copy-start | bytes 196
  21.2 17.7 %copy-start.5 = (bf16[2048]{0:T(1024)(128)(2,1)S(1)}, bf16[2048]{0:T(1024)(128)(2,1)}, u32[]{:S(2)}) copy-start(bf16[2048]{0:T(1024)(128)(2,1)} %param.17) | copy-start | bytes 12292
  38.9 8.3 %copy-start.1 = (bf16[4,1024,256]{2,1,0:T(8,128)(2,1)S(1)}, bf16[4,1024,256]{2,1,0:T(8,128)(2,1)}, u32[]{:S(2)}) copy-start(bf16[4,1024,256]{2,1,0:T(8,128)(2,1)} %keys_ref.2) | copy-start | bytes 6291460
  38.9 8.3 %copy-start.9 = (s32[4]{0:T(128)S(1)}, s32[4]{0:T(128)}, u32[]{:S(2)}) copy-start(s32[4]{0:T(128)} %length_ref.2) | copy-start | bytes 52
  41.8 7.4 %copy-start = (bf16[4,1024,256]{2,1,0:T(8,128)(2,1)S(1)}, bf16[4,1024,256]{2,1,0:T(8,128)(2,1)}, u32[]{:S(2)}) copy-start(bf16[4,1024,256]{2,1,0:T(8,128)(2,1)} %values_ref.2) | copy-start | bytes 6291460
  41.8 14.9 %copy-start.2 = (bf16[4,1024,256]{2,1,0:T(8,128)(2,1)S(1)}, bf16[4,1024,256]{2,1,0:T(8,128)(2,1)}, u32[]{:S(2)}) copy-start(bf16[4,1024,256]{2,1,0:T(8,128)(2,1)} %keys_ref.3) | copy-start | bytes 6291460
  41.9 14.9 %copy-start.6 = (bf16[2048]{0:T(1024)(128)(2,1)S(1)}, bf16[2048]{0:T(1024)(128)(2,1)}, u32[]{:S(2)}) copy-start(bf16[2048]{0:T(1024)(128)(2,1)} %param.23) | copy-start | bytes 12292
  41.9 14.9 %copy-start.10 = (s32[4]{0:T(128)S(1)}, s32[4]{0:T(128)}, u32[]{:S(2)}) copy-start(s32[4]{0:T(128)} %length_ref.3) | copy-start | bytes 52
  41.9 6.8 %collective-permute-start = (bf16[16,768]{1,0:T(8,128)(2,1)S(1)}, bf16[16,768]{1,0:T(8,128)(2,1)S(1)}, u32[]{:S(2)}, u32[]{:S(2)}) collective-permute-start(bf16[16,768]{1,0:T(8,128)(2,1)S(1)} %get-tuple-element.19), channel_id=1, source_target_pairs={{0,1},{1,0},{2,3},{3,2},{4,5},{5,4},{6,7},{7,6},{8,9},{9,8},{10,11... | collective-permute-start | bytes 73736 | tf_op jit(solution)/shard_map/ppermute | solution.py:553
  45.5 3.2 %collective-permute-start.1 = (bf16[16,768]{1,0:T(8,128)(2,1)S(1)}, bf16[16,768]{1,0:T(8,128)(2,1)S(1)}, u32[]{:S(2)}, u32[]{:S(2)}) collective-permute-start(bf16[16,768]{1,0:T(8,128)(2,1)S(1)} %get-tuple-element.20), channel_id=1, source_target_pairs={{0,2},{1,3},{2,0},{3,1},{4,6},{5,7},{6,4},{7,5},{8,10},{9,11},{10,... | collective-permute-start | bytes 73736 | tf_op jit(solution)/shard_map/ppermute | solution.py:553
  45.8 3.5 %collective-permute-start.2 = (bf16[16,768]{1,0:T(8,128)(2,1)S(1)}, bf16[16,768]{1,0:T(8,128)(2,1)S(1)}, u32[]{:S(2)}, u32[]{:S(2)}) collective-permute-start(bf16[16,768]{1,0:T(8,128)(2,1)S(1)} %get-tuple-element.21), channel_id=1, source_target_pairs={{0,3},{1,2},{2,1},{3,0},{4,7},{5,6},{6,5},{7,4},{8,11},{9,10},{10,... | collective-permute-start | bytes 73736 | tf_op jit(solution)/shard_map/ppermute | solution.py:553
  48.6 9.6 %copy-start.3 = (bf16[4,1024,256]{2,1,0:T(8,128)(2,1)S(1)}, bf16[4,1024,256]{2,1,0:T(8,128)(2,1)}, u32[]{:S(2)}) copy-start(bf16[4,1024,256]{2,1,0:T(8,128)(2,1)} %values_ref.3) | copy-start | bytes 6291460
  48.6 9.6 %copy-start.4 = (bf16[2048,51]{0,1:T(8,128)(2,1)S(1)}, bf16[2048,51]{0,1:T(8,128)(2,1)}, u32[]{:S(2)}) copy-start(bf16[2048,51]{0,1:T(8,128)(2,1)} %param.27) | copy-start | bytes 626692
  48.6 9.6 %copy-start.7 = (bf16[2048]{0:T(1024)(128)(2,1)S(1)}, bf16[2048]{0:T(1024)(128)(2,1)}, u32[]{:S(2)}) copy-start(bf16[2048]{0:T(1024)(128)(2,1)} %param.26) | copy-start | bytes 12292
  50.5 5.1 %collective-permute-start.3 = (bf16[16,2048]{1,0:T(8,128)(2,1)S(1)}, bf16[16,2048]{1,0:T(8,128)(2,1)S(1)}, u32[]{:S(2)}, u32[]{:S(2)}) collective-permute-start(bf16[16,2048]{1,0:T(8,128)(2,1)S(1)} %get-tuple-element.26.rows_ref), channel_id=1, source_target_pairs={{0,64},{4,68},{8,72},{12,76},{16,80},{20,84},{24,88},{28,92},{32,9... | collective-permute-start | bytes 196616 | tf_op jit(solution)/shard_map/ppermute | solution.py:558
  51.5 1.5 %collective-permute-start.5 = (f32[16,128]{1,0:T(8,128)S(1)}, f32[16,128]{1,0:T(8,128)S(1)}, u32[]{:S(2)}, u32[]{:S(2)}) collective-permute-start(f32[16,128]{1,0:T(8,128)S(1)} %get-tuple-element.27.one_ref), channel_id=1, source_target_pairs={{0,1},{1,0},{2,3},{3,2},{4,5},{5,4},{6,7},{7,6},{8,9},{9,8},{10,11... | collective-permute-start | bytes 24584 | tf_op jit(solution)/shard_map/ppermute | solution.py:553
  53.0 5.2 %collective-permute-start.6 = (f32[16,128]{1,0:T(8,128)S(1)}, f32[16,128]{1,0:T(8,128)S(1)}, u32[]{:S(2)}, u32[]{:S(2)}) collective-permute-start(f32[16,128]{1,0:T(8,128)S(1)} %add.1), channel_id=1, source_target_pairs={{0,66},{1,67},{2,64},{3,65},{4,70},{5,71},{6,68},{7,69},{8,74},{9,... | collective-permute-start | bytes 24584 | tf_op jit(solution)/shard_map/ppermute | solution.py:569
  55.7 2.6 %collective-permute-start.4 = (f32[16,128]{1,0:T(8,128)S(1)}, f32[16,128]{1,0:T(8,128)S(1)}, u32[]{:S(2)}, u32[]{:S(2)}) collective-permute-start(f32[16,128]{1,0:T(8,128)S(1)} %row_squares.1.own_ref), channel_id=1, source_target_pairs={{0,1},{1,0},{2,3},{3,2},{4,5},{5,4},{6,7},{7,6},{8,9},{9,8},{10,11... | collective-permute-start | bytes 24584 | tf_op jit(solution)/shard_map/ppermute | solution.py:553
  59.0 3.3 %collective-permute-start.9 = (f32[16,128]{1,0:T(8,128)S(1)}, f32[16,128]{1,0:T(8,128)S(1)}, u32[]{:S(2)}, u32[]{:S(2)}) collective-permute-start(f32[16,128]{1,0:T(8,128)S(1)} %critic.1.own_ref), channel_id=1, source_target_pairs={{0,3},{1,2},{2,1},{3,0},{4,7},{5,6},{6,5},{7,4},{8,11},{9,10},{10,... | collective-permute-start | bytes 24584 | tf_op jit(solution)/shard_map/ppermute | solution.py:553
  61.0 2.6 %collective-permute-start.8 = (f32[16,128]{1,0:T(8,128)S(1)}, f32[16,128]{1,0:T(8,128)S(1)}, u32[]{:S(2)}, u32[]{:S(2)}) collective-permute-start(f32[16,128]{1,0:T(8,128)S(1)} %critic.1.own_ref), channel_id=1, source_target_pairs={{0,2},{1,3},{2,0},{3,1},{4,6},{5,7},{6,4},{7,5},{8,10},{9,11},{10,... | collective-permute-start | bytes 24584 | tf_op jit(solution)/shard_map/ppermute | solution.py:553
  61.6 2.0 %collective-permute-start.7 = (f32[16,128]{1,0:T(8,128)S(1)}, f32[16,128]{1,0:T(8,128)S(1)}, u32[]{:S(2)}, u32[]{:S(2)}) collective-permute-start(f32[16,128]{1,0:T(8,128)S(1)} %critic.1.own_ref), channel_id=1, source_target_pairs={{0,1},{1,0},{2,3},{3,2},{4,5},{5,4},{6,7},{7,6},{8,9},{9,8},{10,11... | collective-permute-start | bytes 24584 | tf_op jit(solution)/shard_map/ppermute | solution.py:553

commit v9 on v7

--- a/solution.py
+++ b/solution.py
@@ -61,8 +61,24 @@
 
 
 def pick_rows_kernel(
-    token_ref, table_ref, weight_ref, out_ref, early_ref, tiles_ref, sems, early_sem
+    source_ref,
+    table_ref,
+    weight_ref,
+    out_ref,
+    early_ref,
+    token_ref,
+    tiles_ref,
+    sems,
+    early_sem,
+    token_sem,
 ):
+    early = pltpu.make_async_copy(
+        weight_ref.at[pl.ds(0, early_ref.shape[0])], early_ref, early_sem
+    )
+    early.start()
+    tokens = pltpu.make_async_copy(source_ref, token_ref, token_sem)
+    tokens.start()
+    tokens.wait()
     width = table_ref.shape[0]
     pieces = sems.shape[0]
     destinations = token_ref.shape[0] // pieces
@@ -89,10 +105,6 @@
 
         lax.fori_loop(0, destinations, fetch, 0)
 
-    early = pltpu.make_async_copy(
-        weight_ref.at[pl.ds(0, early_ref.shape[0])], early_ref, early_sem
-    )
-    early.start()
     empty = jnp.zeros((width, LANES), jnp.float32)
     pair = (empty, empty)
     for piece in range(pieces):
@@ -128,10 +140,12 @@
     return kernel_call(
         pick_rows_kernel,
         (array((rows, LANES), table.dtype), pltpu.VMEM(early, weight.dtype)),
-        [SMEM, HBM, HBM],
+        [VMEM, HBM, HBM],
         scratch=[
+            pltpu.SMEM(tokens.shape, tokens.dtype),
             pltpu.VMEM((2, rows, width, LANES), table.dtype),
             pltpu.SemaphoreType.DMA((pieces,)),
+            pltpu.SemaphoreType.DMA,
             pltpu.SemaphoreType.DMA,
         ],
         limit=24,

time: 64.6 us -> 64.4 us (level)
  no operation moved by 1% of the time
where the time goes in v9:
time: 64.4 us; the launch traced here: 64.2 us
  blocking collectives  31.7 us (49%)
  Pallas kernels  15.1 us (23%)
  starting transfers between devices  12.7 us (20%)
  waiting for transfers between devices  3.26 us (5%)
  between operations  0.74 us (1%)
  local copies, waits for them, and re-layouts  0.72 us (1%)
    all_to_all x1, blocking collectives, on_device(): all_tokens = lax.all_to_all(laid_out(tokens, row_groups), 'rows', 0, 0)  19.8 us
    all_to_all x1, blocking collectives, on_device(): blocks = lax.all_to_all(picked.reshape(row_groups, -1, LANES), 'rows', 0, 0)  11.9 us
    ppermute x7, starting transfers between devices, swapped(): return lax.ppermute(shard, 'tp', [(i, i ^ by) for i in range(peers)])  9.11 us
    pallas_call x1, Pallas kernels, pick_rows(): kernel_call(pick_rows_kernel, (array((rows, LANES), table.dtype), pltpu.V...  5.55 us
    pallas_call x1, Pallas kernels, project(): kernel_call(project_kernel, (array((count, width), jnp.bfloat16), array(q...  2.94 us
    ppermute x1, starting transfers between devices, crossed(): return lax.ppermute(shard, ('rows', 'tp'), pairs)  2.62 us
    ppermute x7, waiting for transfers between devices, swapped(): return lax.ppermute(shard, 'tp', [(i, i ^ by) for i in range(peers)])  2.25 us
    pallas_call x1, Pallas kernels, critic_scores(): kernel_call(critic_scores_kernel, (raw, array(placed, jnp.float32)), [SME...  1.45 us
  transfers between devices with their start and end apart: 9, of which 5 were waited for; matrix products, arithmetic and copies ran while one was open for 0% of the time, Pallas kernels for 6%

profile of v9, /device:TPU:1, one launch (start us, length us, event | category | flops | bytes accessed | tf_op | source)
XLA Modules:
  0.0 64.2 jit_solution(14163387495906355361)
XLA Ops:
  0.6 0.0 copy-start.8
  0.6 0.7 %copy-done.8 = s32[4,4]{1,0:T(4,128)S(1)} copy-done((s32[4,4]{1,0:T(4,128)S(1)}, s32[4,4]{1,0:T(4,128)}, u32[]{:S(2)}) %copy-start.8) | copy-done | bytes 88
  1.3 0.1 lay_out.1
  1.4 19.8 %all_to_all.10.source_ref = s32[32,1,16]{2,1,0:T(1,128)S(1)} all-to-all(s32[32,1,16]{2,1,0:T(1,128)S(1)} %lay_out.1), channel_id=1, replica_groups=mesh['rows'=32,'tp'=4] {'rows'}, dimensions={0} | all-to-all | bytes 4096 | tf_op jit(solution)/shard_map/all_to_all | solution.py:605
  21.2 0.0 copy-start.5
  21.2 5.6 %pick_rows.1 = (bf16[256,128]{1,0:T(8,128)(2,1)S(1)}, bf16[1536,1024]{1,0:T(8,128)(2,1)S(1)}) custom-call(s32[32,1,16]{2,1,0:T(1,128)S(1)} %all_to_all.10.source_ref, bf16[64,76032]{1,0:T(8,128)(2,1)} %bitcast.15, bf16[2048,1024]{1,0:T(8,128)(2,1)} %value_ref.1), custom_call_target="tpu_custom_call" | custom-call | tf_op jit(solution)/shard_map/pick_rows/pallas_call | solution.py:140
  26.7 11.9 %all_to_all.11 = bf16[32,8,128]{2,1,0:T(8,128)(2,1)S(1)} all-to-all(bf16[32,8,128]{2,1,0:T(8,128)(2,1)S(1)} %bitcast.11), channel_id=1, replica_groups=mesh['rows'=32,'tp'=4] {'rows'}, dimensions={0} | all-to-all | bytes 131072 | tf_op jit(solution)/shard_map/all_to_all | solution.py:607
  38.6 0.0 copy-done.5
  38.7 0.0 copy-start.1
  38.7 0.0 copy-start.9
  38.7 2.9 %project.1 = (bf16[16,2048]{1,0:T(8,128)(2,1)S(1)}, bf16[8,32,128]{2,1,0:T(8,128)(2,1)S(1)}, f32[16,640]{1,0:T(8,128)S(1)}, bf16[16,768]{1,0:T(8,128)(2,1)S(1)},...) custom-call(bf16[256,128]{1,0:T(8,128)(2,1)S(1)} %bitcast.9, bf16[16,128]{1,0:T(8,128)(2,1)S(1)} %bitcast.12, ...), custom_call_target="tpu_custom_call" | custom-call | flops 134217728 | bytes 8388608 | tf_op jit(solution)/shard_map/project/pallas_call | solution.py:228
  41.6 0.0 copy-start
  41.6 0.0 copy-start.2
  41.6 0.0 copy-start.6
  41.6 0.0 copy-start.10
  41.7 3.6 %collective-permute-start = (bf16[16,768]{1,0:T(8,128)(2,1)S(1)}, bf16[16,768]{1,0:T(8,128)(2,1)S(1)}, u32[]{:S(2)}, u32[]{:S(2)}) collective-permute-start(bf16[16,768]{1,0:T(8,128)(2,1)S(1)} %get-tuple-element.19), channel_id=1, source_target_pairs={{0,1},{1,0},{2,3},{3,2},{4,5},{5,4},{6,7},{7,6},{8,9},{9,8},{10,11... | collective-permute-start | bytes 73736 | tf_op jit(solution)/shard_map/ppermute | solution.py:560
  45.2 0.3 collective-permute-start.1
  45.6 1.4 %collective-permute-start.2 = (bf16[16,768]{1,0:T(8,128)(2,1)S(1)}, bf16[16,768]{1,0:T(8,128)(2,1)S(1)}, u32[]{:S(2)}, u32[]{:S(2)}) collective-permute-start(bf16[16,768]{1,0:T(8,128)(2,1)S(1)} %get-tuple-element.21), channel_id=1, source_target_pairs={{0,3},{1,2},{2,1},{3,0},{4,7},{5,6},{6,5},{7,4},{8,11},{9,10},{10,... | collective-permute-start | bytes 73736 | tf_op jit(solution)/shard_map/ppermute | solution.py:560
  47.0 0.0 copy-done.1
  47.0 0.0 copy-done.9
  47.0 1.4 %policy_scores.1 = (f32[8,32,1024]{2,1,0:T(8,128)S(1)}, f32[8,32,128]{2,1,0:T(8,128)S(1)}) custom-call(s32[4]{0:T(128)S(1)} %copy-done.9, bf16[8,32,128]{2,1,0:T(8,128)(2,1)S(1)} %get-tuple-element.22.query_ref, bf16[4,1024,256]{2,1,0:T(8,128)(2,1)S(1)} %copy-done.1), custom_call_target="tpu_custom_call" | custom-call | flops 67108864 | bytes 3145728 | tf_op jit(solution)/shard_map/policy_scores/pallas_call | solution.py:270
  48.4 0.0 copy-start.3
  48.4 0.0 copy-start.4
  48.4 0.0 copy-start.7
  48.4 0.0 collective-permute-done.one_ref
  48.4 0.0 collective-permute-done.1.two_ref
  48.4 0.6 collective-permute-done.2.three_ref
  49.0 0.0 copy-done
  49.0 1.2 %policy.1 = (bf16[16,2048]{1,0:T(8,128)(2,1)S(1)}, f32[16,128]{1,0:T(8,128)S(1)}) custom-call(f32[16,640]{1,0:T(8,128)S(1)} %get-tuple-element.18.own_ref, bf16[16,768]{1,0:T(8,128)(2,1)S(1)} %collective-permute-done.one_ref, bf16[16,768]{1,0:T(8,128)(2,1)S(1)} %collective-permute-done.1.two_ref, bf16[16,768]{1,0:T(8,128)(2,1)S(1)} %collective-permute-done.2.three_ref, ...), custom_call_target="tpu_custom_call" | custom-call | flops 67108864 | bytes 3145728 | tf_op jit(solution)/shard_map/policy/pallas_call | solution.py:382
  50.2 1.0 %collective-permute-start.3 = (bf16[16,2048]{1,0:T(8,128)(2,1)S(1)}, bf16[16,2048]{1,0:T(8,128)(2,1)S(1)}, u32[]{:S(2)}, u32[]{:S(2)}) collective-permute-start(bf16[16,2048]{1,0:T(8,128)(2,1)S(1)} %get-tuple-element.26.rows_ref), channel_id=1, source_target_pairs={{0,64},{4,68},{8,72},{12,76},{16,80},{20,84},{24,88},{28,92},{32,9... | collective-permute-start | bytes 196616 | tf_op jit(solution)/shard_map/ppermute | solution.py:565
  51.2 2.6 %collective-permute-start.4 = (f32[16,128]{1,0:T(8,128)S(1)}, f32[16,128]{1,0:T(8,128)S(1)}, u32[]{:S(2)}, u32[]{:S(2)}) collective-permute-start(f32[16,128]{1,0:T(8,128)S(1)} %get-tuple-element.27), channel_id=1, source_target_pairs={{0,66},{1,67},{2,64},{3,65},{4,70},{5,71},{6,68},{7,69},{8,74},{9,... | collective-permute-start | bytes 24584 | tf_op jit(solution)/shard_map/ppermute | solution.py:576
  53.9 1.0 %collective-permute-done.3.rows_ref = bf16[16,2048]{1,0:T(8,128)(2,1)S(1)} collective-permute-done((bf16[16,2048]{1,0:T(8,128)(2,1)S(1)}, bf16[16,2048]{1,0:T(8,128)(2,1)S(1)}, u32[]{:S(2)}, u32[]{:S(2)}) %collective-permute-start.3) | collective-permute-done | bytes 65568 | tf_op jit(solution)/shard_map/ppermute | solution.py:565
  54.9 0.0 copy-done.2
  54.9 0.0 copy-done.6
  54.9 0.0 copy-done.10
  54.9 1.5 %critic_scores.1 = (f32[8,32,1024]{2,1,0:T(8,128)S(1)}, f32[8,32,128]{2,1,0:T(8,128)S(1)}) custom-call(s32[4]{0:T(128)S(1)} %copy-done.10, bf16[16,2048]{1,0:T(8,128)(2,1)S(1)} %collective-permute-done.3.rows_ref, bf16[16,128]{1,0:T(8,128)(2,1)S(1)} %bitcast.13, bf16[4,1024,256]{2,1,0:T(8,128)(2,1)S(1)} %copy-done.2), custom_call_target="tpu_custom_call" | custom-call | flops 67108864 | bytes 3145728 | tf_op jit(solution)/shard_map/critic_scores/pallas_call | solution.py:455
  56.3 0.0 collective-permute-done.4.other_ref
  56.3 0.1 row_squares.1.near_ref
  56.4 1.6 %collective-permute-start.5 = (f32[16,128]{1,0:T(8,128)S(1)}, f32[16,128]{1,0:T(8,128)S(1)}, u32[]{:S(2)}, u32[]{:S(2)}) collective-permute-start(f32[16,128]{1,0:T(8,128)S(1)} %row_squares.1.near_ref), channel_id=1, source_target_pairs={{0,1},{1,0},{2,3},{3,2},{4,5},{5,4},{6,7},{7,6},{8,9},{9,8},{10,11... | collective-permute-start | bytes 24584 | tf_op jit(solution)/shard_map/ppermute | solution.py:560
  58.1 0.8 %collective-permute-done.5.far_ref = f32[16,128]{1,0:T(8,128)S(1)} collective-permute-done((f32[16,128]{1,0:T(8,128)S(1)}, f32[16,128]{1,0:T(8,128)S(1)}, u32[]{:S(2)}, u32[]{:S(2)}) %collective-permute-start.5) | collective-permute-done | bytes 8224 | tf_op jit(solution)/shard_map/ppermute | solution.py:560
  58.9 0.0 copy-done.3
  58.9 0.0 copy-done.4
  58.9 0.0 copy-done.7
  58.9 0.8 %critic.1.own_ref = f32[16,128]{1,0:T(8,128)S(1)} custom-call(f32[16,128]{1,0:T(8,128)S(1)} %row_squares.1.near_ref, f32[16,128]{1,0:T(8,128)S(1)} %collective-permute-done.5.far_ref, f32[8,32,1024]{2,1,0:T(8,128)S(1)} %get-tuple-element.29.raw_ref, f32[8,32,128]{2,1,0:T(8,128)S(1)} %get-tuple-element.28._.top_ref, ...), custom_call_target="tpu_custom_call" | custom-call | flops 67108864 | bytes 3145728 | tf_op jit(solution)/shard_map/critic/pallas_call | solution.py:519
  59.7 1.2 %collective-permute-start.8 = (f32[16,128]{1,0:T(8,128)S(1)}, f32[16,128]{1,0:T(8,128)S(1)}, u32[]{:S(2)}, u32[]{:S(2)}) collective-permute-start(f32[16,128]{1,0:T(8,128)S(1)} %critic.1.own_ref), channel_id=1, source_target_pairs={{0,3},{1,2},{2,1},{3,0},{4,7},{5,6},{6,5},{7,4},{8,11},{9,10},{10,... | collective-permute-start | bytes 24584 | tf_op jit(solution)/shard_map/ppermute | solution.py:560
  60.9 0.6 collective-permute-start.7
  61.5 0.4 collective-permute-start.6
  61.9 0.7 %by_step.1 = bf16[4,4,2048]{2,1,0:T(4,128)(2,1)} custom-call(bf16[16,2048]{1,0:T(8,128)(2,1)S(1)} %get-tuple-element.26.rows_ref), custom_call_target="tpu_custom_call" | custom-call | bytes 524288 | tf_op jit(solution)/shard_map/by_step/pallas_call | solution.py:408
  62.6 0.3 collective-permute-done.8.three_ref
  62.8 0.5 collective-permute-done.7.two_ref
  63.4 0.0 collective-permute-done.6.one_ref
  63.4 0.8 %expect.1 = f32[4,4]{1,0:T(4,128)} custom-call(f32[16,128]{1,0:T(8,128)S(1)} %critic.1.own_ref, f32[16,128]{1,0:T(8,128)S(1)} %collective-permute-done.6.one_ref, f32[16,128]{1,0:T(8,128)S(1)} %collective-permute-done.7.two_ref, f32[16,128]{1,0:T(8,128)S(1)} %collective-permute-done.8.three_ref), custom_call_target="tpu_custom_call" | custom-call | tf_op jit(solution)/shard_map/expect/pallas_call | solution.py:555
Async XLA Ops:
  0.6 0.7 %copy-start.8 = (s32[4,4]{1,0:T(4,128)S(1)}, s32[4,4]{1,0:T(4,128)}, u32[]{:S(2)}) copy-start(s32[4,4]{1,0:T(4,128)} %token_ref.1) | copy-start | bytes 196
  21.2 17.5 %copy-start.5 = (bf16[2048]{0:T(1024)(128)(2,1)S(1)}, bf16[2048]{0:T(1024)(128)(2,1)}, u32[]{:S(2)}) copy-start(bf16[2048]{0:T(1024)(128)(2,1)} %param.17) | copy-start | bytes 12292
  38.7 8.3 %copy-start.1 = (bf16[4,1024,256]{2,1,0:T(8,128)(2,1)S(1)}, bf16[4,1024,256]{2,1,0:T(8,128)(2,1)}, u32[]{:S(2)}) copy-start(bf16[4,1024,256]{2,1,0:T(8,128)(2,1)} %keys_ref.2) | copy-start | bytes 6291460
  38.7 8.3 %copy-start.9 = (s32[4]{0:T(128)S(1)}, s32[4]{0:T(128)}, u32[]{:S(2)}) copy-start(s32[4]{0:T(128)} %length_ref.2) | copy-start | bytes 52
  41.6 7.4 %copy-start = (bf16[4,1024,256]{2,1,0:T(8,128)(2,1)S(1)}, bf16[4,1024,256]{2,1,0:T(8,128)(2,1)}, u32[]{:S(2)}) copy-start(bf16[4,1024,256]{2,1,0:T(8,128)(2,1)} %values_ref.2) | copy-start | bytes 6291460
  41.6 13.3 %copy-start.2 = (bf16[4,1024,256]{2,1,0:T(8,128)(2,1)S(1)}, bf16[4,1024,256]{2,1,0:T(8,128)(2,1)}, u32[]{:S(2)}) copy-start(bf16[4,1024,256]{2,1,0:T(8,128)(2,1)} %keys_ref.3) | copy-start | bytes 6291460
  41.6 13.3 %copy-start.6 = (bf16[2048]{0:T(1024)(128)(2,1)S(1)}, bf16[2048]{0:T(1024)(128)(2,1)}, u32[]{:S(2)}) copy-start(bf16[2048]{0:T(1024)(128)(2,1)} %param.23) | copy-start | bytes 12292
  41.6 13.2 %copy-start.10 = (s32[4]{0:T(128)S(1)}, s32[4]{0:T(128)}, u32[]{:S(2)}) copy-start(s32[4]{0:T(128)} %length_ref.3) | copy-start | bytes 52
  41.7 6.8 %collective-permute-start = (bf16[16,768]{1,0:T(8,128)(2,1)S(1)}, bf16[16,768]{1,0:T(8,128)(2,1)S(1)}, u32[]{:S(2)}, u32[]{:S(2)}) collective-permute-start(bf16[16,768]{1,0:T(8,128)(2,1)S(1)} %get-tuple-element.19), channel_id=1, source_target_pairs={{0,1},{1,0},{2,3},{3,2},{4,5},{5,4},{6,7},{7,6},{8,9},{9,8},{10,11... | collective-permute-start | bytes 73736 | tf_op jit(solution)/shard_map/ppermute | solution.py:560
  45.2 3.2 %collective-permute-start.1 = (bf16[16,768]{1,0:T(8,128)(2,1)S(1)}, bf16[16,768]{1,0:T(8,128)(2,1)S(1)}, u32[]{:S(2)}, u32[]{:S(2)}) collective-permute-start(bf16[16,768]{1,0:T(8,128)(2,1)S(1)} %get-tuple-element.20), channel_id=1, source_target_pairs={{0,2},{1,3},{2,0},{3,1},{4,6},{5,7},{6,4},{7,5},{8,10},{9,11},{10,... | collective-permute-start | bytes 73736 | tf_op jit(solution)/shard_map/ppermute | solution.py:560
  45.6 3.5 %collective-permute-start.2 = (bf16[16,768]{1,0:T(8,128)(2,1)S(1)}, bf16[16,768]{1,0:T(8,128)(2,1)S(1)}, u32[]{:S(2)}, u32[]{:S(2)}) collective-permute-start(bf16[16,768]{1,0:T(8,128)(2,1)S(1)} %get-tuple-element.21), channel_id=1, source_target_pairs={{0,3},{1,2},{2,1},{3,0},{4,7},{5,6},{6,5},{7,4},{8,11},{9,10},{10,... | collective-permute-start | bytes 73736 | tf_op jit(solution)/shard_map/ppermute | solution.py:560
  48.4 10.5 %copy-start.3 = (bf16[4,1024,256]{2,1,0:T(8,128)(2,1)S(1)}, bf16[4,1024,256]{2,1,0:T(8,128)(2,1)}, u32[]{:S(2)}) copy-start(bf16[4,1024,256]{2,1,0:T(8,128)(2,1)} %values_ref.3) | copy-start | bytes 6291460
  48.4 10.5 %copy-start.4 = (bf16[2048,51]{0,1:T(8,128)(2,1)S(1)}, bf16[2048,51]{0,1:T(8,128)(2,1)}, u32[]{:S(2)}) copy-start(bf16[2048,51]{0,1:T(8,128)(2,1)} %param.27) | copy-start | bytes 626692
  48.4 10.5 %copy-start.7 = (bf16[2048]{0:T(1024)(128)(2,1)S(1)}, bf16[2048]{0:T(1024)(128)(2,1)}, u32[]{:S(2)}) copy-start(bf16[2048]{0:T(1024)(128)(2,1)} %param.26) | copy-start | bytes 12292
  50.2 4.6 %collective-permute-start.3 = (bf16[16,2048]{1,0:T(8,128)(2,1)S(1)}, bf16[16,2048]{1,0:T(8,128)(2,1)S(1)}, u32[]{:S(2)}, u32[]{:S(2)}) collective-permute-start(bf16[16,2048]{1,0:T(8,128)(2,1)S(1)} %get-tuple-element.26.rows_ref), channel_id=1, source_target_pairs={{0,64},{4,68},{8,72},{12,76},{16,80},{20,84},{24,88},{28,92},{32,9... | collective-permute-start | bytes 196616 | tf_op jit(solution)/shard_map/ppermute | solution.py:565
  51.2 5.1 %collective-permute-start.4 = (f32[16,128]{1,0:T(8,128)S(1)}, f32[16,128]{1,0:T(8,128)S(1)}, u32[]{:S(2)}, u32[]{:S(2)}) collective-permute-start(f32[16,128]{1,0:T(8,128)S(1)} %get-tuple-element.27), channel_id=1, source_target_pairs={{0,66},{1,67},{2,64},{3,65},{4,70},{5,71},{6,68},{7,69},{8,74},{9,... | collective-permute-start | bytes 24584 | tf_op jit(solution)/shard_map/ppermute | solution.py:576
  56.4 2.5 %collective-permute-start.5 = (f32[16,128]{1,0:T(8,128)S(1)}, f32[16,128]{1,0:T(8,128)S(1)}, u32[]{:S(2)}, u32[]{:S(2)}) collective-permute-start(f32[16,128]{1,0:T(8,128)S(1)} %row_squares.1.near_ref), channel_id=1, source_target_pairs={{0,1},{1,0},{2,3},{3,2},{4,5},{5,4},{6,7},{7,6},{8,9},{9,8},{10,11... | collective-permute-start | bytes 24584 | tf_op jit(solution)/shard_map/ppermute | solution.py:560
  59.7 3.1 %collective-permute-start.8 = (f32[16,128]{1,0:T(8,128)S(1)}, f32[16,128]{1,0:T(8,128)S(1)}, u32[]{:S(2)}, u32[]{:S(2)}) collective-permute-start(f32[16,128]{1,0:T(8,128)S(1)} %critic.1.own_ref), channel_id=1, source_target_pairs={{0,3},{1,2},{2,1},{3,0},{4,7},{5,6},{6,5},{7,4},{8,11},{9,10},{10,... | collective-permute-start | bytes 24584 | tf_op jit(solution)/shard_map/ppermute | solution.py:560
  60.9 2.5 %collective-permute-start.7 = (f32[16,128]{1,0:T(8,128)S(1)}, f32[16,128]{1,0:T(8,128)S(1)}, u32[]{:S(2)}, u32[]{:S(2)}) collective-permute-start(f32[16,128]{1,0:T(8,128)S(1)} %critic.1.own_ref), channel_id=1, source_target_pairs={{0,2},{1,3},{2,0},{3,1},{4,6},{5,7},{6,4},{7,5},{8,10},{9,11},{10,... | collective-permute-start | bytes 24584 | tf_op jit(solution)/shard_map/ppermute | solution.py:560
  61.5 1.9 %collective-permute-start.6 = (f32[16,128]{1,0:T(8,128)S(1)}, f32[16,128]{1,0:T(8,128)S(1)}, u32[]{:S(2)}, u32[]{:S(2)}) collective-permute-start(f32[16,128]{1,0:T(8,128)S(1)} %critic.1.own_ref), channel_id=1, source_target_pairs={{0,1},{1,0},{2,3},{3,2},{4,5},{5,4},{6,7},{7,6},{8,9},{9,8},{10,11... | collective-permute-start | bytes 24584 | tf_op jit(solution)/shard_map/ppermute | solution.py:560

commit v10 on v9

--- a/solution.py
+++ b/solution.py
@@ -163,14 +163,15 @@
     tp = lax.axis_index("tp")
     early = early_ref.shape[0]
     chunk = width - early
+    piece = chunk // 2
     copies = [pltpu.make_async_copy(value_ref.at[pl.ds(early, chunk)], late_ref, sems.at[0])]
-    for at in range(width // chunk):
-        rows = pl.ds(at * chunk, chunk)
+    for at in range(width // piece):
+        rows = pl.ds(at * piece, piece)
         copies.append(
             pltpu.make_async_copy(key_ref.at[rows], keys_ref.at[rows], sems.at[at + 1])
         )
     for copy in copies:
-        copy.start()
+        copy.start(priority=1)
     left = lax.broadcasted_iota(jnp.int32, (8, LANES), 1) < HALF
     squares = jnp.zeros((count, LANES), jnp.float32)
     for k in range(width // LANES):
@@ -197,8 +198,8 @@
     copies[0].wait()
     sums_ref[1] = values + product(pl.ds(early, chunk), late_ref[...])
     keys = None
-    for at in range(width // chunk):
-        rows = pl.ds(at * chunk, chunk)
+    for at in range(width // piece):
+        rows = pl.ds(at * piece, piece)
         copies[at + 1].wait()
         partial = product(rows, keys_ref[rows, :])
         keys = partial if keys is None else keys + partial
@@ -235,7 +236,7 @@
             pltpu.VMEM((2, count, kv_all), jnp.float32),
             pltpu.VMEM((width - early, kv_all), key_weight.dtype),
             pltpu.VMEM((width, kv_all), key_weight.dtype),
-            pltpu.SemaphoreType.DMA((1 + width // (width - early),)),
+            pltpu.SemaphoreType.DMA((1 + 2 * width // (width - early),)),
         ],
         flops=4 * count * width * kv_all,
         moved=4 * width * kv_all,

time: 64.4 us -> 64.4 us (level)
  no operation moved by 1% of the time
where the time goes in v10:
time: 64.4 us; the launch traced here: 64.2 us
  blocking collectives  31.7 us (49%)
  Pallas kernels  15 us (23%)
  starting transfers between devices  12.7 us (20%)
  waiting for transfers between devices  3.26 us (5%)
  between operations  0.74 us (1%)
  local copies, waits for them, and re-layouts  0.72 us (1%)
    all_to_all x1, blocking collectives, on_device(): all_tokens = lax.all_to_all(laid_out(tokens, row_groups), 'rows', 0, 0)  19.8 us
    all_to_all x1, blocking collectives, on_device(): blocks = lax.all_to_all(picked.reshape(row_groups, -1, LANES), 'rows', 0, 0)  11.9 us
    ppermute x7, starting transfers between devices, swapped(): return lax.ppermute(shard, 'tp', [(i, i ^ by) for i in range(peers)])  9.11 us
    pallas_call x1, Pallas kernels, pick_rows(): kernel_call(pick_rows_kernel, (array((rows, LANES), table.dtype), pltpu.V...  5.55 us
    pallas_call x1, Pallas kernels, project(): kernel_call(project_kernel, (array((count, width), jnp.bfloat16), array(q...  2.89 us
    ppermute x1, starting transfers between devices, crossed(): return lax.ppermute(shard, ('rows', 'tp'), pairs)  2.62 us
    ppermute x7, waiting for transfers between devices, swapped(): return lax.ppermute(shard, 'tp', [(i, i ^ by) for i in range(peers)])  2.25 us
    pallas_call x1, Pallas kernels, critic_scores(): kernel_call(critic_scores_kernel, (raw, array(placed, jnp.float32)), [SME...  1.45 us
  transfers between devices with their start and end apart: 9, of which 5 were waited for; matrix products, arithmetic and copies ran while one was open for 0% of the time, Pallas kernels for 6%

profile of v10, /device:TPU:1, one launch (start us, length us, event | category | flops | bytes accessed | tf_op | source)
XLA Modules:
  0.0 64.2 jit_solution(1228550063311061589)
XLA Ops:
  0.6 0.0 copy-start.8
  0.6 0.7 %copy-done.8 = s32[4,4]{1,0:T(4,128)S(1)} copy-done((s32[4,4]{1,0:T(4,128)S(1)}, s32[4,4]{1,0:T(4,128)}, u32[]{:S(2)}) %copy-start.8) | copy-done | bytes 88
  1.3 0.1 lay_out.1
  1.4 19.8 %all_to_all.10.source_ref = s32[32,1,16]{2,1,0:T(1,128)S(1)} all-to-all(s32[32,1,16]{2,1,0:T(1,128)S(1)} %lay_out.1), channel_id=1, replica_groups=mesh['rows'=32,'tp'=4] {'rows'}, dimensions={0} | all-to-all | bytes 4096 | tf_op jit(solution)/shard_map/all_to_all | solution.py:606
  21.2 0.0 copy-start.5
  21.2 5.6 %pick_rows.1 = (bf16[256,128]{1,0:T(8,128)(2,1)S(1)}, bf16[1536,1024]{1,0:T(8,128)(2,1)S(1)}) custom-call(s32[32,1,16]{2,1,0:T(1,128)S(1)} %all_to_all.10.source_ref, bf16[64,76032]{1,0:T(8,128)(2,1)} %bitcast.15, bf16[2048,1024]{1,0:T(8,128)(2,1)} %value_ref.1), custom_call_target="tpu_custom_call" | custom-call | tf_op jit(solution)/shard_map/pick_rows/pallas_call | solution.py:140
  26.7 11.9 %all_to_all.11 = bf16[32,8,128]{2,1,0:T(8,128)(2,1)S(1)} all-to-all(bf16[32,8,128]{2,1,0:T(8,128)(2,1)S(1)} %bitcast.11), channel_id=1, replica_groups=mesh['rows'=32,'tp'=4] {'rows'}, dimensions={0} | all-to-all | bytes 131072 | tf_op jit(solution)/shard_map/all_to_all | solution.py:608
  38.6 0.0 copy-done.5
  38.7 0.0 copy-start.1
  38.7 0.0 copy-start.9
  38.7 2.9 %project.1 = (bf16[16,2048]{1,0:T(8,128)(2,1)S(1)}, bf16[8,32,128]{2,1,0:T(8,128)(2,1)S(1)}, f32[16,640]{1,0:T(8,128)S(1)}, bf16[16,768]{1,0:T(8,128)(2,1)S(1)},...) custom-call(bf16[256,128]{1,0:T(8,128)(2,1)S(1)} %bitcast.9, bf16[16,128]{1,0:T(8,128)(2,1)S(1)} %bitcast.12, ...), custom_call_target="tpu_custom_call" | custom-call | flops 134217728 | bytes 8388608 | tf_op jit(solution)/shard_map/project/pallas_call | solution.py:229
  41.5 0.0 copy-start
  41.6 0.0 copy-start.2
  41.6 0.0 copy-start.6
  41.6 0.0 copy-start.10
  41.6 3.6 %collective-permute-start = (bf16[16,768]{1,0:T(8,128)(2,1)S(1)}, bf16[16,768]{1,0:T(8,128)(2,1)S(1)}, u32[]{:S(2)}, u32[]{:S(2)}) collective-permute-start(bf16[16,768]{1,0:T(8,128)(2,1)S(1)} %get-tuple-element.19), channel_id=1, source_target_pairs={{0,1},{1,0},{2,3},{3,2},{4,5},{5,4},{6,7},{7,6},{8,9},{9,8},{10,11... | collective-permute-start | bytes 73736 | tf_op jit(solution)/shard_map/ppermute | solution.py:561
  45.2 0.3 collective-permute-start.1
  45.5 1.4 %collective-permute-start.2 = (bf16[16,768]{1,0:T(8,128)(2,1)S(1)}, bf16[16,768]{1,0:T(8,128)(2,1)S(1)}, u32[]{:S(2)}, u32[]{:S(2)}) collective-permute-start(bf16[16,768]{1,0:T(8,128)(2,1)S(1)} %get-tuple-element.21), channel_id=1, source_target_pairs={{0,3},{1,2},{2,1},{3,0},{4,7},{5,6},{6,5},{7,4},{8,11},{9,10},{10,... | collective-permute-start | bytes 73736 | tf_op jit(solution)/shard_map/ppermute | solution.py:561
  46.9 0.0 copy-done.1
  46.9 0.0 copy-done.9
  46.9 1.4 %policy_scores.1 = (f32[8,32,1024]{2,1,0:T(8,128)S(1)}, f32[8,32,128]{2,1,0:T(8,128)S(1)}) custom-call(s32[4]{0:T(128)S(1)} %copy-done.9, bf16[8,32,128]{2,1,0:T(8,128)(2,1)S(1)} %get-tuple-element.22.query_ref, bf16[4,1024,256]{2,1,0:T(8,128)(2,1)S(1)} %copy-done.1), custom_call_target="tpu_custom_call" | custom-call | flops 67108864 | bytes 3145728 | tf_op jit(solution)/shard_map/policy_scores/pallas_call | solution.py:271
  48.3 0.0 copy-start.3
  48.4 0.0 copy-start.4
  48.4 0.0 copy-start.7
  48.4 0.0 collective-permute-done.one_ref
  48.4 0.0 collective-permute-done.1.two_ref
  48.4 0.6 collective-permute-done.2.three_ref
  49.0 0.0 copy-done
  49.0 1.2 %policy.1 = (bf16[16,2048]{1,0:T(8,128)(2,1)S(1)}, f32[16,128]{1,0:T(8,128)S(1)}) custom-call(f32[16,640]{1,0:T(8,128)S(1)} %get-tuple-element.18.own_ref, bf16[16,768]{1,0:T(8,128)(2,1)S(1)} %collective-permute-done.one_ref, bf16[16,768]{1,0:T(8,128)(2,1)S(1)} %collective-permute-done.1.two_ref, bf16[16,768]{1,0:T(8,128)(2,1)S(1)} %collective-permute-done.2.three_ref, ...), custom_call_target="tpu_custom_call" | custom-call | flops 67108864 | bytes 3145728 | tf_op jit(solution)/shard_map/policy/pallas_call | solution.py:383
  50.2 1.0 %collective-permute-start.3 = (bf16[16,2048]{1,0:T(8,128)(2,1)S(1)}, bf16[16,2048]{1,0:T(8,128)(2,1)S(1)}, u32[]{:S(2)}, u32[]{:S(2)}) collective-permute-start(bf16[16,2048]{1,0:T(8,128)(2,1)S(1)} %get-tuple-element.26.rows_ref), channel_id=1, source_target_pairs={{0,64},{4,68},{8,72},{12,76},{16,80},{20,84},{24,88},{28,92},{32,9... | collective-permute-start | bytes 196616 | tf_op jit(solution)/shard_map/ppermute | solution.py:566
  51.2 2.6 %collective-permute-start.4 = (f32[16,128]{1,0:T(8,128)S(1)}, f32[16,128]{1,0:T(8,128)S(1)}, u32[]{:S(2)}, u32[]{:S(2)}) collective-permute-start(f32[16,128]{1,0:T(8,128)S(1)} %get-tuple-element.27), channel_id=1, source_target_pairs={{0,66},{1,67},{2,64},{3,65},{4,70},{5,71},{6,68},{7,69},{8,74},{9,... | collective-permute-start | bytes 24584 | tf_op jit(solution)/shard_map/ppermute | solution.py:577
  53.8 1.0 %collective-permute-done.3.rows_ref = bf16[16,2048]{1,0:T(8,128)(2,1)S(1)} collective-permute-done((bf16[16,2048]{1,0:T(8,128)(2,1)S(1)}, bf16[16,2048]{1,0:T(8,128)(2,1)S(1)}, u32[]{:S(2)}, u32[]{:S(2)}) %collective-permute-start.3) | collective-permute-done | bytes 65568 | tf_op jit(solution)/shard_map/ppermute | solution.py:566
  54.8 0.0 copy-done.2
  54.8 0.0 copy-done.6
  54.8 0.0 copy-done.10
  54.8 1.5 %critic_scores.1 = (f32[8,32,1024]{2,1,0:T(8,128)S(1)}, f32[8,32,128]{2,1,0:T(8,128)S(1)}) custom-call(s32[4]{0:T(128)S(1)} %copy-done.10, bf16[16,2048]{1,0:T(8,128)(2,1)S(1)} %collective-permute-done.3.rows_ref, bf16[16,128]{1,0:T(8,128)(2,1)S(1)} %bitcast.13, bf16[4,1024,256]{2,1,0:T(8,128)(2,1)S(1)} %copy-done.2), custom_call_target="tpu_custom_call" | custom-call | flops 67108864 | bytes 3145728 | tf_op jit(solution)/shard_map/critic_scores/pallas_call | solution.py:456
  56.3 0.0 collective-permute-done.4.other_ref
  56.3 0.1 row_squares.1.near_ref
  56.4 1.6 %collective-permute-start.5 = (f32[16,128]{1,0:T(8,128)S(1)}, f32[16,128]{1,0:T(8,128)S(1)}, u32[]{:S(2)}, u32[]{:S(2)}) collective-permute-start(f32[16,128]{1,0:T(8,128)S(1)} %row_squares.1.near_ref), channel_id=1, source_target_pairs={{0,1},{1,0},{2,3},{3,2},{4,5},{5,4},{6,7},{7,6},{8,9},{9,8},{10,11... | collective-permute-start | bytes 24584 | tf_op jit(solution)/shard_map/ppermute | solution.py:561
  58.0 0.8 %collective-permute-done.5.far_ref = f32[16,128]{1,0:T(8,128)S(1)} collective-permute-done((f32[16,128]{1,0:T(8,128)S(1)}, f32[16,128]{1,0:T(8,128)S(1)}, u32[]{:S(2)}, u32[]{:S(2)}) %collective-permute-start.5) | collective-permute-done | bytes 8224 | tf_op jit(solution)/shard_map/ppermute | solution.py:561
  58.9 0.0 copy-done.3
  58.9 0.0 copy-done.4
  58.9 0.0 copy-done.7
  58.9 0.8 %critic.1.own_ref = f32[16,128]{1,0:T(8,128)S(1)} custom-call(f32[16,128]{1,0:T(8,128)S(1)} %row_squares.1.near_ref, f32[16,128]{1,0:T(8,128)S(1)} %collective-permute-done.5.far_ref, f32[8,32,1024]{2,1,0:T(8,128)S(1)} %get-tuple-element.29.raw_ref, f32[8,32,128]{2,1,0:T(8,128)S(1)} %get-tuple-element.28._.top_ref, ...), custom_call_target="tpu_custom_call" | custom-call | flops 67108864 | bytes 3145728 | tf_op jit(solution)/shard_map/critic/pallas_call | solution.py:520
  59.7 1.2 %collective-permute-start.8 = (f32[16,128]{1,0:T(8,128)S(1)}, f32[16,128]{1,0:T(8,128)S(1)}, u32[]{:S(2)}, u32[]{:S(2)}) collective-permute-start(f32[16,128]{1,0:T(8,128)S(1)} %critic.1.own_ref), channel_id=1, source_target_pairs={{0,3},{1,2},{2,1},{3,0},{4,7},{5,6},{6,5},{7,4},{8,11},{9,10},{10,... | collective-permute-start | bytes 24584 | tf_op jit(solution)/shard_map/ppermute | solution.py:561
  60.8 0.6 collective-permute-start.7
  61.4 0.4 collective-permute-start.6
  61.8 0.7 %by_step.1 = bf16[4,4,2048]{2,1,0:T(4,128)(2,1)} custom-call(bf16[16,2048]{1,0:T(8,128)(2,1)S(1)} %get-tuple-element.26.rows_ref), custom_call_target="tpu_custom_call" | custom-call | bytes 524288 | tf_op jit(solution)/shard_map/by_step/pallas_call | solution.py:409
  62.5 0.3 collective-permute-done.8.three_ref
  62.8 0.5 collective-permute-done.7.two_ref
  63.3 0.0 collective-permute-done.6.one_ref
  63.3 0.8 %expect.1 = f32[4,4]{1,0:T(4,128)} custom-call(f32[16,128]{1,0:T(8,128)S(1)} %critic.1.own_ref, f32[16,128]{1,0:T(8,128)S(1)} %collective-permute-done.6.one_ref, f32[16,128]{1,0:T(8,128)S(1)} %collective-permute-done.7.two_ref, f32[16,128]{1,0:T(8,128)S(1)} %collective-permute-done.8.three_ref), custom_call_target="tpu_custom_call" | custom-call | tf_op jit(solution)/shard_map/expect/pallas_call | solution.py:556
Async XLA Ops:
  0.6 0.7 %copy-start.8 = (s32[4,4]{1,0:T(4,128)S(1)}, s32[4,4]{1,0:T(4,128)}, u32[]{:S(2)}) copy-start(s32[4,4]{1,0:T(4,128)} %token_ref.1) | copy-start | bytes 196
  21.2 17.5 %copy-start.5 = (bf16[2048]{0:T(1024)(128)(2,1)S(1)}, bf16[2048]{0:T(1024)(128)(2,1)}, u32[]{:S(2)}) copy-start(bf16[2048]{0:T(1024)(128)(2,1)} %param.17) | copy-start | bytes 12292
  38.7 8.3 %copy-start.1 = (bf16[4,1024,256]{2,1,0:T(8,128)(2,1)S(1)}, bf16[4,1024,256]{2,1,0:T(8,128)(2,1)}, u32[]{:S(2)}) copy-start(bf16[4,1024,256]{2,1,0:T(8,128)(2,1)} %keys_ref.2) | copy-start | bytes 6291460
  38.7 8.3 %copy-start.9 = (s32[4]{0:T(128)S(1)}, s32[4]{0:T(128)}, u32[]{:S(2)}) copy-start(s32[4]{0:T(128)} %length_ref.2) | copy-start | bytes 52
  41.5 7.4 %copy-start = (bf16[4,1024,256]{2,1,0:T(8,128)(2,1)S(1)}, bf16[4,1024,256]{2,1,0:T(8,128)(2,1)}, u32[]{:S(2)}) copy-start(bf16[4,1024,256]{2,1,0:T(8,128)(2,1)} %values_ref.2) | copy-start | bytes 6291460
  41.6 13.3 %copy-start.2 = (bf16[4,1024,256]{2,1,0:T(8,128)(2,1)S(1)}, bf16[4,1024,256]{2,1,0:T(8,128)(2,1)}, u32[]{:S(2)}) copy-start(bf16[4,1024,256]{2,1,0:T(8,128)(2,1)} %keys_ref.3) | copy-start | bytes 6291460
  41.6 13.3 %copy-start.6 = (bf16[2048]{0:T(1024)(128)(2,1)S(1)}, bf16[2048]{0:T(1024)(128)(2,1)}, u32[]{:S(2)}) copy-start(bf16[2048]{0:T(1024)(128)(2,1)} %param.23) | copy-start | bytes 12292
  41.6 13.2 %copy-start.10 = (s32[4]{0:T(128)S(1)}, s32[4]{0:T(128)}, u32[]{:S(2)}) copy-start(s32[4]{0:T(128)} %length_ref.3) | copy-start | bytes 52
  41.6 6.8 %collective-permute-start = (bf16[16,768]{1,0:T(8,128)(2,1)S(1)}, bf16[16,768]{1,0:T(8,128)(2,1)S(1)}, u32[]{:S(2)}, u32[]{:S(2)}) collective-permute-start(bf16[16,768]{1,0:T(8,128)(2,1)S(1)} %get-tuple-element.19), channel_id=1, source_target_pairs={{0,1},{1,0},{2,3},{3,2},{4,5},{5,4},{6,7},{7,6},{8,9},{9,8},{10,11... | collective-permute-start | bytes 73736 | tf_op jit(solution)/shard_map/ppermute | solution.py:561
  45.2 3.2 %collective-permute-start.1 = (bf16[16,768]{1,0:T(8,128)(2,1)S(1)}, bf16[16,768]{1,0:T(8,128)(2,1)S(1)}, u32[]{:S(2)}, u32[]{:S(2)}) collective-permute-start(bf16[16,768]{1,0:T(8,128)(2,1)S(1)} %get-tuple-element.20), channel_id=1, source_target_pairs={{0,2},{1,3},{2,0},{3,1},{4,6},{5,7},{6,4},{7,5},{8,10},{9,11},{10,... | collective-permute-start | bytes 73736 | tf_op jit(solution)/shard_map/ppermute | solution.py:561
  45.5 3.5 %collective-permute-start.2 = (bf16[16,768]{1,0:T(8,128)(2,1)S(1)}, bf16[16,768]{1,0:T(8,128)(2,1)S(1)}, u32[]{:S(2)}, u32[]{:S(2)}) collective-permute-start(bf16[16,768]{1,0:T(8,128)(2,1)S(1)} %get-tuple-element.21), channel_id=1, source_target_pairs={{0,3},{1,2},{2,1},{3,0},{4,7},{5,6},{6,5},{7,4},{8,11},{9,10},{10,... | collective-permute-start | bytes 73736 | tf_op jit(solution)/shard_map/ppermute | solution.py:561
  48.3 10.5 %copy-start.3 = (bf16[4,1024,256]{2,1,0:T(8,128)(2,1)S(1)}, bf16[4,1024,256]{2,1,0:T(8,128)(2,1)}, u32[]{:S(2)}) copy-start(bf16[4,1024,256]{2,1,0:T(8,128)(2,1)} %values_ref.3) | copy-start | bytes 6291460
  48.4 10.5 %copy-start.4 = (bf16[2048,51]{0,1:T(8,128)(2,1)S(1)}, bf16[2048,51]{0,1:T(8,128)(2,1)}, u32[]{:S(2)}) copy-start(bf16[2048,51]{0,1:T(8,128)(2,1)} %param.27) | copy-start | bytes 626692
  48.4 10.5 %copy-start.7 = (bf16[2048]{0:T(1024)(128)(2,1)S(1)}, bf16[2048]{0:T(1024)(128)(2,1)}, u32[]{:S(2)}) copy-start(bf16[2048]{0:T(1024)(128)(2,1)} %param.26) | copy-start | bytes 12292
  50.2 4.6 %collective-permute-start.3 = (bf16[16,2048]{1,0:T(8,128)(2,1)S(1)}, bf16[16,2048]{1,0:T(8,128)(2,1)S(1)}, u32[]{:S(2)}, u32[]{:S(2)}) collective-permute-start(bf16[16,2048]{1,0:T(8,128)(2,1)S(1)} %get-tuple-element.26.rows_ref), channel_id=1, source_target_pairs={{0,64},{4,68},{8,72},{12,76},{16,80},{20,84},{24,88},{28,92},{32,9... | collective-permute-start | bytes 196616 | tf_op jit(solution)/shard_map/ppermute | solution.py:566
  51.2 5.1 %collective-permute-start.4 = (f32[16,128]{1,0:T(8,128)S(1)}, f32[16,128]{1,0:T(8,128)S(1)}, u32[]{:S(2)}, u32[]{:S(2)}) collective-permute-start(f32[16,128]{1,0:T(8,128)S(1)} %get-tuple-element.27), channel_id=1, source_target_pairs={{0,66},{1,67},{2,64},{3,65},{4,70},{5,71},{6,68},{7,69},{8,74},{9,... | collective-permute-start | bytes 24584 | tf_op jit(solution)/shard_map/ppermute | solution.py:577
  56.4 2.5 %collective-permute-start.5 = (f32[16,128]{1,0:T(8,128)S(1)}, f32[16,128]{1,0:T(8,128)S(1)}, u32[]{:S(2)}, u32[]{:S(2)}) collective-permute-start(f32[16,128]{1,0:T(8,128)S(1)} %row_squares.1.near_ref), channel_id=1, source_target_pairs={{0,1},{1,0},{2,3},{3,2},{4,5},{5,4},{6,7},{7,6},{8,9},{9,8},{10,11... | collective-permute-start | bytes 24584 | tf_op jit(solution)/shard_map/ppermute | solution.py:561
  59.7 3.1 %collective-permute-start.8 = (f32[16,128]{1,0:T(8,128)S(1)}, f32[16,128]{1,0:T(8,128)S(1)}, u32[]{:S(2)}, u32[]{:S(2)}) collective-permute-start(f32[16,128]{1,0:T(8,128)S(1)} %critic.1.own_ref), channel_id=1, source_target_pairs={{0,3},{1,2},{2,1},{3,0},{4,7},{5,6},{6,5},{7,4},{8,11},{9,10},{10,... | collective-permute-start | bytes 24584 | tf_op jit(solution)/shard_map/ppermute | solution.py:561
  60.8 2.5 %collective-permute-start.7 = (f32[16,128]{1,0:T(8,128)S(1)}, f32[16,128]{1,0:T(8,128)S(1)}, u32[]{:S(2)}, u32[]{:S(2)}) collective-permute-start(f32[16,128]{1,0:T(8,128)S(1)} %critic.1.own_ref), channel_id=1, source_target_pairs={{0,2},{1,3},{2,0},{3,1},{4,6},{5,7},{6,4},{7,5},{8,10},{9,11},{10,... | collective-permute-start | bytes 24584 | tf_op jit(solution)/shard_map/ppermute | solution.py:561
  61.4 1.9 %collective-permute-start.6 = (f32[16,128]{1,0:T(8,128)S(1)}, f32[16,128]{1,0:T(8,128)S(1)}, u32[]{:S(2)}, u32[]{:S(2)}) collective-permute-start(f32[16,128]{1,0:T(8,128)S(1)} %critic.1.own_ref), channel_id=1, source_target_pairs={{0,1},{1,0},{2,3},{3,2},{4,5},{5,4},{6,7},{7,6},{8,9},{9,8},{10,11... | collective-permute-start | bytes 24584 | tf_op jit(solution)/shard_map/ppermute | solution.py:561
